TPU v7x, 128 devices: a whole 4x4x4 slice. The times are simulated.
128 devices in a mesh: dp: 4 (over x_hi, core), seq: 32 (over z, x_lo, y).
Axes of the slice: x: 4 (x_hi: 2, x_lo: 2; x = x_hi * 2 + x_lo), y: 4, z: 4, core: 2. Of those that a mesh axis runs over, the one named last changes fastest.
Arguments:
- features: bfloat16 [4, 32768, 768], P('dp', 'seq'), may hold values from -24 to 24
- cotangent: bfloat16 [4, 32768, 768], P('dp', 'seq'), may hold values from -6 to 6
- strand_pairs: int32 [768], replicated, may hold values from 0 to 767, as said below
- dilations: int32 [2], replicated, may hold values from 1 to 64, as said below
- down_weight: bfloat16 [2, 768, 384], replicated, may hold values from -0.21875 to 0.21875
- conv_weight: bfloat16 [2, 3, 384, 384], replicated, may hold values from -0.1875 to 0.1875
- up_weight: bfloat16 [2, 384, 768], replicated, may hold values from -0.3125 to 0.3125
Outputs:
- block_out: bfloat16 [4, 32768, 768], P('dp', 'seq')
- input_grad: bfloat16 [4, 32768, 768], P('dp', 'seq')
- grad_down: float32 [2, 768, 384], replicated
- grad_conv: float32 [2, 3, 384, 384], replicated
- grad_up: float32 [2, 384, 768], replicated
Inputs may be any that keep to these rules, and one draw needn't show every extreme that they name: strand_pairs is an involution without fixed points: strand_pairs[strand_pairs[c]] = c and strand_pairs[c] != c. `dilations`: every dilation is a power of two and some layer has dilation exactly 64.
All inputs are finite; a program needn't handle non-finite values.
Results may differ from a plain program's by a relative error of at most 0.02.
Values may be sent and summed in bfloat16 or wider, within the bound.
No kernel may reach another device: no remote copies, remote signals or barrier semaphores. Data moves between devices by JAX's collectives and lax.ppermute only.
A program may use at most 128 MiB of HBM per device.

v0:
```python
import functools
import math

import jax
import jax.numpy as jnp
from jax import lax
from jax.experimental import pallas as pl
from jax.experimental.pallas import tpu as pltpu
from jax.sharding import Mesh, PartitionSpec as P

C = 768
B = 384
PAD = 64
ROWS = 1024
TILE = 256
STEPS = ROWS // TILE
BLOCKS = 32
MID_ROWS, TOP_ROWS, BACK_ROWS = ROWS + 6 * PAD, ROWS + 4 * PAD, ROWS + 2 * PAD
MID_TILE, TOP_TILE, BACK_TILE = MID_ROWS // 4, TOP_ROWS // 4, BACK_ROWS // 3
EPS = 1e-06
ROOT = math.sqrt(2.0 / math.pi)
CUBE = 0.044715
BF = jnp.bfloat16
F32 = jnp.float32
SEQ = ("z", "xl", "y")
CHIPS = ("xh", "z", "xl", "y")


def mm(left, right):
    return lax.dot_general(left, right, (((1,), (0,)), ((), ())), preferred_element_type=F32)


def mm_nt(left, right):
    return lax.dot_general(left, right, (((1,), (1,)), ((), ())), preferred_element_type=F32)


def mm_tn(left, right):
    return lax.dot_general(left, right, (((0,), (0,)), ((), ())), preferred_element_type=F32)


def swap(pairs_ref):
    cols = lax.broadcasted_iota(jnp.int32, (C, C), 1)
    return (cols == pairs_ref[...]).astype(F32).astype(BF)


def scale_of(wide):
    return lax.rsqrt(jnp.mean(wide * wide, axis=-1, keepdims=True) + EPS)


def lay(dst, top, mid, bot):
    start = 0
    for piece in (top, mid, bot):
        rows = piece.shape[0]
        dst[start : start + rows, :] = piece.astype(dst.dtype)
        start += rows


def shift(pad, dil, start, before, after):
    rows = before.shape[0]
    base = pl.multiple_of(start + PAD, 8)

    @pl.when(dil >= 8)
    def _():
        for sign, ref in ((-1, before), (1, after)):
            ref[...] = pad[pl.ds(pl.multiple_of(base + sign * dil, 8), rows), :].astype(BF)

    for small in (1, 2, 4):

        @pl.when(dil == small)
        def _():
            window = pad[pl.ds(pl.multiple_of(base - 8, 8), rows + 16), :]
            before[...] = window[8 - small : 8 - small + rows].astype(BF)
            after[...] = window[8 + small : 8 + small + rows].astype(BF)


def centre(pad, start, rows):
    return pad[pl.ds(pl.multiple_of(start + PAD, 8), rows), :].astype(BF)


def conv(first, last, mid, weight):
    rows = mid.shape[0]
    rows_a = jnp.concatenate([first[:, :B], mid[:, :B], last[:, :B]], axis=1)
    rows_b = jnp.concatenate([last[:, B:], mid[:, B:], first[:, B:]], axis=1)
    both = mm(jnp.concatenate([rows_a, rows_b], axis=0), weight)
    return jnp.concatenate([both[:rows], both[rows:]], axis=1)


def inside(block, start, values):
    rows = lax.broadcasted_iota(jnp.int32, (values.shape[0], 1), 0) + (block * ROWS + start)
    return jnp.where((rows >= 0) & (rows < BLOCKS * ROWS), values, 0.0)


def gelu_both(pre):
    sq = pre * pre
    t = jnp.tanh(ROOT * (pre + CUBE * (pre * sq)))
    half = 0.5 + 0.5 * t
    slope = half + (0.5 * pre) * ((1.0 - t * t) * (ROOT + (3.0 * CUBE * ROOT) * sq))
    return pre * half, slope


def k_enter(pairs, down, x, dcat, normed, inner):
    @pl.when(pl.program_id(0) == 0)
    def _():
        dcat[:, :B] = down[...]
        dcat[:, B:] = mm(swap(pairs), down[...]).astype(BF)

    wide = x[...].astype(F32)
    n = (wide * scale_of(wide)).astype(BF)
    normed[...] = n
    inner[...] = mm(n, dcat[...]).astype(BF)


def k_prep(pairs, down1, up, kern, dcat1, upcat, kern_t):
    s = swap(pairs)
    dcat1[:, :B] = down1[...]
    dcat1[:, B:] = mm(s, down1[...]).astype(BF)
    for layer in range(2):
        upcat[layer, :B, :] = up[layer]
        upcat[layer, B:, :] = mm(up[layer], s).astype(BF)
        for k in range(3):
            kern_t[layer, k * B : (k + 1) * B, :] = kern[layer, k].astype(F32).T.astype(BF)


def k_middle(dil, block, mid, x, top, bot, dcat0, weight, upcat, dcat,
             act, slope, tm, tc, tp, stream, normed, inner, pad, field):
    start = pl.program_id(0) * MID_TILE

    @pl.when(pl.program_id(0) == 0)
    def _():
        lay(field, top[PAD:, :], x[...], bot[: 4 * PAD - PAD, :])
        ends = []
        for halo in (top, bot):
            wide = halo[...].astype(F32)
            ends.append(mm((wide * scale_of(wide)).astype(BF), dcat0[...]).astype(BF))
        lay(pad, ends[0], mid[...], ends[1])

    shift(pad, dil[0], start, tm, tp)
    m = centre(pad, start, MID_TILE)
    tc[...] = m
    g, s = gelu_both(conv(tm[...], tp[...], m, weight[...]))
    g = g.astype(BF)
    act[...] = g
    slope[...] = s.astype(BF)
    rows = pl.ds(pl.multiple_of(start, 16), MID_TILE)
    out = (field[rows, :].astype(F32) + mm(g, upcat[...])).astype(BF)
    stream[...] = out
    wide = out.astype(F32)
    n = (wide * scale_of(wide)).astype(BF)
    normed[...] = n
    inner[...] = inside(block[0], start - 3 * PAD, mm(n, dcat[...])).astype(BF)


def k_top(dil, mid, cot, ctop, cbot, weight, upcat, act, d_pre, tm, tc, tp, pad, grad):
    start = pl.program_id(0) * TOP_TILE

    @pl.when(pl.program_id(0) == 0)
    def _():
        pad[...] = mid[...].astype(F32)
        lay(grad, ctop[...], cot[...], cbot[...])

    shift(pad, dil[0], start, tm, tp)
    m = centre(pad, start, TOP_TILE)
    tc[...] = m
    rows = pl.ds(pl.multiple_of(start, 16), TOP_TILE)
    d_act = mm_nt(grad[rows, :], upcat[...])
    g, s = gelu_both(conv(tm[...], tp[...], m, weight[...]))
    act[...] = g.astype(BF)
    d_pre[...] = (d_act * s).astype(BF)


def put(ref, start, value):
    rows, cols = value.shape
    for i in range(cols // LANES):
        ref[start + i * rows : start + (i + 1) * rows, :] = value[:, i * LANES : (i + 1) * LANES].astype(BF)


def take(ref, start, rows, cols):
    pieces = [ref[start + i * rows : start + (i + 1) * rows, :] for i in range(cols // LANES)]
    return jnp.concatenate(pieces, axis=1).astype(F32)


def own(ref, before):
    return ref[before : before + ROWS, :]


def weight_sums(factor, pairs, act, cot, taps, d_pre, rest):
    up = mm_tn(act, cot) * factor
    put(rest, 0, up[:B] + mm(up[B:].astype(BF), swap(pairs)))
    for k in range(3):
        total = mm_tn(taps[k][:, :B], d_pre[:, :B]) + mm_tn(taps[2 - k][:, B:], d_pre[:, B:])
        put(rest, UP + k * 3 * B, total * factor)
    rest[REST - LANES :, :] = jnp.zeros((LANES, LANES), BF)


def sort_out(core, lower, upper, send, keep):
    @pl.when(core[0] == 0)
    def _():
        send[...] = upper[...]
        keep[...] = lower[...]

    @pl.when(core[0] != 0)
    def _():
        send[...] = lower[...]
        keep[...] = upper[...]


def k_sums_out(factor, pairs, act, cot, tm, tc, tp, d_pre, stream, upcat, rest, out):
    a = own(act, 2 * PAD)
    out[...] = (own(stream, 3 * PAD).astype(F32) + mm(a, upcat[...])).astype(BF)
    taps = [own(ref, 2 * PAD) for ref in (tm, tc, tp)]
    weight_sums(factor, pairs, a, cot[...], taps, own(d_pre, 2 * PAD), rest)


def k_sums(factor, core, pairs, act, cot, tm, tc, tp, d_pre, upper, send, keep, rest):
    taps = [own(ref, 3 * PAD) for ref in (tm, tc, tp)]
    weight_sums(factor, pairs, own(act, 3 * PAD), own(cot, PAD), taps, own(d_pre, PAD), rest)
    sort_out(core, rest, upper, send, keep)


def down_sum(factor, pairs, normed, d_inner, down):
    total = mm_tn(normed, d_inner) * factor
    put(down, 0, total[:, :B] + mm(swap(pairs), total[:, B:].astype(BF)))


def k_join(keep_a, got_a, keep_b, got_b, out):
    out[:REST, :] = (keep_a[...].astype(F32) + got_a[...].astype(F32)).astype(BF)
    out[REST:, :] = (keep_b[...].astype(F32) + got_b[...].astype(F32)).astype(BF)


def k_share(parts, out):
    share = jnp.sum(parts[...].astype(F32), axis=0).astype(BF)
    out[...] = jnp.broadcast_to(share[None], out.shape)


def k_finish(core, own, other, down, kern, up):
    layer = pl.program_id(0)
    for mine, ref in ((True, own), (False, other)):

        @pl.when((core[0] == layer) == mine)
        def _():
            up[0] = take(ref, 0, B, C)
            for k in range(3):
                kern[0, k] = take(ref, UP + k * 3 * B, B, B)
            down[0] = take(ref, REST, C, B)


def norm_back(v, d_norm):
    wide = v.astype(F32)
    scale = scale_of(wide)
    mixed = jnp.mean(d_norm * wide, axis=-1, keepdims=True)
    return scale * d_norm - wide * (scale * scale * scale * mixed)


def k_back(factor, dil, block, pairs, mid, weight, normed, stream, cot, ctop, cbot, dcat, upcat, slope,
           grad, d_pre, down, pad, before, after, d_inner, given):
    start = pl.program_id(0) * BACK_TILE

    @pl.when(pl.program_id(0) == 0)
    def _():
        pad[...] = mid[...].astype(F32)
        lay(given, ctop[PAD:, :], cot[...], cbot[:PAD, :])

    shift(pad, dil[0], start, before, after)
    di = conv(after[...], before[...], centre(pad, start, BACK_TILE), weight[...]).astype(BF)
    rows = pl.ds(pl.multiple_of(start, 16), BACK_TILE)
    saved = pl.ds(pl.multiple_of(start + 2 * PAD, 16), BACK_TILE)
    d_inner[rows, :] = di
    g = given[rows, :].astype(F32) + norm_back(stream[saved, :], mm_nt(di, dcat[...]))
    g = inside(block[0], start - PAD, g).astype(BF)
    grad[...] = g
    d_pre[...] = (mm_nt(g, upcat[...]) * slope[saved, :].astype(F32)).astype(BF)

    @pl.when(pl.program_id(0) == pl.num_programs(0) - 1)
    def _():
        down_sum(factor, pairs, own(normed, 3 * PAD), own(d_inner, PAD), down)


def k_last(factor, core, dil, pairs, mid, weight, normed, upper, send, keep, d_inner, pad, before, after, down):
    start = pl.program_id(0) * TILE

    @pl.when(pl.program_id(0) == 0)
    def _():
        pad[...] = mid[...].astype(F32)

    shift(pad, dil[0], start, before, after)
    di = conv(after[...], before[...], centre(pad, start, TILE), weight[...]).astype(BF)
    d_inner[pl.ds(pl.multiple_of(start, 16), TILE), :] = di

    @pl.when(pl.program_id(0) == pl.num_programs(0) - 1)
    def _():
        down_sum(factor, pairs, normed[...], d_inner[...], down)
        sort_out(core, down, upper, send, keep)


def k_input(d_inner, x, cot, dcat, out):
    rows = pl.ds(pl.multiple_of(pl.program_id(0) * TILE + PAD, 16), TILE)
    out[...] = (cot[rows, :].astype(F32) + norm_back(x[...], mm_nt(d_inner[...], dcat[...]))).astype(BF)


def tile(rows=TILE):
    return pl.BlockSpec((rows, C), lambda i: (i, 0))


def whole(*shape):
    return pl.BlockSpec(shape, lambda i: (0,) * len(shape))


def scalar():
    return pl.BlockSpec(memory_space=pltpu.SMEM)


def shape(*dims, kind=BF):
    return jax.ShapeDtypeStruct(dims, kind)


def call(body, steps, ins, outs, scratch, flops, name):
    size = lambda s: 2 * math.prod(s.shape)
    return pl.pallas_call(
        body,
        grid=(steps,),
        in_specs=ins,
        out_specs=[spec for spec, _ in outs],
        out_shape=[form for _, form in outs],
        scratch_shapes=scratch,
        compiler_params=pltpu.CompilerParams(vmem_limit_bytes=48 * 1024 * 1024),
        cost_estimate=pl.CostEstimate(
            flops=int(flops), bytes_accessed=2 * sum(size(f) for _, f in outs), transcendentals=0
        ),
        name=name,
    )


LANES = 128
UP = 6 * B
REST = UP + 9 * B + LANES
DOWN = 6 * B
UNIT = 2 * ROWS * C * C
FULL = (tile(), shape(ROWS, C))


def store(rows, kind=BF):
    return pltpu.VMEM((rows, C), kind)


def edges(cells, rows):
    top = lax.ppermute(cells[ROWS - rows :], SEQ, [(i, i + 1) for i in range(BLOCKS - 1)])
    bot = lax.ppermute(cells[:rows], SEQ, [(i + 1, i) for i in range(BLOCKS - 1)])
    return top, bot


SWAP = [(0, 1), (1, 0)]
SHARES = (64, (REST + DOWN) // 64, LANES)


def exchange(parts):
    return lax.all_to_all(parts, CHIPS, 0, 0, tiled=True)


def other_core(cells):
    return lax.ppermute(cells, "core", SWAP)


def local(features, cotangent, strand_pairs, dilations, down_weight, conv_weight, up_weight):
    x = features[0]
    cot = cotangent[0]
    pairs = strand_pairs.reshape(C, 1)
    factor = 1.0 / math.sqrt(131072.0)
    dil = [dilations[layer : layer + 1] for layer in range(2)]
    kern = [conv_weight[layer].reshape(3 * B, B) for layer in range(2)]
    block = lax.axis_index(SEQ).reshape(1)
    square = whole(C, C)
    resident = whole(ROWS, C)
    taps_w = whole(3 * B, B)

    top, bot = edges(x, 4 * PAD)
    ctop, cbot = edges(cot, 2 * PAD)
    dcat0, normed0, inner0 = call(
        k_enter, STEPS, [whole(C, 1), whole(C, B), tile()],
        [(square, shape(C, C)), FULL, FULL], [], UNIT, "enter",
    )(pairs, down_weight[0], x)
    dcat1, upcat, kern_t = call(
        k_prep, 1, [whole(C, 1), whole(C, B), whole(2, B, C), whole(2, 3, B, B)],
        [(square, shape(C, C)), (whole(2, C, C), shape(2, C, C)), (whole(2, 3 * B, B), shape(2, 3 * B, B))],
        [], 2.5 * UNIT, "prep",
    )(pairs, down_weight[1], up_weight, conv_weight)
    up0, up1 = upcat[0], upcat[1]
    mid = (tile(MID_TILE), shape(MID_ROWS, C))
    act0, slope0, tm0, tc0, tp0, stream1, normed1, inner1 = call(
        k_middle, 4,
        [scalar(), scalar(), resident, resident, whole(4 * PAD, C), whole(4 * PAD, C), square, taps_w, square, square],
        [mid] * 8, [store(ROWS + 8 * PAD, F32), store(MID_ROWS)], 6 * UNIT, "middle",
    )(dil[0], block, inner0, x, top, bot, dcat0, kern[0], up0, dcat1)
    upper = (tile(TOP_TILE), shape(TOP_ROWS, C))
    c_halo = whole(2 * PAD, C)
    act1, d_pre1, tm1, tc1, tp1 = call(
        k_top, 4, [scalar(), whole(MID_ROWS, C), resident, c_halo, c_halo, taps_w, square],
        [upper] * 5, [store(MID_ROWS, F32), store(TOP_ROWS)], 3 * UNIT, "top",
    )(dil[1], inner1, cot, ctop, cbot, kern[1], up1)
    core = lax.axis_index("core").reshape(1)
    sums = (whole(REST, LANES), shape(REST, LANES))
    downs = (whole(DOWN, LANES), shape(DOWN, LANES))
    joined = (whole(REST + DOWN, LANES), shape(REST + DOWN, LANES))
    shares = (whole(*SHARES), shape(*SHARES))
    wide_top, wide_mid, wide_back = whole(TOP_ROWS, C), whole(MID_ROWS, C), whole(BACK_ROWS, C)
    rest1, out = call(
        functools.partial(k_sums_out, factor), 1,
        [whole(C, 1), wide_top, resident] + [wide_top] * 4 + [wide_mid, square],
        [sums, (resident, shape(ROWS, C))], [], 4 * UNIT, "sums_out",
    )(pairs, act1, cot, tm1, tc1, tp1, d_pre1, stream1, up1)
    back = (tile(BACK_TILE), shape(BACK_ROWS, C))
    grad, d_pre0, down1 = call(
        functools.partial(k_back, factor), 3,
        [scalar(), scalar(), whole(C, 1), wide_top, taps_w, wide_mid, wide_mid, resident, c_halo, c_halo,
         square, square, wide_mid],
        [back, back, downs],
        [store(TOP_ROWS, F32), store(BACK_TILE), store(BACK_TILE), store(BACK_ROWS), store(BACK_ROWS)],
        5 * UNIT, "back",
    )(dil[1], block, pairs, d_pre1, kern_t[1], normed1, stream1, cot, ctop, cbot, dcat1, up0, slope0)
    send_a, keep_a = call(
        functools.partial(k_sums, factor), 1,
        [scalar(), whole(C, 1), wide_mid, wide_back, wide_mid, wide_mid, wide_mid, wide_back, sums[0]],
        [sums, sums], [pltpu.VMEM((REST, LANES), BF)], 3 * UNIT, "sums",
    )(core, pairs, act0, grad, tm0, tc0, tp0, d_pre0, rest1)
    send_b, keep_b, d_inner0 = call(
        functools.partial(k_last, factor), STEPS,
        [scalar(), scalar(), whole(C, 1), wide_back, taps_w, resident, downs[0]],
        [downs, downs, (resident, shape(ROWS, C))],
        [store(BACK_ROWS, F32), store(TILE), store(TILE), pltpu.VMEM((DOWN, LANES), BF)],
        3 * UNIT, "last",
    )(core, dil[0], pairs, d_pre0, kern_t[0], normed0, down1)
    (parts,) = call(
        k_join, 1, [sums[0], sums[0], downs[0], downs[0]], [joined], [], 0, "join",
    )(keep_a, other_core(send_a), keep_b, other_core(send_b))
    parts = exchange(parts.reshape(SHARES))
    (shared,) = call(k_share, 1, [shares[0]], [shares], [], 0, "share")(parts)
    (input_grad,) = call(
        k_input, STEPS, [tile(), tile(), wide_back, square], [FULL], [], UNIT, "input",
    )(d_inner0, x, grad, dcat0)
    own = exchange(shared).reshape(REST + DOWN, LANES)
    layered = lambda *dims: (
        pl.BlockSpec((1,) + dims, lambda i: (i,) + (0,) * len(dims)), shape(2, *dims, kind=F32)
    )
    grads = call(
        k_finish, 2, [scalar()] + [joined[0]] * 2,
        [layered(C, B), layered(3, B, B), layered(B, C)], [], 0, "finish",
    )(core, own, other_core(own))
    return (out[None], input_grad[None], *grads)


def solution(mesh):
    fine = Mesh(mesh.devices.reshape(2, 2, 4, 2, 4), ("xh", "core", "z", "xl", "y"))
    rows = P(("xh", "core"), SEQ, None)
    in_specs = (rows, rows, P(), P(), P(), P(), P())
    out_specs = (rows, rows, P(), P(), P())
    return jax.shard_map(local, mesh=fine, in_specs=in_specs, out_specs=out_specs, check_vma=False)
```

profile of v0, /device:TPU:1, one launch (start us, length us, event | category | flops | bytes accessed | tf_op | source)
XLA Modules:
  0.0 204.0 jit_solution(11266765433011242563)
XLA Ops:
  0.6 0.0 copy-start.15
  0.6 0.0 copy-start.14
  0.7 2.2 %slice_bitcast_fusion.6 = (bf16[256,768]{1,0:T(8,128)(2,1)}, bf16[256,768]{1,0:T(8,128)(2,1)}) fusion(bf16[1,1024,768]{2,1,0:T(8,128)(2,1)} %param.7), kind=kLoop, calls=%fused_computation.6 | loop fusion | bytes 1572864 | tf_op jit(solution)/shard_map/slice | solution.py:347
  2.8 4.0 %collective-permute-start = (bf16[256,768]{1,0:T(8,128)(2,1)}, bf16[256,768]{1,0:T(8,128)(2,1)S(1)}, u32[]{:S(2)}, u32[]{:S(2)}) collective-permute-start(bf16[256,768]{1,0:T(8,128)(2,1)} %get-tuple-element.78), channel_id=1, source_target_pairs={{0,1},{1,2},{2,3},{3,4},{4,5},{5,6},{6,7},{7,8},{8,9},{9,10},{10,1... | collective-permute-start | bytes 1179656 | tf_op jit(solution)/shard_map/ppermute | solution.py:346
  6.9 1.3 collective-permute-start.1
  8.2 1.8 slice_bitcast_fusion.8
  10.0 4.7 %collective-permute-start.2 = (bf16[128,768]{1,0:T(8,128)(2,1)}, bf16[128,768]{1,0:T(8,128)(2,1)}, u32[]{:S(2)}, u32[]{:S(2)}) collective-permute-start(bf16[128,768]{1,0:T(8,128)(2,1)} %get-tuple-element.76), channel_id=1, source_target_pairs={{0,1},{1,2},{2,3},{3,4},{4,5},{5,6},{6,7},{7,8},{8,9},{9,10},{10,1... | collective-permute-start | bytes 589832 | tf_op jit(solution)/shard_map/ppermute | solution.py:346
  14.7 1.3 collective-permute-start.3
  16.0 0.0 copy-done.15
  16.0 0.2 reshape.34.pairs
  16.1 0.0 copy-done.14
  16.2 0.1 slice_bitcast_fusion.4
  16.3 0.0 copy-start.6
  16.3 2.9 %fusion = (bf16[1,3,384,384]{3,2,1,0:T(8,128)(2,1)}, bf16[1,3,384,384]{3,2,1,0:T(8,128)(2,1)}) fusion(bf16[2,3,384,384]{3,2,1,0:T(8,128)(2,1)} %kern.1), kind=kLoop, calls=%fused_computation.10 | loop fusion | bytes 3538944 | tf_op jit(solution)/shard_map/slice | solution.py:369
  19.2 0.0 copy-done.6
  19.2 4.7 %prep.1 = (bf16[768,768]{1,0:T(8,128)(2,1)S(1)}, bf16[2,768,768]{2,1,0:T(8,128)(2,1)}, bf16[2,1152,384]{2,1,0:T(8,128)(2,1)S(1)}) custom-call(s32[768,1]{1,0:T(8,128)S(1)} %reshape.34.pairs, bf16[768,384]{1,0:T(8,128)(2,1)S(1)} %get-tuple-element.79.down1, bf16[2,384,768]{2,1,0:T(8,128)(2,1)S(1)} %copy-done.6, bf16[2,3,384,384]{3,2,1,0:T(8,128)(2,1)} %kern.1), custom_call_target="tpu_custom_call" | custom-call | flops 3019898880 | bytes 10616832 | tf_op jit(solution)/shard_map/prep/pallas_call | solution.py:381
  23.9 0.0 copy-start.11
  23.9 1.0 copy-done.11
  24.9 1.1 slice_bitcast_fusion.2
  26.0 0.0 copy-start.16
  26.0 0.0 copy-start.13
  26.0 4.7 %enter.1 = (bf16[768,768]{1,0:T(8,128)(2,1)S(1)}, bf16[1024,768]{1,0:T(8,128)(2,1)S(1)}, bf16[1024,768]{1,0:T(8,128)(2,1)S(1)}) custom-call(s32[768,1]{1,0:T(8,128)S(1)} %reshape.34.pairs, bf16[768,384]{1,0:T(8,128)(2,1)S(1)} %get-tuple-element.80.down, bf16[1024,768]{1,0:T(8,128)(2,1)} %bitcast.32), custom_call_target="tpu_custom_call" | custom-call | flops 1207959552 | bytes 8650752 | tf_op jit(solution)/shard_map/enter/pallas_call | solution.py:377
  30.7 0.0 copy-start.7
  30.8 1.1 copy-done.7
  31.9 0.0 copy-done.16
  31.9 0.0 copy-start.9
  31.9 0.7 fusion.1
  32.6 0.0 copy-done.13
  32.6 0.0 copy-start.4
  32.6 0.2 slice_bitcast_fusion
  32.8 0.2 copy-done.9
  33.0 0.0 collective-permute-done.top
  33.0 0.0 collective-permute-done.1.bot
  33.0 0.8 copy-done.4
  33.8 0.4 copy-done.12
  34.2 16.9 %middle.1 = (bf16[1408,768]{1,0:T(8,128)(2,1)}, bf16[1408,768]{1,0:T(8,128)(2,1)}, bf16[1408,768]{1,0:T(8,128)(2,1)}, bf16[1408,768]{1,0:T(8,128)(2,1)}, bf16[14...) custom-call(s32[1]{0:T(128)} %get-tuple-element.81.dil, ...), custom_call_target="tpu_custom_call" | custom-call | flops 7247757312 | bytes 34603008 | tf_op jit(solution)/shard_map/middle/pallas_call | solution.py:388
  51.1 0.0 collective-permute-done.2.ctop
  51.1 0.0 collective-permute-done.3.cbot
  51.1 0.0 copy-done.3
  51.1 0.0 copy-done.5
  51.1 11.2 %top.1 = (bf16[1280,768]{1,0:T(8,128)(2,1)S(1)}, bf16[1280,768]{1,0:T(8,128)(2,1)}, bf16[1280,768]{1,0:T(8,128)(2,1)}, bf16[1280,768]{1,0:T(8,128)(2,1)}, bf16[1280,768]{1,0:T(8,128)(2,1)}) custom-call(s32[1]{0:T(128)} %get-tuple-element.82.dil, bf16[1408,768]{1,0:T(8,128)(2,1)} %get-tuple-element.41.mid, bf16[1024,768]{1,0:T(8,128)(2,1)S(1)} %bitcast.37, ...), custom_call_target="tpu_custom_call" | custom-call | flops 3623878656 | bytes 19660800 | tf_op jit(solution)/shard_map/top/pallas_call | solution.py:395
  62.3 1.3 copy-done.10
  63.6 10.1 %sums_out.1 = (bf16[5888,128]{1,0:T(8,128)(2,1)S(1)}, bf16[1024,768]{1,0:T(8,128)(2,1)}) custom-call(s32[768,1]{1,0:T(8,128)S(1)} %reshape.34.pairs, bf16[1280,768]{1,0:T(8,128)(2,1)} %copy-done.10, bf16[1024,768]{1,0:T(8,128)(2,1)S(1)} %bitcast.38, bf16[1280,768]{1,0:T(8,128)(2,1)} %get-tuple-element.43.tm, bf16[1280,768]{1,0:T(8,128)(2,1)} %get-tuple-element.44.tc, ...), custom_call_target="tpu_custom_call" | custom-call | flops 4831838208 | bytes 6160384 | tf_op jit(solution)/shard_map/sums_out/pallas_call | solution.py:405
  73.7 16.7 %back.1 = (bf16[1152,768]{1,0:T(8,128)(2,1)}, bf16[1152,768]{1,0:T(8,128)(2,1)}, bf16[2304,128]{1,0:T(8,128)(2,1)S(1)}) custom-call(s32[1]{0:T(128)} %get-tuple-element.82.dil, s32[1]{0:T(128)} %bitcast.block, s32[768,1]{1,0:T(8,128)S(1)} %reshape.34.pairs, bf16[1280,768]{1,0:T(8,128)(2,1)} %get-tuple-element.46.d_pre.mid, ...), custom_call_target="tpu_custom_call" | custom-call | flops 6039797760 | bytes 8257536 | tf_op jit(solution)/shard_map/back/pallas_call | solution.py:411
  90.4 9.9 %sums.1 = (bf16[5888,128]{1,0:T(8,128)(2,1)S(1)}, bf16[5888,128]{1,0:T(8,128)(2,1)S(1)}) custom-call(s32[1]{0:T(128)} %bitcast.14.core, s32[768,1]{1,0:T(8,128)S(1)} %reshape.34.pairs, bf16[1408,768]{1,0:T(8,128)(2,1)} %get-tuple-element.57.act, bf16[1152,768]{1,0:T(8,128)(2,1)} %get-tuple-element.56.cot, bf16[1408,768]{1,0:T(8,128)(2,1)} %get-tuple-element.58.tm, ...), custom_call_target="tpu_custom_call" | custom-call | flops 3623878656 | bytes 6029312 | tf_op jit(solution)/shard_map/sums/pallas_call | solution.py:419
  100.3 1.6 collective-permute-start.4
  101.9 0.0 copy-done.2
  101.9 0.0 copy-done.8
  101.9 8.8 %last.1 = (bf16[2304,128]{1,0:T(8,128)(2,1)S(1)}, bf16[2304,128]{1,0:T(8,128)(2,1)S(1)}, bf16[1024,768]{1,0:T(8,128)(2,1)S(1)}) custom-call(s32[1]{0:T(128)} %bitcast.14.core, s32[1]{0:T(128)} %get-tuple-element.81.dil, s32[768,1]{1,0:T(8,128)S(1)} %reshape.34.pairs, bf16[1152,768]{1,0:T(8,128)(2,1)} %get-tuple-element.52.mid.d_pre, ...), custom_call_target="tpu_custom_call" | custom-call | flops 3623878656 | bytes 5505024 | tf_op jit(solution)/shard_map/last/pallas_call | solution.py:424
  110.7 0.1 collective-permute-start.5
  110.8 2.0 collective-permute-done.5.got_b
  112.8 0.0 collective-permute-done.4.got_a
  112.8 1.8 join.1
  114.6 43.6 %all_to_all.10.parts = bf16[64,128,128]{2,1,0:T(8,128)(2,1)S(1)} all-to-all(bf16[64,128,128]{2,1,0:T(8,128)(2,1)} %bitcast.40), channel_id=1, replica_groups=mesh['xh'=2,'core'=2,'z'=4,'xl'=2,'y'=4] {'xh','z','xl','y'}, dimensions={0} | all-to-all | bytes 4194304 | tf_op jit(solution)/shard_map/all_to_all | solution.py:356
  158.2 0.5 share.1
  158.7 0.0 copy-start
  158.7 0.0 copy-start.1
  158.7 35.7 %all_to_all.11 = bf16[64,128,128]{2,1,0:T(8,128)(2,1)S(1)} all-to-all(bf16[64,128,128]{2,1,0:T(8,128)(2,1)S(1)} %share.1), channel_id=1, replica_groups=mesh['xh'=2,'core'=2,'z'=4,'xl'=2,'y'=4] {'xh','z','xl','y'}, dimensions={0} | all-to-all | bytes 4194304 | tf_op jit(solution)/shard_map/all_to_all | solution.py:356
  194.4 2.2 %collective-permute-start.6 = (bf16[8192,128]{1,0:T(8,128)(2,1)S(1)}, bf16[8192,128]{1,0:T(8,128)(2,1)S(1)}, u32[]{:S(2)}, u32[]{:S(2)}) collective-permute-start(bf16[8192,128]{1,0:T(8,128)(2,1)S(1)} %bitcast.30), channel_id=1, source_target_pairs={{0,32},{32,0},{1,33},{33,1},{2,34},{34,2},{3,35},{35,3},{4,36},{36... | collective-permute-start | bytes 6291464 | tf_op jit(solution)/shard_map/ppermute | solution.py:360
  196.7 0.0 copy-done
  196.7 0.0 copy-done.1
  196.7 3.6 %input.1 = bf16[1024,768]{1,0:T(8,128)(2,1)} custom-call(bf16[1024,768]{1,0:T(8,128)(2,1)S(1)} %get-tuple-element.55.d_inner, bf16[1024,768]{1,0:T(8,128)(2,1)S(1)} %bitcast.34, bf16[1152,768]{1,0:T(8,128)(2,1)S(1)} %copy-done, bf16[768,768]{1,0:T(8,128)(2,1)S(1)} %get-tuple-element.38.dcat0.dcat), custom_call_target="tpu_custom_call" | custom-call | flops 1207959552 | bytes 3145728 | tf_op jit(solution)/shard_map/input/pallas_call | solution.py:436
  200.2 0.2 collective-permute-done.6.other
  200.4 3.6 %finish.1 = (f32[2,768,384]{2,1,0:T(8,128)}, f32[2,3,384,384]{3,2,1,0:T(8,128)}, f32[2,384,768]{2,1,0:T(8,128)}) custom-call(s32[1]{0:T(128)} %bitcast.14.core, bf16[8192,128]{1,0:T(8,128)(2,1)S(1)} %bitcast.31, bf16[8192,128]{1,0:T(8,128)(2,1)S(1)} %collective-permute-done.6.other), custom_call_target="tpu_custom_call" | custom-call | bytes 8257536 | tf_op jit(solution)/shard_map/finish/pallas_call | solution.py:443
  (6 shorter events, 0.0 us)
Async XLA Ops:
  0.6 15.3 %copy-start.15 = (s32[768]{0:T(1024)S(1)}, s32[768]{0:T(1024)}, u32[]{:S(2)}) copy-start(s32[768]{0:T(1024)} %param.9) | copy-start | bytes 9220
  0.6 15.5 %copy-start.14 = (bf16[2,768,384]{2,1,0:T(8,128)(2,1)S(1)}, bf16[2,768,384]{2,1,0:T(8,128)(2,1)}, u32[]{:S(2)}) copy-start(bf16[2,768,384]{2,1,0:T(8,128)(2,1)} %param.11) | copy-start | bytes 3538948
  2.8 30.2 %collective-permute-start = (bf16[256,768]{1,0:T(8,128)(2,1)}, bf16[256,768]{1,0:T(8,128)(2,1)S(1)}, u32[]{:S(2)}, u32[]{:S(2)}) collective-permute-start(bf16[256,768]{1,0:T(8,128)(2,1)} %get-tuple-element.78), channel_id=1, source_target_pairs={{0,1},{1,2},{2,3},{3,4},{4,5},{5,6},{6,7},{7,8},{8,9},{9,10},{10,1... | collective-permute-start | bytes 1179656 | tf_op jit(solution)/shard_map/ppermute | solution.py:346
  6.9 26.2 %collective-permute-start.1 = (bf16[256,768]{1,0:T(8,128)(2,1)}, bf16[256,768]{1,0:T(8,128)(2,1)}, u32[]{:S(2)}, u32[]{:S(2)}) collective-permute-start(bf16[256,768]{1,0:T(8,128)(2,1)} %get-tuple-element.77), channel_id=1, source_target_pairs={{1,0},{2,1},{3,2},{4,3},{5,4},{6,5},{7,6},{8,7},{9,8},{10,9},{11,1... | collective-permute-start | bytes 1179656 | tf_op jit(solution)/shard_map/ppermute | solution.py:347
  10.0 41.1 %collective-permute-start.2 = (bf16[128,768]{1,0:T(8,128)(2,1)}, bf16[128,768]{1,0:T(8,128)(2,1)}, u32[]{:S(2)}, u32[]{:S(2)}) collective-permute-start(bf16[128,768]{1,0:T(8,128)(2,1)} %get-tuple-element.76), channel_id=1, source_target_pairs={{0,1},{1,2},{2,3},{3,4},{4,5},{5,6},{6,7},{7,8},{8,9},{9,10},{10,1... | collective-permute-start | bytes 589832 | tf_op jit(solution)/shard_map/ppermute | solution.py:346
  14.7 36.4 %collective-permute-start.3 = (bf16[128,768]{1,0:T(8,128)(2,1)}, bf16[128,768]{1,0:T(8,128)(2,1)}, u32[]{:S(2)}, u32[]{:S(2)}) collective-permute-start(bf16[128,768]{1,0:T(8,128)(2,1)} %get-tuple-element.75), channel_id=1, source_target_pairs={{1,0},{2,1},{3,2},{4,3},{5,4},{6,5},{7,6},{8,7},{9,8},{10,9},{11,1... | collective-permute-start | bytes 589832 | tf_op jit(solution)/shard_map/ppermute | solution.py:347
  16.3 2.9 %copy-start.6 = (bf16[2,384,768]{2,1,0:T(8,128)(2,1)S(1)}, bf16[2,384,768]{2,1,0:T(8,128)(2,1)}, u32[]{:S(2)}) copy-start(bf16[2,384,768]{2,1,0:T(8,128)(2,1)} %up.1) | copy-start | bytes 3538948
  23.9 1.0 copy-start.11
  26.0 5.9 %copy-start.16 = (s32[2]{0:T(128)S(1)}, s32[2]{0:T(128)}, u32[]{:S(2)}) copy-start(s32[2]{0:T(128)} %param.10) | copy-start | bytes 28
  26.0 6.6 %copy-start.13 = (bf16[2,768,768]{2,1,0:T(8,128)(2,1)S(1)}, bf16[2,768,768]{2,1,0:T(8,128)(2,1)}, u32[]{:S(2)}) copy-start(bf16[2,768,768]{2,1,0:T(8,128)(2,1)} %get-tuple-element.39) | copy-start | bytes 7077892
  30.7 1.1 copy-start.7
  31.9 1.1 copy-start.9
  32.6 1.2 copy-start.4
  32.6 1.5 copy-start.12
  34.2 16.9 %copy-start.3 = (bf16[1,3,384,384]{3,2,1,0:T(8,128)(2,1)S(1)}, bf16[1,3,384,384]{3,2,1,0:T(8,128)(2,1)}, u32[]{:S(2)}) copy-start(bf16[1,3,384,384]{3,2,1,0:T(8,128)(2,1)} %get-tuple-element.73) | copy-start | bytes 2654212
  34.2 16.9 %copy-start.5 = (bf16[1,1024,768]{2,1,0:T(8,128)(2,1)S(1)}, bf16[1,1024,768]{2,1,0:T(8,128)(2,1)}, u32[]{:S(2)}) copy-start(bf16[1,1024,768]{2,1,0:T(8,128)(2,1)} %param.8) | copy-start | bytes 4718596
  62.3 1.3 copy-start.10
  90.4 11.5 %copy-start.2 = (bf16[1152,384]{1,0:T(8,128)(2,1)S(1)}, bf16[1152,384]{1,0:T(8,128)(2,1)}, u32[]{:S(2)}) copy-start(bf16[1152,384]{1,0:T(8,128)(2,1)} %get-tuple-element.71.weight) | copy-start | bytes 2654212
  90.4 11.5 %copy-start.8 = (bf16[1024,768]{1,0:T(8,128)(2,1)S(1)}, bf16[1024,768]{1,0:T(8,128)(2,1)}, u32[]{:S(2)}) copy-start(bf16[1024,768]{1,0:T(8,128)(2,1)} %copy-done.7) | copy-start | bytes 4718596
  100.3 12.5 %collective-permute-start.4 = (bf16[5888,128]{1,0:T(8,128)(2,1)S(1)}, bf16[5888,128]{1,0:T(8,128)(2,1)S(1)}, u32[]{:S(2)}, u32[]{:S(2)}) collective-permute-start(bf16[5888,128]{1,0:T(8,128)(2,1)S(1)} %get-tuple-element.63), channel_id=1, source_target_pairs={{0,32},{32,0},{1,33},{33,1},{2,34},{34,2},{3,35},{35,3},{4,36},{36... | collective-permute-start | bytes 4521992 | tf_op jit(solution)/shard_map/ppermute | solution.py:360
  110.7 2.1 %collective-permute-start.5 = (bf16[2304,128]{1,0:T(8,128)(2,1)S(1)}, bf16[2304,128]{1,0:T(8,128)(2,1)S(1)}, u32[]{:S(2)}, u32[]{:S(2)}) collective-permute-start(bf16[2304,128]{1,0:T(8,128)(2,1)S(1)} %get-tuple-element.65), channel_id=1, source_target_pairs={{0,32},{32,0},{1,33},{33,1},{2,34},{34,2},{3,35},{35,3},{4,36},{36... | collective-permute-start | bytes 1769480 | tf_op jit(solution)/shard_map/ppermute | solution.py:360
  158.7 38.0 %copy-start = (bf16[1152,768]{1,0:T(8,128)(2,1)S(1)}, bf16[1152,768]{1,0:T(8,128)(2,1)}, u32[]{:S(2)}) copy-start(bf16[1152,768]{1,0:T(8,128)(2,1)} %get-tuple-element.56.cot) | copy-start | bytes 5308420
  158.7 38.0 %copy-start.1 = (bf16[1,1024,768]{2,1,0:T(8,128)(2,1)S(1)}, bf16[1,1024,768]{2,1,0:T(8,128)(2,1)}, u32[]{:S(2)}) copy-start(bf16[1,1024,768]{2,1,0:T(8,128)(2,1)} %param.7) | copy-start | bytes 4718596
  194.4 6.0 %collective-permute-start.6 = (bf16[8192,128]{1,0:T(8,128)(2,1)S(1)}, bf16[8192,128]{1,0:T(8,128)(2,1)S(1)}, u32[]{:S(2)}, u32[]{:S(2)}) collective-permute-start(bf16[8192,128]{1,0:T(8,128)(2,1)S(1)} %bitcast.30), channel_id=1, source_target_pairs={{0,32},{32,0},{1,33},{33,1},{2,34},{34,2},{3,35},{35,3},{4,36},{36... | collective-permute-start | bytes 6291464 | tf_op jit(solution)/shard_map/ppermute | solution.py:360
where the time goes:
time: 205 us; the launch traced here: 204 us
  Pallas kernels  92.5 us (45%)
  blocking collectives  79.3 us (39%)
  starting transfers between devices  15.2 us (7%)
  local copies, waits for them, and re-layouts  14 us (7%)
  waiting for transfers between devices  2.21 us (1%)
    all_to_all x2, blocking collectives, exchange(): return lax.all_to_all(parts, CHIPS, 0, 0, tiled=True)  79.3 us
    pallas_call x1, Pallas kernels, local(): call(k_middle, 4, [scalar(), scalar(), resident, resident, whole(4 * PAD,...  16.9 us
    pallas_call x1, Pallas kernels, local(): call(functools.partial(k_back, factor), 3, [scalar(), scalar(), whole(C,...  16.7 us
    pallas_call x1, Pallas kernels, local(): call(k_top, 4, [scalar(), whole(MID_ROWS, C), resident, c_halo, c_halo, t...  11.2 us
    pallas_call x1, Pallas kernels, local(): call(functools.partial(k_sums_out, factor), 1, [whole(C, 1), wide_top, re...  10.1 us
    pallas_call x1, Pallas kernels, local(): call(functools.partial(k_sums, factor), 1, [scalar(), whole(C, 1), wide_m...  9.9 us
    pallas_call x1, Pallas kernels, local(): call(functools.partial(k_last, factor), STEPS, [scalar(), scalar(), whole...  8.85 us
    ppermute x2, starting transfers between devices, edges(): lax.ppermute(cells[ROWS - rows:], SEQ, [(i, i + 1) for i in range(BLOCKS...  8.71 us
  transfers between devices with their start and end apart: 7, of which 2 were waited for; matrix products, arithmetic and copies ran while one was open for 3% of the time, Pallas kernels for 19%

commit v1 on v0

--- a/solution.py
+++ b/solution.py
@@ -30,17 +30,13 @@
     return lax.dot_general(left, right, (((1,), (0,)), ((), ())), preferred_element_type=F32)
 
 
-def mm_nt(left, right):
-    return lax.dot_general(left, right, (((1,), (1,)), ((), ())), preferred_element_type=F32)
-
-
 def mm_tn(left, right):
     return lax.dot_general(left, right, (((0,), (0,)), ((), ())), preferred_element_type=F32)
 
 
 def swap(pairs_ref):
-    cols = lax.broadcasted_iota(jnp.int32, (C, C), 1)
-    return (cols == pairs_ref[...]).astype(F32).astype(BF)
+    rows = lax.broadcasted_iota(jnp.int32, (C, C), 0)
+    return (rows == pairs_ref[...]).astype(F32).astype(BF)
 
 
 def scale_of(wide):
@@ -98,27 +94,28 @@
     return pre * half, slope
 
 
-def k_enter(pairs, down, x, dcat, normed, inner):
+def k_enter(pairs, down, up, kern, x, dcat, dcat_t, upcat, upcat_t, kern_t, normed, inner):
     @pl.when(pl.program_id(0) == 0)
     def _():
-        dcat[:, :B] = down[...]
-        dcat[:, B:] = mm(swap(pairs), down[...]).astype(BF)
+        s = swap(pairs)
+        for layer in range(2):
+            other = mm(s, down[layer])
+            dcat[layer, :, :B] = down[layer]
+            dcat[layer, :, B:] = other.astype(BF)
+            dcat_t[layer, :B, :] = down[layer].astype(F32).T.astype(BF)
+            dcat_t[layer, B:, :] = other.T.astype(BF)
+            other = mm(up[layer], s)
+            upcat[layer, :B, :] = up[layer]
+            upcat[layer, B:, :] = other.astype(BF)
+            upcat_t[layer, :, :B] = up[layer].astype(F32).T.astype(BF)
+            upcat_t[layer, :, B:] = other.T.astype(BF)
+            for k in range(3):
+                kern_t[layer, k] = kern[layer, k].astype(F32).T.astype(BF)
 
     wide = x[...].astype(F32)
     n = (wide * scale_of(wide)).astype(BF)
     normed[...] = n
-    inner[...] = mm(n, dcat[...]).astype(BF)
-
-
-def k_prep(pairs, down1, up, kern, dcat1, upcat, kern_t):
-    s = swap(pairs)
-    dcat1[:, :B] = down1[...]
-    dcat1[:, B:] = mm(s, down1[...]).astype(BF)
-    for layer in range(2):
-        upcat[layer, :B, :] = up[layer]
-        upcat[layer, B:, :] = mm(up[layer], s).astype(BF)
-        for k in range(3):
-            kern_t[layer, k * B : (k + 1) * B, :] = kern[layer, k].astype(F32).T.astype(BF)
+    inner[...] = mm(n, dcat[0]).astype(BF)
 
 
 def k_middle(dil, block, mid, x, top, bot, dcat0, weight, upcat, dcat,
@@ -127,17 +124,17 @@
 
     @pl.when(pl.program_id(0) == 0)
     def _():
-        lay(field, top[PAD:, :], x[...], bot[: 4 * PAD - PAD, :])
+        lay(field, top[PAD : 4 * PAD, :], x[...], bot[: 3 * PAD, :])
         ends = []
         for halo in (top, bot):
-            wide = halo[...].astype(F32)
+            wide = halo[: 4 * PAD, :].astype(F32)
             ends.append(mm((wide * scale_of(wide)).astype(BF), dcat0[...]).astype(BF))
         lay(pad, ends[0], mid[...], ends[1])
 
     shift(pad, dil[0], start, tm, tp)
     m = centre(pad, start, MID_TILE)
     tc[...] = m
-    g, s = gelu_both(conv(tm[...], tp[...], m, weight[...]))
+    g, s = gelu_both(conv(tm[...], tp[...], m, weight[...].reshape(3 * B, B)))
     g = g.astype(BF)
     act[...] = g
     slope[...] = s.astype(BF)
@@ -150,20 +147,20 @@
     inner[...] = inside(block[0], start - 3 * PAD, mm(n, dcat[...])).astype(BF)
 
 
-def k_top(dil, mid, cot, ctop, cbot, weight, upcat, act, d_pre, tm, tc, tp, pad, grad):
+def k_top(dil, mid, cot, top, bot, weight, upcat_t, act, d_pre, tm, tc, tp, pad, grad):
     start = pl.program_id(0) * TOP_TILE
 
     @pl.when(pl.program_id(0) == 0)
     def _():
         pad[...] = mid[...].astype(F32)
-        lay(grad, ctop[...], cot[...], cbot[...])
-
-    shift(pad, dil[0], start, tm, tp)
+        lay(grad, top[4 * PAD :, :], cot[...], bot[4 * PAD :, :])
+
+    shift(pad, dil[1], start, tm, tp)
     m = centre(pad, start, TOP_TILE)
     tc[...] = m
     rows = pl.ds(pl.multiple_of(start, 16), TOP_TILE)
-    d_act = mm_nt(grad[rows, :], upcat[...])
-    g, s = gelu_both(conv(tm[...], tp[...], m, weight[...]))
+    d_act = mm(grad[rows, :], upcat_t[...])
+    g, s = gelu_both(conv(tm[...], tp[...], m, weight[...].reshape(3 * B, B)))
     act[...] = g.astype(BF)
     d_pre[...] = (d_act * s).astype(BF)
 
@@ -186,9 +183,11 @@
 def weight_sums(factor, pairs, act, cot, taps, d_pre, rest):
     up = mm_tn(act, cot) * factor
     put(rest, 0, up[:B] + mm(up[B:].astype(BF), swap(pairs)))
+    rows_a = jnp.concatenate([tap[:, :B] for tap in taps], axis=1)
+    rows_b = jnp.concatenate([tap[:, B:] for tap in taps[::-1]], axis=1)
+    total = (mm_tn(d_pre[:, :B], rows_a) + mm_tn(d_pre[:, B:], rows_b)) * factor
     for k in range(3):
-        total = mm_tn(taps[k][:, :B], d_pre[:, :B]) + mm_tn(taps[2 - k][:, B:], d_pre[:, B:])
-        put(rest, UP + k * 3 * B, total * factor)
+        put(rest, UP + k * 3 * B, total[:, k * B : (k + 1) * B].T)
     rest[REST - LANES :, :] = jnp.zeros((LANES, LANES), BF)
 
 
@@ -251,24 +250,24 @@
     return scale * d_norm - wide * (scale * scale * scale * mixed)
 
 
-def k_back(factor, dil, block, pairs, mid, weight, normed, stream, cot, ctop, cbot, dcat, upcat, slope,
+def k_back(factor, dil, block, pairs, mid, weight, normed, stream, cot, top, bot, dcat_t, upcat_t, slope,
            grad, d_pre, down, pad, before, after, d_inner, given):
     start = pl.program_id(0) * BACK_TILE
 
     @pl.when(pl.program_id(0) == 0)
     def _():
         pad[...] = mid[...].astype(F32)
-        lay(given, ctop[PAD:, :], cot[...], cbot[:PAD, :])
-
-    shift(pad, dil[0], start, before, after)
-    di = conv(after[...], before[...], centre(pad, start, BACK_TILE), weight[...]).astype(BF)
+        lay(given, top[5 * PAD :, :], cot[...], bot[4 * PAD : 5 * PAD, :])
+
+    shift(pad, dil[1], start, before, after)
+    di = conv(after[...], before[...], centre(pad, start, BACK_TILE), weight[...].reshape(3 * B, B)).astype(BF)
     rows = pl.ds(pl.multiple_of(start, 16), BACK_TILE)
     saved = pl.ds(pl.multiple_of(start + 2 * PAD, 16), BACK_TILE)
     d_inner[rows, :] = di
-    g = given[rows, :].astype(F32) + norm_back(stream[saved, :], mm_nt(di, dcat[...]))
+    g = given[rows, :].astype(F32) + norm_back(stream[saved, :], mm(di, dcat_t[...]))
     g = inside(block[0], start - PAD, g).astype(BF)
     grad[...] = g
-    d_pre[...] = (mm_nt(g, upcat[...]) * slope[saved, :].astype(F32)).astype(BF)
+    d_pre[...] = (mm(g, upcat_t[...]) * slope[saved, :].astype(F32)).astype(BF)
 
     @pl.when(pl.program_id(0) == pl.num_programs(0) - 1)
     def _():
@@ -283,7 +282,7 @@
         pad[...] = mid[...].astype(F32)
 
     shift(pad, dil[0], start, before, after)
-    di = conv(after[...], before[...], centre(pad, start, TILE), weight[...]).astype(BF)
+    di = conv(after[...], before[...], centre(pad, start, TILE), weight[...].reshape(3 * B, B)).astype(BF)
     d_inner[pl.ds(pl.multiple_of(start, 16), TILE), :] = di
 
     @pl.when(pl.program_id(0) == pl.num_programs(0) - 1)
@@ -292,9 +291,9 @@
         sort_out(core, down, upper, send, keep)
 
 
-def k_input(d_inner, x, cot, dcat, out):
+def k_input(d_inner, x, cot, dcat_t, out):
     rows = pl.ds(pl.multiple_of(pl.program_id(0) * TILE + PAD, 16), TILE)
-    out[...] = (cot[rows, :].astype(F32) + norm_back(x[...], mm_nt(d_inner[...], dcat[...]))).astype(BF)
+    out[...] = (cot[rows, :].astype(F32) + norm_back(x[...], mm(d_inner[...], dcat_t[...]))).astype(BF)
 
 
 def tile(rows=TILE):
@@ -342,9 +341,11 @@
     return pltpu.VMEM((rows, C), kind)
 
 
-def edges(cells, rows):
-    top = lax.ppermute(cells[ROWS - rows :], SEQ, [(i, i + 1) for i in range(BLOCKS - 1)])
-    bot = lax.ppermute(cells[:rows], SEQ, [(i + 1, i) for i in range(BLOCKS - 1)])
+def edges(x, cot):
+    last = jnp.concatenate([x[ROWS - 4 * PAD :], cot[ROWS - 2 * PAD :]], axis=0)
+    first = jnp.concatenate([x[: 4 * PAD], cot[: 2 * PAD]], axis=0)
+    top = lax.ppermute(last, SEQ, [(i, i + 1) for i in range(BLOCKS - 1)])
+    bot = lax.ppermute(first, SEQ, [(i + 1, i) for i in range(BLOCKS - 1)])
     return top, bot
 
 
@@ -363,39 +364,31 @@
 def local(features, cotangent, strand_pairs, dilations, down_weight, conv_weight, up_weight):
     x = features[0]
     cot = cotangent[0]
-    pairs = strand_pairs.reshape(C, 1)
+    pairs = strand_pairs.reshape(1, C)
     factor = 1.0 / math.sqrt(131072.0)
-    dil = [dilations[layer : layer + 1] for layer in range(2)]
-    kern = [conv_weight[layer].reshape(3 * B, B) for layer in range(2)]
     block = lax.axis_index(SEQ).reshape(1)
-    square = whole(C, C)
     resident = whole(ROWS, C)
-    taps_w = whole(3 * B, B)
-
-    top, bot = edges(x, 4 * PAD)
-    ctop, cbot = edges(cot, 2 * PAD)
-    dcat0, normed0, inner0 = call(
-        k_enter, STEPS, [whole(C, 1), whole(C, B), tile()],
-        [(square, shape(C, C)), FULL, FULL], [], UNIT, "enter",
-    )(pairs, down_weight[0], x)
-    dcat1, upcat, kern_t = call(
-        k_prep, 1, [whole(C, 1), whole(C, B), whole(2, B, C), whole(2, 3, B, B)],
-        [(square, shape(C, C)), (whole(2, C, C), shape(2, C, C)), (whole(2, 3 * B, B), shape(2, 3 * B, B))],
-        [], 2.5 * UNIT, "prep",
-    )(pairs, down_weight[1], up_weight, conv_weight)
-    up0, up1 = upcat[0], upcat[1]
+    taps_w = [pl.BlockSpec((None, 3, B, B), lambda i, n=n: (n, 0, 0, 0)) for n in range(2)]
+    square_of = [pl.BlockSpec((None, C, C), lambda i, n=n: (n, 0, 0)) for n in range(2)]
+    halo = whole(6 * PAD, C)
+
+    top, bot = edges(x, cot)
+    squares = (whole(2, C, C), shape(2, C, C))
+    dcat, dcat_t, upcat, upcat_t, kern_t, normed0, inner0 = call(
+        k_enter, STEPS, [whole(1, C), whole(2, C, B), whole(2, B, C), whole(2, 3, B, B), tile()],
+        [squares] * 4 + [(whole(2, 3, B, B), shape(2, 3, B, B)), FULL, FULL], [], 3 * UNIT, "enter",
+    )(pairs, down_weight, up_weight, conv_weight, x)
     mid = (tile(MID_TILE), shape(MID_ROWS, C))
     act0, slope0, tm0, tc0, tp0, stream1, normed1, inner1 = call(
         k_middle, 4,
-        [scalar(), scalar(), resident, resident, whole(4 * PAD, C), whole(4 * PAD, C), square, taps_w, square, square],
+        [scalar(), scalar(), resident, resident, halo, halo, square_of[0], taps_w[0], square_of[0], square_of[1]],
         [mid] * 8, [store(ROWS + 8 * PAD, F32), store(MID_ROWS)], 6 * UNIT, "middle",
-    )(dil[0], block, inner0, x, top, bot, dcat0, kern[0], up0, dcat1)
+    )(dilations, block, inner0, x, top, bot, dcat, conv_weight, upcat, dcat)
     upper = (tile(TOP_TILE), shape(TOP_ROWS, C))
-    c_halo = whole(2 * PAD, C)
     act1, d_pre1, tm1, tc1, tp1 = call(
-        k_top, 4, [scalar(), whole(MID_ROWS, C), resident, c_halo, c_halo, taps_w, square],
+        k_top, 4, [scalar(), whole(MID_ROWS, C), resident, halo, halo, taps_w[1], square_of[1]],
         [upper] * 5, [store(MID_ROWS, F32), store(TOP_ROWS)], 3 * UNIT, "top",
-    )(dil[1], inner1, cot, ctop, cbot, kern[1], up1)
+    )(dilations, inner1, cot, top, bot, conv_weight, upcat_t)
     core = lax.axis_index("core").reshape(1)
     sums = (whole(REST, LANES), shape(REST, LANES))
     downs = (whole(DOWN, LANES), shape(DOWN, LANES))
@@ -404,38 +397,38 @@
     wide_top, wide_mid, wide_back = whole(TOP_ROWS, C), whole(MID_ROWS, C), whole(BACK_ROWS, C)
     rest1, out = call(
         functools.partial(k_sums_out, factor), 1,
-        [whole(C, 1), wide_top, resident] + [wide_top] * 4 + [wide_mid, square],
+        [whole(1, C), wide_top, resident] + [wide_top] * 4 + [wide_mid, square_of[1]],
         [sums, (resident, shape(ROWS, C))], [], 4 * UNIT, "sums_out",
-    )(pairs, act1, cot, tm1, tc1, tp1, d_pre1, stream1, up1)
+    )(pairs, act1, cot, tm1, tc1, tp1, d_pre1, stream1, upcat)
     back = (tile(BACK_TILE), shape(BACK_ROWS, C))
     grad, d_pre0, down1 = call(
         functools.partial(k_back, factor), 3,
-        [scalar(), scalar(), whole(C, 1), wide_top, taps_w, wide_mid, wide_mid, resident, c_halo, c_halo,
-         square, square, wide_mid],
+        [scalar(), scalar(), whole(1, C), wide_top, taps_w[1], wide_mid, wide_mid, resident, halo, halo,
+         square_of[1], square_of[0], wide_mid],
         [back, back, downs],
         [store(TOP_ROWS, F32), store(BACK_TILE), store(BACK_TILE), store(BACK_ROWS), store(BACK_ROWS)],
         5 * UNIT, "back",
-    )(dil[1], block, pairs, d_pre1, kern_t[1], normed1, stream1, cot, ctop, cbot, dcat1, up0, slope0)
+    )(dilations, block, pairs, d_pre1, kern_t, normed1, stream1, cot, top, bot, dcat_t, upcat_t, slope0)
     send_a, keep_a = call(
         functools.partial(k_sums, factor), 1,
-        [scalar(), whole(C, 1), wide_mid, wide_back, wide_mid, wide_mid, wide_mid, wide_back, sums[0]],
+        [scalar(), whole(1, C), wide_mid, wide_back, wide_mid, wide_mid, wide_mid, wide_back, sums[0]],
         [sums, sums], [pltpu.VMEM((REST, LANES), BF)], 3 * UNIT, "sums",
     )(core, pairs, act0, grad, tm0, tc0, tp0, d_pre0, rest1)
     send_b, keep_b, d_inner0 = call(
         functools.partial(k_last, factor), STEPS,
-        [scalar(), scalar(), whole(C, 1), wide_back, taps_w, resident, downs[0]],
+        [scalar(), scalar(), whole(1, C), wide_back, taps_w[0], resident, downs[0]],
         [downs, downs, (resident, shape(ROWS, C))],
         [store(BACK_ROWS, F32), store(TILE), store(TILE), pltpu.VMEM((DOWN, LANES), BF)],
         3 * UNIT, "last",
-    )(core, dil[0], pairs, d_pre0, kern_t[0], normed0, down1)
+    )(core, dilations, pairs, d_pre0, kern_t, normed0, down1)
     (parts,) = call(
         k_join, 1, [sums[0], sums[0], downs[0], downs[0]], [joined], [], 0, "join",
     )(keep_a, other_core(send_a), keep_b, other_core(send_b))
     parts = exchange(parts.reshape(SHARES))
     (shared,) = call(k_share, 1, [shares[0]], [shares], [], 0, "share")(parts)
     (input_grad,) = call(
-        k_input, STEPS, [tile(), tile(), wide_back, square], [FULL], [], UNIT, "input",
-    )(d_inner0, x, grad, dcat0)
+        k_input, STEPS, [tile(), tile(), wide_back, square_of[0]], [FULL], [], UNIT, "input",
+    )(d_inner0, x, grad, dcat_t)
     own = exchange(shared).reshape(REST + DOWN, LANES)
     layered = lambda *dims: (
         pl.BlockSpec((1,) + dims, lambda i: (i,) + (0,) * len(dims)), shape(2, *dims, kind=F32)

time: 205 us -> 194 us (0.946)
  local copies, waits for them, and re-layouts: 14 us -> 5.18 us
  starting transfers between devices: 15.2 us -> 9.6 us
  waiting for transfers between devices: 2.21 us -> 5.78 us
    ppermute x4 -> x2, starting transfers between devices: 11.3 us -> 5.33 us  [the longest x1 4.05 us: edges(): top = lax.ppermute(last, SEQ, [(i, i + 1) for i in range(BLOCKS - 1)])]
    slice x4 -> x2, local copies, waits for them, and re-layouts: 7.65 us -> 2.37 us  [edges(): first = jnp.concatenate([x[:4 * PAD], cot[:2 * PAD]], axis=0)]
    ppermute x4 -> x2, waiting for transfers between devices: 0.01 us -> 3.8 us  [the longest x1 3.8 us: edges(): bot = lax.ppermute(first, SEQ, [(i + 1, i) for i in range(BLOCKS - 1)])]
    unnamed x34 -> x24, local copies, waits for them, and re-layouts: 4.82 us -> 2.81 us
    pallas_call x8 -> x7, Pallas kernels: 77.8 us -> 77.9 us  [the longest x1 16.7 us: local(): call(functools.partial(k_back, factor), 3, [scalar(), scalar(), whole(1,...]
  transfers between devices with their start and end apart: 7 -> 5, of which waited for: 2 -> 2; matrix products, arithmetic and copies ran while one was open for 3% -> 0% of each run, Pallas kernels for 19% -> 12%
where the time goes in v1:
time: 194 us; the launch traced here: 193 us
  Pallas kernels  92.3 us (48%)
  blocking collectives  77.8 us (40%)
  starting transfers between devices  9.6 us (5%)
  waiting for transfers between devices  5.78 us (3%)
  local copies, waits for them, and re-layouts  5.18 us (3%)
    all_to_all x2, blocking collectives, exchange(): return lax.all_to_all(parts, CHIPS, 0, 0, tiled=True)  77.8 us
    pallas_call x1, Pallas kernels, local(): call(functools.partial(k_back, factor), 3, [scalar(), scalar(), whole(1,...  16.7 us
    pallas_call x1, Pallas kernels, local(): call(k_middle, 4, [scalar(), scalar(), resident, resident, halo, halo, sq...  16.1 us
    pallas_call x1, Pallas kernels, local(): call(k_top, 4, [scalar(), whole(MID_ROWS, C), resident, halo, halo, taps_...  11 us
    pallas_call x1, Pallas kernels, local(): call(k_enter, STEPS, [whole(1, C), whole(2, C, B), whole(2, B, C), whole(...  10.8 us
    pallas_call x1, Pallas kernels, local(): call(functools.partial(k_sums_out, factor), 1, [whole(1, C), wide_top, re...  9.84 us
    pallas_call x1, Pallas kernels, local(): call(functools.partial(k_sums, factor), 1, [scalar(), whole(1, C), wide_m...  8.82 us
    pallas_call x1, Pallas kernels, local(): call(functools.partial(k_last, factor), STEPS, [scalar(), scalar(), whole...  8.49 us
  transfers between devices with their start and end apart: 5, of which 2 were waited for; matrix products, arithmetic and copies ran while one was open for 0% of the time, Pallas kernels for 12%

profile of v1, /device:TPU:1, one launch (start us, length us, event | category | flops | bytes accessed | tf_op | source)
XLA Modules:
  0.0 193.1 jit_solution(17544862956067432295)
XLA Ops:
  0.6 1.1 slice_bitcast_fusion.2
  1.7 0.0 copy-start.11
  1.7 0.0 copy-start.5
  1.7 0.0 copy-start.6
  1.7 1.3 slice_bitcast_fusion
  3.0 0.9 pad_maximum_fusion
  3.9 4.1 %collective-permute-start = (bf16[384,768]{1,0:T(8,128)(2,1)}, bf16[384,768]{1,0:T(8,128)(2,1)S(1)}, u32[]{:S(2)}, u32[]{:S(2)}) collective-permute-start(bf16[384,768]{1,0:T(8,128)(2,1)} %pad_maximum_fusion), channel_id=1, source_target_pairs={{0,1},{1,2},{2,3},{3,4},{4,5},{5,6},{6,7},{7,8},{8,9},{9,10},{10,1... | collective-permute-start | bytes 1769480 | tf_op jit(solution)/shard_map/ppermute | solution.py:347
  8.0 0.9 pad_maximum_fusion.1
  8.8 1.3 collective-permute-start.1
  10.1 0.0 copy-done.11
  10.1 0.0 copy-done.5
  10.2 0.0 copy-done.6
  10.2 0.0 copy-start.2
  10.2 0.0 copy-start.4
  10.2 0.0 copy-start.7
  10.2 10.8 %enter.1 = (bf16[2,768,768]{2,1,0:T(8,128)(2,1)}, bf16[2,768,768]{2,1,0:T(8,128)(2,1)}, bf16[2,768,768]{2,1,0:T(8,128)(2,1)}, bf16[2,768,768]{2,1,0:T(8,128)(2,1...) custom-call(s32[1,768]{1,0:T(1,128)S(1)} %reshape.29.pairs, ...), custom_call_target="tpu_custom_call" | custom-call | flops 3623878656 | bytes 28704768 | tf_op jit(solution)/shard_map/enter/pallas_call | solution.py:377
  21.0 0.0 copy-start.9
  21.0 0.0 collective-permute-done.top
  21.0 3.8 %collective-permute-done.1.bot = bf16[384,768]{1,0:T(8,128)(2,1)S(1)} collective-permute-done((bf16[384,768]{1,0:T(8,128)(2,1)}, bf16[384,768]{1,0:T(8,128)(2,1)S(1)}, u32[]{:S(2)}, u32[]{:S(2)}) %collective-permute-start.1) | collective-permute-done | bytes 589856 | tf_op jit(solution)/shard_map/ppermute | solution.py:348
  24.8 0.0 copy-done.2
  24.8 0.0 copy-done.4
  24.8 0.0 copy-done.7
  24.8 0.0 copy-start.3
  24.8 16.1 %middle.1 = (bf16[1408,768]{1,0:T(8,128)(2,1)}, bf16[1408,768]{1,0:T(8,128)(2,1)}, bf16[1408,768]{1,0:T(8,128)(2,1)}, bf16[1408,768]{1,0:T(8,128)(2,1)}, bf16[14...) custom-call(s32[2]{0:T(128)S(1)} %copy-done.7, ...), custom_call_target="tpu_custom_call" | custom-call | flops 7247757312 | bytes 34603008 | tf_op jit(solution)/shard_map/middle/pallas_call | solution.py:382
  40.9 0.0 copy-done.9
  41.0 0.0 copy-done.3
  41.0 11.0 %top.1 = (bf16[1280,768]{1,0:T(8,128)(2,1)}, bf16[1280,768]{1,0:T(8,128)(2,1)}, bf16[1280,768]{1,0:T(8,128)(2,1)}, bf16[1280,768]{1,0:T(8,128)(2,1)}, bf16[1280,768]{1,0:T(8,128)(2,1)}) custom-call(s32[2]{0:T(128)S(1)} %copy-done.7, bf16[1408,768]{1,0:T(8,128)(2,1)} %get-tuple-element.41.mid, bf16[1024,768]{1,0:T(8,128)(2,1)S(1)} %bitcast.21, ...), custom_call_target="tpu_custom_call" | custom-call | flops 3623878656 | bytes 19660800 | tf_op jit(solution)/shard_map/top/pallas_call | solution.py:388
  52.0 0.0 copy-start.8
  52.0 1.5 copy-done.8
  53.5 9.8 %sums_out.1 = (bf16[5888,128]{1,0:T(8,128)(2,1)S(1)}, bf16[1024,768]{1,0:T(8,128)(2,1)}) custom-call(s32[1,768]{1,0:T(1,128)S(1)} %reshape.29.pairs, bf16[1280,768]{1,0:T(8,128)(2,1)S(1)} %copy-done.8, bf16[1024,768]{1,0:T(8,128)(2,1)S(1)} %bitcast.22, bf16[1280,768]{1,0:T(8,128)(2,1)} %get-tuple-element.44.tm, bf16[1280,768]{1,0:T(8,128)(2,1)} %get-tuple-element.45.tc, ...), custom_call_target="tpu_custom_call" | custom-call | flops 4831838208 | bytes 6160384 | tf_op jit(solution)/shard_map/sums_out/pallas_call | solution.py:398
  63.4 16.7 %back.1 = (bf16[1152,768]{1,0:T(8,128)(2,1)S(1)}, bf16[1152,768]{1,0:T(8,128)(2,1)}, bf16[2304,128]{1,0:T(8,128)(2,1)S(1)}) custom-call(s32[2]{0:T(128)S(1)} %copy-done.7, s32[1]{0:T(128)} %bitcast.block, s32[1,768]{1,0:T(1,128)S(1)} %reshape.29.pairs, bf16[1280,768]{1,0:T(8,128)(2,1)} %get-tuple-element.47.d_pre.mid, ...), custom_call_target="tpu_custom_call" | custom-call | flops 6039797760 | bytes 8257536 | tf_op jit(solution)/shard_map/back/pallas_call | solution.py:404
  80.0 0.0 copy-start
  80.0 1.2 copy-done
  81.3 0.0 copy-start.10
  81.3 8.8 %sums.1 = (bf16[5888,128]{1,0:T(8,128)(2,1)S(1)}, bf16[5888,128]{1,0:T(8,128)(2,1)S(1)}) custom-call(s32[1]{0:T(128)} %bitcast.8.core, s32[1,768]{1,0:T(1,128)S(1)} %reshape.29.pairs, bf16[1408,768]{1,0:T(8,128)(2,1)} %get-tuple-element.59.act, bf16[1152,768]{1,0:T(8,128)(2,1)} %copy-done, bf16[1408,768]{1,0:T(8,128)(2,1)} %get-tuple-element.60.tm, ...), custom_call_target="tpu_custom_call" | custom-call | flops 3623878656 | bytes 6029312 | tf_op jit(solution)/shard_map/sums/pallas_call | solution.py:412
  90.1 1.9 collective-permute-start.2
  92.0 0.0 copy-done.10
  92.0 8.5 %last.1 = (bf16[2304,128]{1,0:T(8,128)(2,1)S(1)}, bf16[2304,128]{1,0:T(8,128)(2,1)S(1)}, bf16[1024,768]{1,0:T(8,128)(2,1)S(1)}) custom-call(s32[1]{0:T(128)} %bitcast.8.core, s32[2]{0:T(128)S(1)} %copy-done.7, s32[1,768]{1,0:T(1,128)S(1)} %reshape.29.pairs, bf16[1152,768]{1,0:T(8,128)(2,1)} %get-tuple-element.54.mid.d_pre, ...), custom_call_target="tpu_custom_call" | custom-call | flops 3623878656 | bytes 5505024 | tf_op jit(solution)/shard_map/last/pallas_call | solution.py:417
  100.5 0.1 collective-permute-start.3
  100.6 2.0 %collective-permute-done.3.got_b = bf16[2304,128]{1,0:T(8,128)(2,1)S(1)} collective-permute-done((bf16[2304,128]{1,0:T(8,128)(2,1)S(1)}, bf16[2304,128]{1,0:T(8,128)(2,1)S(1)}, u32[]{:S(2)}, u32[]{:S(2)}) %collective-permute-start.3) | collective-permute-done | bytes 589856 | tf_op jit(solution)/shard_map/ppermute | solution.py:361
  102.6 0.0 collective-permute-done.2.got_a
  102.6 1.8 join.1
  104.4 42.1 %all_to_all.10.parts = bf16[64,128,128]{2,1,0:T(8,128)(2,1)S(1)} all-to-all(bf16[64,128,128]{2,1,0:T(8,128)(2,1)} %bitcast.24), channel_id=1, replica_groups=mesh['xh'=2,'core'=2,'z'=4,'xl'=2,'y'=4] {'xh','z','xl','y'}, dimensions={0} | all-to-all | bytes 4194304 | tf_op jit(solution)/shard_map/all_to_all | solution.py:357
  146.5 0.5 share.1
  147.0 0.0 copy-start.1
  147.0 35.6 %all_to_all.11 = bf16[64,128,128]{2,1,0:T(8,128)(2,1)S(1)} all-to-all(bf16[64,128,128]{2,1,0:T(8,128)(2,1)S(1)} %share.1), channel_id=1, replica_groups=mesh['xh'=2,'core'=2,'z'=4,'xl'=2,'y'=4] {'xh','z','xl','y'}, dimensions={0} | all-to-all | bytes 4194304 | tf_op jit(solution)/shard_map/all_to_all | solution.py:357
  182.6 2.2 %collective-permute-start.4 = (bf16[8192,128]{1,0:T(8,128)(2,1)S(1)}, bf16[8192,128]{1,0:T(8,128)(2,1)S(1)}, u32[]{:S(2)}, u32[]{:S(2)}) collective-permute-start(bf16[8192,128]{1,0:T(8,128)(2,1)S(1)} %bitcast.16), channel_id=1, source_target_pairs={{0,32},{32,0},{1,33},{33,1},{2,34},{34,2},{3,35},{35,3},{4,36},{36... | collective-permute-start | bytes 6291464 | tf_op jit(solution)/shard_map/ppermute | solution.py:361
  184.9 0.0 copy-done.1
  184.9 4.7 %input.1 = bf16[1024,768]{1,0:T(8,128)(2,1)} custom-call(bf16[1024,768]{1,0:T(8,128)(2,1)S(1)} %get-tuple-element.57.d_inner, bf16[1024,768]{1,0:T(8,128)(2,1)S(1)} %bitcast.20, bf16[1152,768]{1,0:T(8,128)(2,1)S(1)} %copy-done.1, bf16[2,768,768]{2,1,0:T(8,128)(2,1)} %get-tuple-element.52.dcat_t), custom_call_target="tpu_custom_call" | custom-call | flops 1207959552 | bytes 3145728 | tf_op jit(solution)/shard_map/input/pallas_call | solution.py:429
  189.5 0.0 collective-permute-done.4.other
  189.5 3.6 %finish.1 = (f32[2,768,384]{2,1,0:T(8,128)}, f32[2,3,384,384]{3,2,1,0:T(8,128)}, f32[2,384,768]{2,1,0:T(8,128)}) custom-call(s32[1]{0:T(128)} %bitcast.8.core, bf16[8192,128]{1,0:T(8,128)(2,1)S(1)} %bitcast.17, bf16[8192,128]{1,0:T(8,128)(2,1)S(1)} %collective-permute-done.4.other), custom_call_target="tpu_custom_call" | custom-call | bytes 8257536 | tf_op jit(solution)/shard_map/finish/pallas_call | solution.py:436
  (1 shorter events, 0.0 us)
Async XLA Ops:
  1.7 8.4 %copy-start.11 = (s32[768]{0:T(1024)S(1)}, s32[768]{0:T(1024)}, u32[]{:S(2)}) copy-start(s32[768]{0:T(1024)} %param.9) | copy-start | bytes 9220
  1.7 8.4 %copy-start.5 = (bf16[2,768,384]{2,1,0:T(8,128)(2,1)S(1)}, bf16[2,768,384]{2,1,0:T(8,128)(2,1)}, u32[]{:S(2)}) copy-start(bf16[2,768,384]{2,1,0:T(8,128)(2,1)} %down.1) | copy-start | bytes 3538948
  1.7 8.4 %copy-start.6 = (bf16[2,384,768]{2,1,0:T(8,128)(2,1)S(1)}, bf16[2,384,768]{2,1,0:T(8,128)(2,1)}, u32[]{:S(2)}) copy-start(bf16[2,384,768]{2,1,0:T(8,128)(2,1)} %up.1) | copy-start | bytes 3538948
  3.9 17.1 %collective-permute-start = (bf16[384,768]{1,0:T(8,128)(2,1)}, bf16[384,768]{1,0:T(8,128)(2,1)S(1)}, u32[]{:S(2)}, u32[]{:S(2)}) collective-permute-start(bf16[384,768]{1,0:T(8,128)(2,1)} %pad_maximum_fusion), channel_id=1, source_target_pairs={{0,1},{1,2},{2,3},{3,4},{4,5},{5,6},{6,7},{7,8},{8,9},{9,10},{10,1... | collective-permute-start | bytes 1769480 | tf_op jit(solution)/shard_map/ppermute | solution.py:347
  8.8 16.0 %collective-permute-start.1 = (bf16[384,768]{1,0:T(8,128)(2,1)}, bf16[384,768]{1,0:T(8,128)(2,1)S(1)}, u32[]{:S(2)}, u32[]{:S(2)}) collective-permute-start(bf16[384,768]{1,0:T(8,128)(2,1)} %pad_maximum_fusion.1), channel_id=1, source_target_pairs={{1,0},{2,1},{3,2},{4,3},{5,4},{6,5},{7,6},{8,7},{9,8},{10,9},{11,1... | collective-permute-start | bytes 1769480 | tf_op jit(solution)/shard_map/ppermute | solution.py:348
  10.2 14.6 %copy-start.2 = (bf16[1,1024,768]{2,1,0:T(8,128)(2,1)S(1)}, bf16[1,1024,768]{2,1,0:T(8,128)(2,1)}, u32[]{:S(2)}) copy-start(bf16[1,1024,768]{2,1,0:T(8,128)(2,1)} %param.7) | copy-start | bytes 4718596
  10.2 14.6 %copy-start.4 = (bf16[2,3,384,384]{3,2,1,0:T(8,128)(2,1)S(1)}, bf16[2,3,384,384]{3,2,1,0:T(8,128)(2,1)}, u32[]{:S(2)}) copy-start(bf16[2,3,384,384]{3,2,1,0:T(8,128)(2,1)} %weight.3) | copy-start | bytes 5308420
  10.2 14.6 %copy-start.7 = (s32[2]{0:T(128)S(1)}, s32[2]{0:T(128)}, u32[]{:S(2)}) copy-start(s32[2]{0:T(128)} %dil.7) | copy-start | bytes 28
  21.0 20.0 %copy-start.9 = (bf16[1024,768]{1,0:T(8,128)(2,1)}, bf16[1024,768]{1,0:T(8,128)(2,1)S(1)}, u32[]{:S(2)}) copy-start(bf16[1024,768]{1,0:T(8,128)(2,1)S(1)} %get-tuple-element.55.normed) | copy-start | bytes 4718596
  24.8 16.2 %copy-start.3 = (bf16[1,1024,768]{2,1,0:T(8,128)(2,1)S(1)}, bf16[1,1024,768]{2,1,0:T(8,128)(2,1)}, u32[]{:S(2)}) copy-start(bf16[1,1024,768]{2,1,0:T(8,128)(2,1)} %param.8) | copy-start | bytes 4718596
  52.0 1.5 copy-start.8
  80.0 1.2 copy-start
  81.3 10.8 %copy-start.10 = (bf16[1024,768]{1,0:T(8,128)(2,1)S(1)}, bf16[1024,768]{1,0:T(8,128)(2,1)}, u32[]{:S(2)}) copy-start(bf16[1024,768]{1,0:T(8,128)(2,1)} %copy-done.9) | copy-start | bytes 4718596
  90.1 12.5 %collective-permute-start.2 = (bf16[5888,128]{1,0:T(8,128)(2,1)S(1)}, bf16[5888,128]{1,0:T(8,128)(2,1)S(1)}, u32[]{:S(2)}, u32[]{:S(2)}) collective-permute-start(bf16[5888,128]{1,0:T(8,128)(2,1)S(1)} %get-tuple-element.65), channel_id=1, source_target_pairs={{0,32},{32,0},{1,33},{33,1},{2,34},{34,2},{3,35},{35,3},{4,36},{36... | collective-permute-start | bytes 4521992 | tf_op jit(solution)/shard_map/ppermute | solution.py:361
  100.5 2.1 %collective-permute-start.3 = (bf16[2304,128]{1,0:T(8,128)(2,1)S(1)}, bf16[2304,128]{1,0:T(8,128)(2,1)S(1)}, u32[]{:S(2)}, u32[]{:S(2)}) collective-permute-start(bf16[2304,128]{1,0:T(8,128)(2,1)S(1)} %get-tuple-element.67), channel_id=1, source_target_pairs={{0,32},{32,0},{1,33},{33,1},{2,34},{34,2},{3,35},{35,3},{4,36},{36... | collective-permute-start | bytes 1769480 | tf_op jit(solution)/shard_map/ppermute | solution.py:361
  147.0 37.9 %copy-start.1 = (bf16[1152,768]{1,0:T(8,128)(2,1)S(1)}, bf16[1152,768]{1,0:T(8,128)(2,1)}, u32[]{:S(2)}) copy-start(bf16[1152,768]{1,0:T(8,128)(2,1)} %copy-done) | copy-start | bytes 5308420
  182.6 6.9 %collective-permute-start.4 = (bf16[8192,128]{1,0:T(8,128)(2,1)S(1)}, bf16[8192,128]{1,0:T(8,128)(2,1)S(1)}, u32[]{:S(2)}, u32[]{:S(2)}) collective-permute-start(bf16[8192,128]{1,0:T(8,128)(2,1)S(1)} %bitcast.16), channel_id=1, source_target_pairs={{0,32},{32,0},{1,33},{33,1},{2,34},{34,2},{3,35},{35,3},{4,36},{36... | collective-permute-start | bytes 6291464 | tf_op jit(solution)/shard_map/ppermute | solution.py:361

commit v2 on v1

--- a/solution.py
+++ b/solution.py
@@ -51,26 +51,26 @@
         start += rows
 
 
-def shift(pad, dil, start, before, after):
+def shift(cells, dil, start, before, after):
     rows = before.shape[0]
-    base = pl.multiple_of(start + PAD, 8)
-
-    @pl.when(dil >= 8)
+    base = pl.multiple_of(start + PAD, 16)
+
+    @pl.when(dil >= 16)
     def _():
         for sign, ref in ((-1, before), (1, after)):
-            ref[...] = pad[pl.ds(pl.multiple_of(base + sign * dil, 8), rows), :].astype(BF)
-
-    for small in (1, 2, 4):
+            ref[...] = cells[pl.ds(pl.multiple_of(base + sign * dil, 16), rows), :]
+
+    for small in (1, 2, 4, 8):
 
         @pl.when(dil == small)
         def _():
-            window = pad[pl.ds(pl.multiple_of(base - 8, 8), rows + 16), :]
-            before[...] = window[8 - small : 8 - small + rows].astype(BF)
-            after[...] = window[8 + small : 8 + small + rows].astype(BF)
-
-
-def centre(pad, start, rows):
-    return pad[pl.ds(pl.multiple_of(start + PAD, 8), rows), :].astype(BF)
+            window = cells[pl.ds(pl.multiple_of(base - 16, 16), rows + 32), :].astype(F32)
+            before[...] = window[16 - small : 16 - small + rows].astype(BF)
+            after[...] = window[16 + small : 16 + small + rows].astype(BF)
+
+
+def centre(cells, start, rows):
+    return cells[pl.ds(pl.multiple_of(start + PAD, 16), rows), :]
 
 
 def conv(first, last, mid, weight):
@@ -88,10 +88,10 @@
 
 def gelu_both(pre):
     sq = pre * pre
-    t = jnp.tanh(ROOT * (pre + CUBE * (pre * sq)))
+    t = jnp.tanh(pre * (ROOT + (ROOT * CUBE) * sq))
     half = 0.5 + 0.5 * t
-    slope = half + (0.5 * pre) * ((1.0 - t * t) * (ROOT + (3.0 * CUBE * ROOT) * sq))
-    return pre * half, slope
+    act = pre * half
+    return act, half + (act * (1.0 - t)) * (ROOT + (3.0 * CUBE * ROOT) * sq)
 
 
 def k_enter(pairs, down, up, kern, x, dcat, dcat_t, upcat, upcat_t, kern_t, normed, inner):
@@ -119,7 +119,7 @@
 
 
 def k_middle(dil, block, mid, x, top, bot, dcat0, weight, upcat, dcat,
-             act, slope, tm, tc, tp, stream, normed, inner, pad, field):
+             act, slope, tm, tp, stream, normed, inner, pad, field):
     start = pl.program_id(0) * MID_TILE
 
     @pl.when(pl.program_id(0) == 0)
@@ -133,7 +133,6 @@
 
     shift(pad, dil[0], start, tm, tp)
     m = centre(pad, start, MID_TILE)
-    tc[...] = m
     g, s = gelu_both(conv(tm[...], tp[...], m, weight[...].reshape(3 * B, B)))
     g = g.astype(BF)
     act[...] = g
@@ -147,17 +146,15 @@
     inner[...] = inside(block[0], start - 3 * PAD, mm(n, dcat[...])).astype(BF)
 
 
-def k_top(dil, mid, cot, top, bot, weight, upcat_t, act, d_pre, tm, tc, tp, pad, grad):
+def k_top(dil, mid, cot, top, bot, weight, upcat_t, act, d_pre, tm, tp, grad):
     start = pl.program_id(0) * TOP_TILE
 
     @pl.when(pl.program_id(0) == 0)
     def _():
-        pad[...] = mid[...].astype(F32)
         lay(grad, top[4 * PAD :, :], cot[...], bot[4 * PAD :, :])
 
-    shift(pad, dil[1], start, tm, tp)
-    m = centre(pad, start, TOP_TILE)
-    tc[...] = m
+    shift(mid, dil[1], start, tm, tp)
+    m = centre(mid, start, TOP_TILE)
     rows = pl.ds(pl.multiple_of(start, 16), TOP_TILE)
     d_act = mm(grad[rows, :], upcat_t[...])
     g, s = gelu_both(conv(tm[...], tp[...], m, weight[...].reshape(3 * B, B)))
@@ -206,12 +203,12 @@
 def k_sums_out(factor, pairs, act, cot, tm, tc, tp, d_pre, stream, upcat, rest, out):
     a = own(act, 2 * PAD)
     out[...] = (own(stream, 3 * PAD).astype(F32) + mm(a, upcat[...])).astype(BF)
-    taps = [own(ref, 2 * PAD) for ref in (tm, tc, tp)]
+    taps = [own(tm, 2 * PAD), own(tc, 3 * PAD), own(tp, 2 * PAD)]
     weight_sums(factor, pairs, a, cot[...], taps, own(d_pre, 2 * PAD), rest)
 
 
 def k_sums(factor, core, pairs, act, cot, tm, tc, tp, d_pre, upper, send, keep, rest):
-    taps = [own(ref, 3 * PAD) for ref in (tm, tc, tp)]
+    taps = [own(tm, 3 * PAD), tc[...], own(tp, 3 * PAD)]
     weight_sums(factor, pairs, own(act, 3 * PAD), own(cot, PAD), taps, own(d_pre, PAD), rest)
     sort_out(core, rest, upper, send, keep)
 
@@ -251,16 +248,15 @@
 
 
 def k_back(factor, dil, block, pairs, mid, weight, normed, stream, cot, top, bot, dcat_t, upcat_t, slope,
-           grad, d_pre, down, pad, before, after, d_inner, given):
+           grad, d_pre, down, before, after, d_inner, given):
     start = pl.program_id(0) * BACK_TILE
 
     @pl.when(pl.program_id(0) == 0)
     def _():
-        pad[...] = mid[...].astype(F32)
         lay(given, top[5 * PAD :, :], cot[...], bot[4 * PAD : 5 * PAD, :])
 
-    shift(pad, dil[1], start, before, after)
-    di = conv(after[...], before[...], centre(pad, start, BACK_TILE), weight[...].reshape(3 * B, B)).astype(BF)
+    shift(mid, dil[1], start, before, after)
+    di = conv(after[...], before[...], centre(mid, start, BACK_TILE), weight[...].reshape(3 * B, B)).astype(BF)
     rows = pl.ds(pl.multiple_of(start, 16), BACK_TILE)
     saved = pl.ds(pl.multiple_of(start + 2 * PAD, 16), BACK_TILE)
     d_inner[rows, :] = di
@@ -274,15 +270,11 @@
         down_sum(factor, pairs, own(normed, 3 * PAD), own(d_inner, PAD), down)
 
 
-def k_last(factor, core, dil, pairs, mid, weight, normed, upper, send, keep, d_inner, pad, before, after, down):
+def k_last(factor, core, dil, pairs, mid, weight, normed, upper, send, keep, d_inner, before, after, down):
     start = pl.program_id(0) * TILE
 
-    @pl.when(pl.program_id(0) == 0)
-    def _():
-        pad[...] = mid[...].astype(F32)
-
-    shift(pad, dil[0], start, before, after)
-    di = conv(after[...], before[...], centre(pad, start, TILE), weight[...].reshape(3 * B, B)).astype(BF)
+    shift(mid, dil[0], start, before, after)
+    di = conv(after[...], before[...], centre(mid, start, TILE), weight[...].reshape(3 * B, B)).astype(BF)
     d_inner[pl.ds(pl.multiple_of(start, 16), TILE), :] = di
 
     @pl.when(pl.program_id(0) == pl.num_programs(0) - 1)
@@ -301,7 +293,7 @@
 
 
 def whole(*shape):
-    return pl.BlockSpec(shape, lambda i: (0,) * len(shape))
+    return pl.BlockSpec(shape, lambda i: (0,) * len(shape), pipeline_mode=pl.Buffered(1))
 
 
 def scalar():
@@ -321,7 +313,7 @@
         out_specs=[spec for spec, _ in outs],
         out_shape=[form for _, form in outs],
         scratch_shapes=scratch,
-        compiler_params=pltpu.CompilerParams(vmem_limit_bytes=48 * 1024 * 1024),
+        compiler_params=pltpu.CompilerParams(vmem_limit_bytes=20 * 1024 * 1024),
         cost_estimate=pl.CostEstimate(
             flops=int(flops), bytes_accessed=2 * sum(size(f) for _, f in outs), transcendentals=0
         ),
@@ -368,8 +360,8 @@
     factor = 1.0 / math.sqrt(131072.0)
     block = lax.axis_index(SEQ).reshape(1)
     resident = whole(ROWS, C)
-    taps_w = [pl.BlockSpec((None, 3, B, B), lambda i, n=n: (n, 0, 0, 0)) for n in range(2)]
-    square_of = [pl.BlockSpec((None, C, C), lambda i, n=n: (n, 0, 0)) for n in range(2)]
+    taps_w = [pl.BlockSpec((None, 3, B, B), lambda i, n=n: (n, 0, 0, 0), pipeline_mode=pl.Buffered(1)) for n in range(2)]
+    square_of = [pl.BlockSpec((None, C, C), lambda i, n=n: (n, 0, 0), pipeline_mode=pl.Buffered(1)) for n in range(2)]
     halo = whole(6 * PAD, C)
 
     top, bot = edges(x, cot)
@@ -379,15 +371,15 @@
         [squares] * 4 + [(whole(2, 3, B, B), shape(2, 3, B, B)), FULL, FULL], [], 3 * UNIT, "enter",
     )(pairs, down_weight, up_weight, conv_weight, x)
     mid = (tile(MID_TILE), shape(MID_ROWS, C))
-    act0, slope0, tm0, tc0, tp0, stream1, normed1, inner1 = call(
+    act0, slope0, tm0, tp0, stream1, normed1, inner1 = call(
         k_middle, 4,
         [scalar(), scalar(), resident, resident, halo, halo, square_of[0], taps_w[0], square_of[0], square_of[1]],
-        [mid] * 8, [store(ROWS + 8 * PAD, F32), store(MID_ROWS)], 6 * UNIT, "middle",
+        [mid] * 7, [store(ROWS + 8 * PAD), store(MID_ROWS)], 6 * UNIT, "middle",
     )(dilations, block, inner0, x, top, bot, dcat, conv_weight, upcat, dcat)
     upper = (tile(TOP_TILE), shape(TOP_ROWS, C))
-    act1, d_pre1, tm1, tc1, tp1 = call(
+    act1, d_pre1, tm1, tp1 = call(
         k_top, 4, [scalar(), whole(MID_ROWS, C), resident, halo, halo, taps_w[1], square_of[1]],
-        [upper] * 5, [store(MID_ROWS, F32), store(TOP_ROWS)], 3 * UNIT, "top",
+        [upper] * 4, [store(TOP_ROWS)], 3 * UNIT, "top",
     )(dilations, inner1, cot, top, bot, conv_weight, upcat_t)
     core = lax.axis_index("core").reshape(1)
     sums = (whole(REST, LANES), shape(REST, LANES))
@@ -397,28 +389,28 @@
     wide_top, wide_mid, wide_back = whole(TOP_ROWS, C), whole(MID_ROWS, C), whole(BACK_ROWS, C)
     rest1, out = call(
         functools.partial(k_sums_out, factor), 1,
-        [whole(1, C), wide_top, resident] + [wide_top] * 4 + [wide_mid, square_of[1]],
+        [whole(1, C), wide_top, resident, wide_top, wide_mid, wide_top, wide_top, wide_mid, square_of[1]],
         [sums, (resident, shape(ROWS, C))], [], 4 * UNIT, "sums_out",
-    )(pairs, act1, cot, tm1, tc1, tp1, d_pre1, stream1, upcat)
+    )(pairs, act1, cot, tm1, inner1, tp1, d_pre1, stream1, upcat)
     back = (tile(BACK_TILE), shape(BACK_ROWS, C))
     grad, d_pre0, down1 = call(
         functools.partial(k_back, factor), 3,
         [scalar(), scalar(), whole(1, C), wide_top, taps_w[1], wide_mid, wide_mid, resident, halo, halo,
          square_of[1], square_of[0], wide_mid],
         [back, back, downs],
-        [store(TOP_ROWS, F32), store(BACK_TILE), store(BACK_TILE), store(BACK_ROWS), store(BACK_ROWS)],
+        [store(BACK_TILE), store(BACK_TILE), store(BACK_ROWS), store(BACK_ROWS)],
         5 * UNIT, "back",
     )(dilations, block, pairs, d_pre1, kern_t, normed1, stream1, cot, top, bot, dcat_t, upcat_t, slope0)
     send_a, keep_a = call(
         functools.partial(k_sums, factor), 1,
-        [scalar(), whole(1, C), wide_mid, wide_back, wide_mid, wide_mid, wide_mid, wide_back, sums[0]],
+        [scalar(), whole(1, C), wide_mid, wide_back, wide_mid, resident, wide_mid, wide_back, sums[0]],
         [sums, sums], [pltpu.VMEM((REST, LANES), BF)], 3 * UNIT, "sums",
-    )(core, pairs, act0, grad, tm0, tc0, tp0, d_pre0, rest1)
+    )(core, pairs, act0, grad, tm0, inner0, tp0, d_pre0, rest1)
     send_b, keep_b, d_inner0 = call(
         functools.partial(k_last, factor), STEPS,
         [scalar(), scalar(), whole(1, C), wide_back, taps_w[0], resident, downs[0]],
         [downs, downs, (resident, shape(ROWS, C))],
-        [store(BACK_ROWS, F32), store(TILE), store(TILE), pltpu.VMEM((DOWN, LANES), BF)],
+        [store(TILE), store(TILE), pltpu.VMEM((DOWN, LANES), BF)],
         3 * UNIT, "last",
     )(core, dilations, pairs, d_pre0, kern_t, normed0, down1)
     (parts,) = call(

time: 194 us -> 171 us (0.88)
  Pallas kernels: 92.3 us -> 65 us
  local copies, waits for them, and re-layouts: 5.18 us -> 10.2 us
    pallas_call x1, Pallas kernels: 10.8 us -> 4.91 us  [local(): call(k_enter, STEPS, [whole(1, C), whole(2, C, B), whole(2, B, C), whole(...]
    unnamed x24 -> x30, local copies, waits for them, and re-layouts: 2.81 us -> 7.87 us
    pallas_call x1, Pallas kernels: 8.82 us -> 4.24 us  [local(): call(functools.partial(k_sums, factor), 1, [scalar(), whole(1, C), wide_m...]
    pallas_call x1, Pallas kernels: 9.84 us -> 5.7 us  [local(): call(functools.partial(k_sums_out, factor), 1, [whole(1, C), wide_top, re...]
    pallas_call x1, Pallas kernels: 16.7 us -> 12.6 us  [local(): call(functools.partial(k_back, factor), 3, [scalar(), scalar(), whole(1,...]
    pallas_call x1, Pallas kernels: 11 us -> 8.56 us  [local(): call(k_top, 4, [scalar(), whole(MID_ROWS, C), resident, halo, halo, taps_...]
    pallas_call x1, Pallas kernels: 16.1 us -> 14 us  [local(): call(k_middle, 4, [scalar(), scalar(), resident, resident, halo, halo, sq...]
  transfers between devices with their start and end apart: 5 -> 5, of which waited for: 2 -> 3; matrix products, arithmetic and copies ran while one was open for 0% -> 1% of each run, Pallas kernels for 12% -> 9%
where the time goes in v2:
time: 171 us
  blocking collectives  76.7 us (45%)
  Pallas kernels  65 us (38%)
  starting transfers between devices  10.4 us (6%)
  local copies, waits for them, and re-layouts  10.2 us (6%)
  waiting for transfers between devices  5.79 us (3%)
  other arithmetic  1.71 us (1%)
    all_to_all x2, blocking collectives, exchange(): return lax.all_to_all(parts, CHIPS, 0, 0, tiled=True)  76.7 us
    pallas_call x1, Pallas kernels, local(): call(k_middle, 4, [scalar(), scalar(), resident, resident, halo, halo, sq...  14 us
    pallas_call x1, Pallas kernels, local(): call(functools.partial(k_back, factor), 3, [scalar(), scalar(), whole(1,...  12.6 us
    pallas_call x1, Pallas kernels, local(): call(k_top, 4, [scalar(), whole(MID_ROWS, C), resident, halo, halo, taps_...  8.56 us
    unnamed x30, local copies, waits for them, and re-layouts  7.87 us
    pallas_call x1, Pallas kernels, local(): call(functools.partial(k_last, factor), STEPS, [scalar(), scalar(), whole...  7.04 us
    pallas_call x1, Pallas kernels, local(): call(functools.partial(k_sums_out, factor), 1, [whole(1, C), wide_top, re...  5.7 us
    pallas_call x1, Pallas kernels, local(): call(k_enter, STEPS, [whole(1, C), whole(2, C, B), whole(2, B, C), whole(...  4.91 us
  transfers between devices with their start and end apart: 5, of which 3 were waited for; matrix products, arithmetic and copies ran while one was open for 1% of the time, Pallas kernels for 9%

profile of v2, /device:TPU:1, one launch (start us, length us, event | category | flops | bytes accessed | tf_op | source)
XLA Modules:
  0.0 170.7 jit_solution(12413320175541548673)
XLA Ops:
  0.6 1.1 slice_bitcast_fusion.2
  1.7 0.0 copy-start.14
  1.7 0.0 copy-start
  1.7 0.0 copy-start.2
  1.7 1.3 slice_bitcast_fusion
  3.0 0.9 pad_maximum_fusion
  3.9 4.9 %collective-permute-start = (bf16[384,768]{1,0:T(8,128)(2,1)}, bf16[384,768]{1,0:T(8,128)(2,1)}, u32[]{:S(2)}, u32[]{:S(2)}) collective-permute-start(bf16[384,768]{1,0:T(8,128)(2,1)} %pad_maximum_fusion), channel_id=1, source_target_pairs={{0,1},{1,2},{2,3},{3,4},{4,5},{5,6},{6,7},{7,8},{8,9},{9,10},{10,1... | collective-permute-start | bytes 1769480 | tf_op jit(solution)/shard_map/ppermute | solution.py:339
  8.7 0.9 pad_maximum_fusion.1
  9.6 1.3 collective-permute-start.1
  10.9 0.0 copy-done.14
  10.9 0.0 copy-done
  10.9 0.0 copy-done.2
  10.9 0.0 copy-start.3
  11.0 1.3 copy-done.3
  12.2 0.0 copy-start.4
  12.2 1.3 copy-done.4
  13.5 0.0 copy-start.5
  13.5 4.9 %enter.1 = (bf16[2,768,768]{2,1,0:T(8,128)(2,1)S(1)}, bf16[2,768,768]{2,1,0:T(8,128)(2,1)S(1)}, bf16[2,768,768]{2,1,0:T(8,128)(2,1)S(1)}, bf16[2,768,768]{2,1,0:...) custom-call(s32[1,768]{1,0:T(1,128)S(1)} %reshape.29.pairs, ...), custom_call_target="tpu_custom_call" | custom-call | flops 3623878656 | bytes 28704768 | tf_op jit(solution)/shard_map/enter/pallas_call | solution.py:369
  18.4 0.0 copy-start.8
  18.4 1.4 copy-done.8
  19.8 0.0 copy-start.10
  19.8 1.2 copy-done.10
  21.0 0.0 copy-start.12
  21.0 1.1 copy-done.12
  22.2 0.0 collective-permute-done.top
  22.2 3.5 %collective-permute-done.1.bot = bf16[384,768]{1,0:T(8,128)(2,1)} collective-permute-done((bf16[384,768]{1,0:T(8,128)(2,1)}, bf16[384,768]{1,0:T(8,128)(2,1)}, u32[]{:S(2)}, u32[]{:S(2)}) %collective-permute-start.1) | collective-permute-done | bytes 589856 | tf_op jit(solution)/shard_map/ppermute | solution.py:340
  25.7 0.0 copy-done.5
  25.7 0.0 copy-start.1
  25.7 0.0 copy-start.9
  25.7 14.0 %middle.1 = (bf16[1408,768]{1,0:T(8,128)(2,1)S(1)}, bf16[1408,768]{1,0:T(8,128)(2,1)S(1)}, bf16[1408,768]{1,0:T(8,128)(2,1)S(1)}, bf16[1408,768]{1,0:T(8,128)(2,...) custom-call(s32[2]{0:T(128)S(1)} %copy-done.5, s32[1]{0:T(128)} %bitcast.block, ...), custom_call_target="tpu_custom_call" | custom-call | flops 7247757312 | bytes 30277632 | tf_op jit(solution)/shard_map/middle/pallas_call | solution.py:374
  39.6 0.0 copy-done.1
  39.7 0.0 copy-done.9
  39.7 8.6 %top.1 = (bf16[1280,768]{1,0:T(8,128)(2,1)S(1)}, bf16[1280,768]{1,0:T(8,128)(2,1)S(1)}, bf16[1280,768]{1,0:T(8,128)(2,1)S(1)}, bf16[1280,768]{1,0:T(8,128)(2,1)S(1)}) custom-call(s32[2]{0:T(128)S(1)} %copy-done.5, bf16[1408,768]{1,0:T(8,128)(2,1)S(1)} %get-tuple-element.39.mid.tc, bf16[1024,768]{1,0:T(8,128)(2,1)S(1)} %bitcast.22, ...), custom_call_target="tpu_custom_call" | custom-call | flops 3623878656 | bytes 15728640 | tf_op jit(solution)/shard_map/top/pallas_call | solution.py:380
  48.2 0.0 copy-start.6
  48.3 0.0 copy-start.11
  48.3 5.7 %sums_out.1 = (bf16[5888,128]{1,0:T(8,128)(2,1)S(1)}, bf16[1024,768]{1,0:T(8,128)(2,1)}) custom-call(s32[1,768]{1,0:T(1,128)S(1)} %reshape.29.pairs, bf16[1280,768]{1,0:T(8,128)(2,1)S(1)} %get-tuple-element.41.act, bf16[1024,768]{1,0:T(8,128)(2,1)S(1)} %bitcast.23, bf16[1280,768]{1,0:T(8,128)(2,1)S(1)} %get-tuple-element.42.tm, ...), custom_call_target="tpu_custom_call" | custom-call | flops 4831838208 | bytes 6160384 | tf_op jit(solution)/shard_map/sums_out/pallas_call | solution.py:390
  54.0 0.0 copy-done.6
  54.0 0.0 copy-done.11
  54.0 0.0 copy-start.7
  54.0 1.5 copy-done.7
  55.5 12.6 %back.1 = (bf16[1152,768]{1,0:T(8,128)(2,1)S(1)}, bf16[1152,768]{1,0:T(8,128)(2,1)S(1)}, bf16[2304,128]{1,0:T(8,128)(2,1)S(1)}) custom-call(s32[2]{0:T(128)S(1)} %copy-done.5, s32[1]{0:T(128)} %bitcast.block, s32[1,768]{1,0:T(1,128)S(1)} %reshape.29.pairs, bf16[1280,768]{1,0:T(8,128)(2,1)S(1)} %copy-done.7, bf16[2,3,384,384]{3,2,1,0:T(8,128)(2,1)S(1)} %copy-done.11, ...), custom_call_target="tpu_custom_call" | custom-call | flops 6039797760 | bytes 8257536 | tf_op jit(solution)/shard_map/back/pallas_call | solution.py:396
  68.1 0.0 copy-start.13
  68.1 4.2 %sums.1 = (bf16[5888,128]{1,0:T(8,128)(2,1)S(1)}, bf16[5888,128]{1,0:T(8,128)(2,1)S(1)}) custom-call(s32[1]{0:T(128)} %bitcast.8.core, s32[1,768]{1,0:T(1,128)S(1)} %reshape.29.pairs, bf16[1408,768]{1,0:T(8,128)(2,1)S(1)} %get-tuple-element.56.act, bf16[1152,768]{1,0:T(8,128)(2,1)S(1)} %get-tuple-element.55.cot, bf16[1408,768]{1,0:T(8,128)(2,1)S(1)} %get-tuple-element.57.tm, ...), custom_call_target="tpu_custom_call" | custom-call | flops 3623878656 | bytes 6029312 | tf_op jit(solution)/shard_map/sums/pallas_call | solution.py:404
  72.4 1.9 %collective-permute-start.2 = (bf16[5888,128]{1,0:T(8,128)(2,1)S(1)}, bf16[5888,128]{1,0:T(8,128)(2,1)S(1)}, u32[]{:S(2)}, u32[]{:S(2)}) collective-permute-start(bf16[5888,128]{1,0:T(8,128)(2,1)S(1)} %get-tuple-element.61), channel_id=1, source_target_pairs={{0,32},{32,0},{1,33},{33,1},{2,34},{34,2},{3,35},{35,3},{4,36},{36... | collective-permute-start | bytes 4521992 | tf_op jit(solution)/shard_map/ppermute | solution.py:353
  74.3 0.0 copy-done.13
  74.3 7.0 %last.1 = (bf16[2304,128]{1,0:T(8,128)(2,1)S(1)}, bf16[2304,128]{1,0:T(8,128)(2,1)S(1)}, bf16[1024,768]{1,0:T(8,128)(2,1)S(1)}) custom-call(s32[1]{0:T(128)} %bitcast.8.core, s32[2]{0:T(128)S(1)} %copy-done.5, s32[1,768]{1,0:T(1,128)S(1)} %reshape.29.pairs, bf16[1152,768]{1,0:T(8,128)(2,1)S(1)} %get-tuple-element.51.mid.d_pre, ...), custom_call_target="tpu_custom_call" | custom-call | flops 3623878656 | bytes 5505024 | tf_op jit(solution)/shard_map/last/pallas_call | solution.py:409
  81.4 0.1 collective-permute-start.3
  81.5 2.0 %collective-permute-done.3.got_b = bf16[2304,128]{1,0:T(8,128)(2,1)S(1)} collective-permute-done((bf16[2304,128]{1,0:T(8,128)(2,1)S(1)}, bf16[2304,128]{1,0:T(8,128)(2,1)S(1)}, u32[]{:S(2)}, u32[]{:S(2)}) %collective-permute-start.3) | collective-permute-done | bytes 589856 | tf_op jit(solution)/shard_map/ppermute | solution.py:353
  83.4 0.0 collective-permute-done.2.got_a
  83.4 0.5 join.1
  83.9 41.2 %all_to_all.10.parts = bf16[64,128,128]{2,1,0:T(8,128)(2,1)S(1)} all-to-all(bf16[64,128,128]{2,1,0:T(8,128)(2,1)S(1)} %bitcast.16), channel_id=1, replica_groups=mesh['xh'=2,'core'=2,'z'=4,'xl'=2,'y'=4] {'xh','z','xl','y'}, dimensions={0} | all-to-all | bytes 4194304 | tf_op jit(solution)/shard_map/all_to_all | solution.py:349
  125.1 0.5 share.1
  125.6 35.5 %all_to_all.11 = bf16[64,128,128]{2,1,0:T(8,128)(2,1)S(1)} all-to-all(bf16[64,128,128]{2,1,0:T(8,128)(2,1)S(1)} %share.1), channel_id=1, replica_groups=mesh['xh'=2,'core'=2,'z'=4,'xl'=2,'y'=4] {'xh','z','xl','y'}, dimensions={0} | all-to-all | bytes 4194304 | tf_op jit(solution)/shard_map/all_to_all | solution.py:349
  161.1 2.2 %collective-permute-start.4 = (bf16[8192,128]{1,0:T(8,128)(2,1)S(1)}, bf16[8192,128]{1,0:T(8,128)(2,1)S(1)}, u32[]{:S(2)}, u32[]{:S(2)}) collective-permute-start(bf16[8192,128]{1,0:T(8,128)(2,1)S(1)} %bitcast.17), channel_id=1, source_target_pairs={{0,32},{32,0},{1,33},{33,1},{2,34},{34,2},{3,35},{35,3},{4,36},{36... | collective-permute-start | bytes 6291464 | tf_op jit(solution)/shard_map/ppermute | solution.py:353
  163.4 3.5 %input.1 = bf16[1024,768]{1,0:T(8,128)(2,1)} custom-call(bf16[1024,768]{1,0:T(8,128)(2,1)S(1)} %get-tuple-element.54.d_inner, bf16[1024,768]{1,0:T(8,128)(2,1)S(1)} %bitcast.21, bf16[1152,768]{1,0:T(8,128)(2,1)S(1)} %get-tuple-element.55.cot, bf16[2,768,768]{2,1,0:T(8,128)(2,1)S(1)} %get-tuple-element.49.dcat_t), custom_call_target="tpu_custom_call" | custom-call | flops 1207959552 | bytes 3145728 | tf_op jit(solution)/shard_map/input/pallas_call | solution.py:421
  166.8 0.3 collective-permute-done.4.other
  167.1 3.6 %finish.1 = (f32[2,768,384]{2,1,0:T(8,128)}, f32[2,3,384,384]{3,2,1,0:T(8,128)}, f32[2,384,768]{2,1,0:T(8,128)}) custom-call(s32[1]{0:T(128)} %bitcast.8.core, bf16[8192,128]{1,0:T(8,128)(2,1)S(1)} %bitcast.18, bf16[8192,128]{1,0:T(8,128)(2,1)S(1)} %collective-permute-done.4.other), custom_call_target="tpu_custom_call" | custom-call | bytes 8257536 | tf_op jit(solution)/shard_map/finish/pallas_call | solution.py:428
  (1 shorter events, 0.0 us)
Async XLA Ops:
  1.7 9.2 %copy-start.14 = (s32[768]{0:T(1024)S(1)}, s32[768]{0:T(1024)}, u32[]{:S(2)}) copy-start(s32[768]{0:T(1024)} %param.9) | copy-start | bytes 9220
  1.7 9.2 %copy-start = (bf16[1,1024,768]{2,1,0:T(8,128)(2,1)S(1)}, bf16[1,1024,768]{2,1,0:T(8,128)(2,1)}, u32[]{:S(2)}) copy-start(bf16[1,1024,768]{2,1,0:T(8,128)(2,1)} %param.7) | copy-start | bytes 4718596
  1.7 9.2 %copy-start.2 = (bf16[2,3,384,384]{3,2,1,0:T(8,128)(2,1)S(1)}, bf16[2,3,384,384]{3,2,1,0:T(8,128)(2,1)}, u32[]{:S(2)}) copy-start(bf16[2,3,384,384]{3,2,1,0:T(8,128)(2,1)} %weight.3) | copy-start | bytes 5308420
  3.9 18.3 %collective-permute-start = (bf16[384,768]{1,0:T(8,128)(2,1)}, bf16[384,768]{1,0:T(8,128)(2,1)}, u32[]{:S(2)}, u32[]{:S(2)}) collective-permute-start(bf16[384,768]{1,0:T(8,128)(2,1)} %pad_maximum_fusion), channel_id=1, source_target_pairs={{0,1},{1,2},{2,3},{3,4},{4,5},{5,6},{6,7},{7,8},{8,9},{9,10},{10,1... | collective-permute-start | bytes 1769480 | tf_op jit(solution)/shard_map/ppermute | solution.py:339
  9.6 16.1 %collective-permute-start.1 = (bf16[384,768]{1,0:T(8,128)(2,1)}, bf16[384,768]{1,0:T(8,128)(2,1)}, u32[]{:S(2)}, u32[]{:S(2)}) collective-permute-start(bf16[384,768]{1,0:T(8,128)(2,1)} %pad_maximum_fusion.1), channel_id=1, source_target_pairs={{1,0},{2,1},{3,2},{4,3},{5,4},{6,5},{7,6},{8,7},{9,8},{10,9},{11,1... | collective-permute-start | bytes 1769480 | tf_op jit(solution)/shard_map/ppermute | solution.py:340
  10.9 1.3 copy-start.3
  12.2 1.3 copy-start.4
  13.5 12.2 %copy-start.5 = (s32[2]{0:T(128)S(1)}, s32[2]{0:T(128)}, u32[]{:S(2)}) copy-start(s32[2]{0:T(128)} %dil.7) | copy-start | bytes 28
  18.4 1.4 copy-start.8
  19.8 1.2 copy-start.10
  21.0 1.1 copy-start.12
  25.7 14.0 %copy-start.1 = (bf16[1,1024,768]{2,1,0:T(8,128)(2,1)S(1)}, bf16[1,1024,768]{2,1,0:T(8,128)(2,1)}, u32[]{:S(2)}) copy-start(bf16[1,1024,768]{2,1,0:T(8,128)(2,1)} %param.8) | copy-start | bytes 4718596
  25.7 14.0 %copy-start.9 = (bf16[2,768,768]{2,1,0:T(8,128)(2,1)S(1)}, bf16[2,768,768]{2,1,0:T(8,128)(2,1)}, u32[]{:S(2)}) copy-start(bf16[2,768,768]{2,1,0:T(8,128)(2,1)} %copy-done.8) | copy-start | bytes 7077892
  48.2 5.7 %copy-start.6 = (bf16[1280,768]{1,0:T(8,128)(2,1)}, bf16[1280,768]{1,0:T(8,128)(2,1)S(1)}, u32[]{:S(2)}) copy-start(bf16[1280,768]{1,0:T(8,128)(2,1)S(1)} %get-tuple-element.44.d_pre.mid) | copy-start | bytes 5898244
  48.3 5.7 %copy-start.11 = (bf16[2,3,384,384]{3,2,1,0:T(8,128)(2,1)S(1)}, bf16[2,3,384,384]{3,2,1,0:T(8,128)(2,1)}, u32[]{:S(2)}) copy-start(bf16[2,3,384,384]{3,2,1,0:T(8,128)(2,1)} %copy-done.10) | copy-start | bytes 5308420
  54.0 1.5 copy-start.7
  68.1 6.2 %copy-start.13 = (bf16[1024,768]{1,0:T(8,128)(2,1)S(1)}, bf16[1024,768]{1,0:T(8,128)(2,1)}, u32[]{:S(2)}) copy-start(bf16[1024,768]{1,0:T(8,128)(2,1)} %copy-done.12) | copy-start | bytes 4718596
  72.4 11.1 %collective-permute-start.2 = (bf16[5888,128]{1,0:T(8,128)(2,1)S(1)}, bf16[5888,128]{1,0:T(8,128)(2,1)S(1)}, u32[]{:S(2)}, u32[]{:S(2)}) collective-permute-start(bf16[5888,128]{1,0:T(8,128)(2,1)S(1)} %get-tuple-element.61), channel_id=1, source_target_pairs={{0,32},{32,0},{1,33},{33,1},{2,34},{34,2},{3,35},{35,3},{4,36},{36... | collective-permute-start | bytes 4521992 | tf_op jit(solution)/shard_map/ppermute | solution.py:353
  81.4 2.1 %collective-permute-start.3 = (bf16[2304,128]{1,0:T(8,128)(2,1)S(1)}, bf16[2304,128]{1,0:T(8,128)(2,1)S(1)}, u32[]{:S(2)}, u32[]{:S(2)}) collective-permute-start(bf16[2304,128]{1,0:T(8,128)(2,1)S(1)} %get-tuple-element.63), channel_id=1, source_target_pairs={{0,32},{32,0},{1,33},{33,1},{2,34},{34,2},{3,35},{35,3},{4,36},{36... | collective-permute-start | bytes 1769480 | tf_op jit(solution)/shard_map/ppermute | solution.py:353
  161.1 6.0 %collective-permute-start.4 = (bf16[8192,128]{1,0:T(8,128)(2,1)S(1)}, bf16[8192,128]{1,0:T(8,128)(2,1)S(1)}, u32[]{:S(2)}, u32[]{:S(2)}) collective-permute-start(bf16[8192,128]{1,0:T(8,128)(2,1)S(1)} %bitcast.17), channel_id=1, source_target_pairs={{0,32},{32,0},{1,33},{33,1},{2,34},{34,2},{3,35},{35,3},{4,36},{36... | collective-permute-start | bytes 6291464 | tf_op jit(solution)/shard_map/ppermute | solution.py:353

commit v3 on v2

--- a/solution.py
+++ b/solution.py
@@ -127,7 +127,7 @@
         lay(field, top[PAD : 4 * PAD, :], x[...], bot[: 3 * PAD, :])
         ends = []
         for halo in (top, bot):
-            wide = halo[: 4 * PAD, :].astype(F32)
+            wide = halo[...].astype(F32)
             ends.append(mm((wide * scale_of(wide)).astype(BF), dcat0[...]).astype(BF))
         lay(pad, ends[0], mid[...], ends[1])
 
@@ -151,7 +151,7 @@
 
     @pl.when(pl.program_id(0) == 0)
     def _():
-        lay(grad, top[4 * PAD :, :], cot[...], bot[4 * PAD :, :])
+        lay(grad, top[...], cot[...], bot[...])
 
     shift(mid, dil[1], start, tm, tp)
     m = centre(mid, start, TOP_TILE)
@@ -200,11 +200,9 @@
         keep[...] = upper[...]
 
 
-def k_sums_out(factor, pairs, act, cot, tm, tc, tp, d_pre, stream, upcat, rest, out):
-    a = own(act, 2 * PAD)
-    out[...] = (own(stream, 3 * PAD).astype(F32) + mm(a, upcat[...])).astype(BF)
+def k_sums_top(factor, pairs, act, cot, tm, tc, tp, d_pre, rest):
     taps = [own(tm, 2 * PAD), own(tc, 3 * PAD), own(tp, 2 * PAD)]
-    weight_sums(factor, pairs, a, cot[...], taps, own(d_pre, 2 * PAD), rest)
+    weight_sums(factor, pairs, own(act, 2 * PAD), cot[...], taps, own(d_pre, 2 * PAD), rest)
 
 
 def k_sums(factor, core, pairs, act, cot, tm, tc, tp, d_pre, upper, send, keep, rest):
@@ -228,16 +226,30 @@
     out[...] = jnp.broadcast_to(share[None], out.shape)
 
 
-def k_finish(core, own, other, down, kern, up):
-    layer = pl.program_id(0)
-    for mine, ref in ((True, own), (False, other)):
-
-        @pl.when((core[0] == layer) == mine)
-        def _():
-            up[0] = take(ref, 0, B, C)
-            for k in range(3):
-                kern[0, k] = take(ref, UP + k * 3 * B, B, B)
-            down[0] = take(ref, REST, C, B)
+def k_finish(layer, ref, *rest):
+    down, kern, up = rest[-3:]
+    up[0] = take(ref, 0, B, C)
+    for k in range(3):
+        kern[0, k] = take(ref, UP + k * 3 * B, B, B)
+    down[0] = take(ref, REST, C, B)
+
+
+def write_layer(layer, total, outs):
+    dims = ((C, B), (3, B, B), (B, C))
+    blocks = [pl.BlockSpec((1,) + d, lambda i, n, d=d: (n[0],) + (0,) * len(d)) for d in dims]
+    return pl.pallas_call(
+        k_finish,
+        grid_spec=pltpu.PrefetchScalarGridSpec(
+            num_scalar_prefetch=1,
+            grid=(1,),
+            in_specs=[pl.BlockSpec(total.shape, lambda i, n: (0, 0))] + [pl.BlockSpec(memory_space=pl.ANY)] * len(outs),
+            out_specs=blocks,
+        ),
+        out_shape=[shape(2, *d, kind=F32) for d in dims],
+        input_output_aliases={2 + i: i for i in range(len(outs))},
+        compiler_params=pltpu.CompilerParams(vmem_limit_bytes=20 * 1024 * 1024),
+        name="finish",
+    )(layer, total, *outs)
 
 
 def norm_back(v, d_norm):
@@ -253,7 +265,7 @@
 
     @pl.when(pl.program_id(0) == 0)
     def _():
-        lay(given, top[5 * PAD :, :], cot[...], bot[4 * PAD : 5 * PAD, :])
+        lay(given, top[PAD:, :], cot[...], bot[:PAD, :])
 
     shift(mid, dil[1], start, before, after)
     di = conv(after[...], before[...], centre(mid, start, BACK_TILE), weight[...].reshape(3 * B, B)).astype(BF)
@@ -281,6 +293,13 @@
     def _():
         down_sum(factor, pairs, normed[...], d_inner[...], down)
         sort_out(core, down, upper, send, keep)
+
+
+def k_out(act, stream, upcat, out):
+    step = pl.program_id(0) * TILE
+    rows = pl.ds(pl.multiple_of(step + 2 * PAD, 16), TILE)
+    base = pl.ds(pl.multiple_of(step + 3 * PAD, 16), TILE)
+    out[...] = (stream[base, :].astype(F32) + mm(act[rows, :], upcat[...])).astype(BF)
 
 
 def k_input(d_inner, x, cot, dcat_t, out):
@@ -333,11 +352,9 @@
     return pltpu.VMEM((rows, C), kind)
 
 
-def edges(x, cot):
-    last = jnp.concatenate([x[ROWS - 4 * PAD :], cot[ROWS - 2 * PAD :]], axis=0)
-    first = jnp.concatenate([x[: 4 * PAD], cot[: 2 * PAD]], axis=0)
-    top = lax.ppermute(last, SEQ, [(i, i + 1) for i in range(BLOCKS - 1)])
-    bot = lax.ppermute(first, SEQ, [(i + 1, i) for i in range(BLOCKS - 1)])
+def edges(cells, rows):
+    top = lax.ppermute(cells[ROWS - rows :], SEQ, [(i, i + 1) for i in range(BLOCKS - 1)])
+    bot = lax.ppermute(cells[:rows], SEQ, [(i + 1, i) for i in range(BLOCKS - 1)])
     return top, bot
 
 
@@ -362,9 +379,10 @@
     resident = whole(ROWS, C)
     taps_w = [pl.BlockSpec((None, 3, B, B), lambda i, n=n: (n, 0, 0, 0), pipeline_mode=pl.Buffered(1)) for n in range(2)]
     square_of = [pl.BlockSpec((None, C, C), lambda i, n=n: (n, 0, 0), pipeline_mode=pl.Buffered(1)) for n in range(2)]
-    halo = whole(6 * PAD, C)
-
-    top, bot = edges(x, cot)
+    halo, c_halo = whole(4 * PAD, C), whole(2 * PAD, C)
+
+    top, bot = edges(x, 4 * PAD)
+    ctop, cbot = edges(cot, 2 * PAD)
     squares = (whole(2, C, C), shape(2, C, C))
     dcat, dcat_t, upcat, upcat_t, kern_t, normed0, inner0 = call(
         k_enter, STEPS, [whole(1, C), whole(2, C, B), whole(2, B, C), whole(2, 3, B, B), tile()],
@@ -378,29 +396,29 @@
     )(dilations, block, inner0, x, top, bot, dcat, conv_weight, upcat, dcat)
     upper = (tile(TOP_TILE), shape(TOP_ROWS, C))
     act1, d_pre1, tm1, tp1 = call(
-        k_top, 4, [scalar(), whole(MID_ROWS, C), resident, halo, halo, taps_w[1], square_of[1]],
+        k_top, 4, [scalar(), whole(MID_ROWS, C), resident, c_halo, c_halo, taps_w[1], square_of[1]],
         [upper] * 4, [store(TOP_ROWS)], 3 * UNIT, "top",
-    )(dilations, inner1, cot, top, bot, conv_weight, upcat_t)
+    )(dilations, inner1, cot, ctop, cbot, conv_weight, upcat_t)
     core = lax.axis_index("core").reshape(1)
     sums = (whole(REST, LANES), shape(REST, LANES))
     downs = (whole(DOWN, LANES), shape(DOWN, LANES))
     joined = (whole(REST + DOWN, LANES), shape(REST + DOWN, LANES))
     shares = (whole(*SHARES), shape(*SHARES))
     wide_top, wide_mid, wide_back = whole(TOP_ROWS, C), whole(MID_ROWS, C), whole(BACK_ROWS, C)
-    rest1, out = call(
-        functools.partial(k_sums_out, factor), 1,
-        [whole(1, C), wide_top, resident, wide_top, wide_mid, wide_top, wide_top, wide_mid, square_of[1]],
-        [sums, (resident, shape(ROWS, C))], [], 4 * UNIT, "sums_out",
-    )(pairs, act1, cot, tm1, inner1, tp1, d_pre1, stream1, upcat)
+    (rest1,) = call(
+        functools.partial(k_sums_top, factor), 1,
+        [whole(1, C), wide_top, resident, wide_top, wide_mid, wide_top, wide_top],
+        [sums], [], 3 * UNIT, "sums_top",
+    )(pairs, act1, cot, tm1, inner1, tp1, d_pre1)
     back = (tile(BACK_TILE), shape(BACK_ROWS, C))
     grad, d_pre0, down1 = call(
         functools.partial(k_back, factor), 3,
-        [scalar(), scalar(), whole(1, C), wide_top, taps_w[1], wide_mid, wide_mid, resident, halo, halo,
+        [scalar(), scalar(), whole(1, C), wide_top, taps_w[1], wide_mid, wide_mid, resident, c_halo, c_halo,
          square_of[1], square_of[0], wide_mid],
         [back, back, downs],
         [store(BACK_TILE), store(BACK_TILE), store(BACK_ROWS), store(BACK_ROWS)],
         5 * UNIT, "back",
-    )(dilations, block, pairs, d_pre1, kern_t, normed1, stream1, cot, top, bot, dcat_t, upcat_t, slope0)
+    )(dilations, block, pairs, d_pre1, kern_t, normed1, stream1, cot, ctop, cbot, dcat_t, upcat_t, slope0)
     send_a, keep_a = call(
         functools.partial(k_sums, factor), 1,
         [scalar(), whole(1, C), wide_mid, wide_back, wide_mid, resident, wide_mid, wide_back, sums[0]],
@@ -416,19 +434,20 @@
     (parts,) = call(
         k_join, 1, [sums[0], sums[0], downs[0], downs[0]], [joined], [], 0, "join",
     )(keep_a, other_core(send_a), keep_b, other_core(send_b))
-    parts = exchange(parts.reshape(SHARES))
-    (shared,) = call(k_share, 1, [shares[0]], [shares], [], 0, "share")(parts)
+    parts, act1, d_inner0 = lax.optimization_barrier((parts, act1, d_inner0))
+    (out,) = call(
+        k_out, STEPS, [wide_top, wide_mid, square_of[1]], [FULL], [], UNIT, "out",
+    )(act1, stream1, upcat)
     (input_grad,) = call(
         k_input, STEPS, [tile(), tile(), wide_back, square_of[0]], [FULL], [], UNIT, "input",
     )(d_inner0, x, grad, dcat_t)
-    own = exchange(shared).reshape(REST + DOWN, LANES)
-    layered = lambda *dims: (
-        pl.BlockSpec((1,) + dims, lambda i: (i,) + (0,) * len(dims)), shape(2, *dims, kind=F32)
-    )
-    grads = call(
-        k_finish, 2, [scalar()] + [joined[0]] * 2,
-        [layered(C, B), layered(3, B, B), layered(B, C)], [], 0, "finish",
-    )(core, own, other_core(own))
+    parts = exchange(parts.reshape(SHARES))
+    parts, out, input_grad = lax.optimization_barrier((parts, out, input_grad))
+    (shared,) = call(k_share, 1, [shares[0]], [shares], [], 0, "share")(parts)
+    mine = exchange(shared).reshape(REST + DOWN, LANES)
+    other = other_core(mine)
+    grads = write_layer(core, mine, ())
+    grads = write_layer(1 - core, other, grads)
     return (out[None], input_grad[None], *grads)
 
 

time: 171 us -> 168 us (0.982)
  blocking collectives: 76.7 us -> 35.5 us
  starting transfers between devices: 10.4 us -> 30.3 us
  waiting for transfers between devices: 5.79 us -> 19.9 us
  local copies, waits for them, and re-layouts: 10.2 us -> 14.6 us
  other arithmetic: 1.71 us -> 0 us
    all_to_all x2 -> x1, blocking collectives: 76.7 us -> 35.5 us  [exchange(): return lax.all_to_all(parts, CHIPS, 0, 0, tiled=True)]
    all_to_all x0 -> x1, waiting for transfers between devices: none -> 16.3 us  [exchange(): return lax.all_to_all(parts, CHIPS, 0, 0, tiled=True)]
    all_to_all x0 -> x1, starting transfers between devices: none -> 15.6 us  [exchange(): return lax.all_to_all(parts, CHIPS, 0, 0, tiled=True)]
    ppermute x2 -> x4, starting transfers between devices: 6.13 us -> 10.6 us  [the longest x2 8.04 us: edges(): lax.ppermute(cells[ROWS - rows:], SEQ, [(i, i + 1) for i in range(BLOCKS...]
    unnamed x30 -> x64, local copies, waits for them, and re-layouts: 7.87 us -> 11.5 us
    ppermute x2 -> x4, waiting for transfers between devices: 3.51 us -> 0.01 us  [the longest x2 0.01 us: edges(): lax.ppermute(cells[ROWS - rows:], SEQ, [(i, i + 1) for i in range(BLOCKS...]
    pallas_call x3 -> x5, Pallas kernels: 17.8 us -> 19.4 us  [the longest x1 7.87 us: local(): call(k_top, 4, [scalar(), whole(MID_ROWS, C), resident, c_halo, c_halo, t...]
  transfers between devices with their start and end apart: 5 -> 8, of which waited for: 3 -> 3; matrix products, arithmetic and copies ran while one was open for 1% -> 1% of each run, Pallas kernels for 9% -> 20%
where the time goes in v3:
time: 168 us
  Pallas kernels  66.3 us (39%)
  blocking collectives  35.5 us (21%)
  starting transfers between devices  30.3 us (18%)
  waiting for transfers between devices  19.9 us (12%)
  local copies, waits for them, and re-layouts  14.6 us (9%)
    all_to_all x1, blocking collectives, exchange(): return lax.all_to_all(parts, CHIPS, 0, 0, tiled=True)  35.5 us
    all_to_all x1, waiting for transfers between devices, exchange(): return lax.all_to_all(parts, CHIPS, 0, 0, tiled=True)  16.3 us
    all_to_all x1, starting transfers between devices, exchange(): return lax.all_to_all(parts, CHIPS, 0, 0, tiled=True)  15.6 us
    pallas_call x1, Pallas kernels, local(): call(k_middle, 4, [scalar(), scalar(), resident, resident, halo, halo, sq...  13.2 us
    pallas_call x1, Pallas kernels, local(): call(functools.partial(k_back, factor), 3, [scalar(), scalar(), whole(1,...  11.8 us
    unnamed x64, local copies, waits for them, and re-layouts  11.5 us
    ppermute x2, starting transfers between devices, edges(): lax.ppermute(cells[ROWS - rows:], SEQ, [(i, i + 1) for i in range(BLOCKS...  8.04 us
    pallas_call x1, Pallas kernels, local(): call(k_top, 4, [scalar(), whole(MID_ROWS, C), resident, c_halo, c_halo, t...  7.87 us
  transfers between devices with their start and end apart: 8, of which 3 were waited for; matrix products, arithmetic and copies ran while one was open for 1% of the time, Pallas kernels for 20%

profile of v3, /device:TPU:1, one launch (start us, length us, event | category | flops | bytes accessed | tf_op | source)
XLA Modules:
  0.0 167.6 jit_solution(13869866364250664183)
XLA Ops:
  0.6 0.0 copy-start
  0.6 0.0 copy-start.31
  0.7 1.3 slice_bitcast_fusion
  1.9 4.1 %collective-permute-start = (bf16[256,768]{1,0:T(8,128)(2,1)S(1)}, bf16[256,768]{1,0:T(8,128)(2,1)S(1)}, u32[]{:S(2)}, u32[]{:S(2)}) collective-permute-start(bf16[256,768]{1,0:T(8,128)(2,1)S(1)} %get-tuple-element.84), channel_id=1, source_target_pairs={{0,1},{1,2},{2,3},{3,4},{4,5},{5,6},{6,7},{7,8},{8,9},{9,10},{10,1... | collective-permute-start | bytes 1179656 | tf_op jit(solution)/shard_map/ppermute | solution.py:356
  6.0 1.3 collective-permute-start.1
  7.3 1.8 %slice_bitcast_fusion.2 = (bf16[128,768]{1,0:T(8,128)(2,1)}, bf16[128,768]{1,0:T(8,128)(2,1)}) fusion(bf16[1,1024,768]{2,1,0:T(8,128)(2,1)} %param.8), kind=kLoop, calls=%fused_computation.2 | loop fusion | bytes 786432 | tf_op jit(solution)/shard_map/slice | solution.py:357
  9.1 4.0 %collective-permute-start.2 = (bf16[128,768]{1,0:T(8,128)(2,1)}, bf16[128,768]{1,0:T(8,128)(2,1)S(1)}, u32[]{:S(2)}, u32[]{:S(2)}) collective-permute-start(bf16[128,768]{1,0:T(8,128)(2,1)} %get-tuple-element.82), channel_id=1, source_target_pairs={{0,1},{1,2},{2,3},{3,4},{4,5},{5,6},{6,7},{7,8},{8,9},{9,10},{10,1... | collective-permute-start | bytes 589832 | tf_op jit(solution)/shard_map/ppermute | solution.py:356
  13.1 1.3 collective-permute-start.3
  14.5 0.0 copy-start.15
  14.5 1.5 copy-done.15
  15.9 1.3 copy-done.17
  17.2 1.3 copy-done.18
  18.5 4.9 %enter.1 = (bf16[2,768,768]{2,1,0:T(8,128)(2,1)S(1)}, bf16[2,768,768]{2,1,0:T(8,128)(2,1)S(1)}, bf16[2,768,768]{2,1,0:T(8,128)(2,1)S(1)}, bf16[2,768,768]{2,1,0:...) custom-call(s32[1,768]{1,0:T(1,128)S(1)} %reshape.30.pairs, ...), custom_call_target="tpu_custom_call" | custom-call | flops 3623878656 | bytes 28704768 | tf_op jit(solution)/shard_map/enter/pallas_call | solution.py:387
  23.4 0.0 copy-start.2
  23.4 0.0 copy-start.20
  23.5 0.0 copy-start.29
  23.5 0.0 copy-start.22
  23.5 0.0 copy-start.4
  23.5 0.0 collective-permute-done.top
  23.5 0.0 collective-permute-done.1.bot
  23.5 0.0 copy-start.14
  23.5 13.2 %middle.1 = (bf16[1408,768]{1,0:T(8,128)(2,1)S(1)}, bf16[1408,768]{1,0:T(8,128)(2,1)S(1)}, bf16[1408,768]{1,0:T(8,128)(2,1)S(1)}, bf16[1408,768]{1,0:T(8,128)(2,...) custom-call(s32[2]{0:T(128)S(1)} %copy-done.19, ...), custom_call_target="tpu_custom_call" | custom-call | flops 7247757312 | bytes 30277632 | tf_op jit(solution)/shard_map/middle/pallas_call | solution.py:392
  36.8 1.4 copy-done.24
  38.2 0.0 collective-permute-done.2.top
  38.2 0.0 collective-permute-done.3.bot
  38.2 7.9 %top.1 = (bf16[1280,768]{1,0:T(8,128)(2,1)S(1)}, bf16[1280,768]{1,0:T(8,128)(2,1)S(1)}, bf16[1280,768]{1,0:T(8,128)(2,1)S(1)}, bf16[1280,768]{1,0:T(8,128)(2,1)S(1)}) custom-call(s32[2]{0:T(128)S(1)} %copy-done.19, bf16[1408,768]{1,0:T(8,128)(2,1)S(1)} %get-tuple-element.47.mid.tc, bf16[1024,768]{1,0:T(8,128)(2,1)S(1)} %bitcast.21, ...), custom_call_target="tpu_custom_call" | custom-call | flops 3623878656 | bytes 15728640 | tf_op jit(solution)/shard_map/top/pallas_call | solution.py:398
  46.1 0.0 copy-start.23
  46.1 0.0 copy-start.25
  46.1 0.0 copy-start.27
  46.1 4.1 %sums_top.1.upper = bf16[5888,128]{1,0:T(8,128)(2,1)S(1)} custom-call(s32[1,768]{1,0:T(1,128)S(1)} %reshape.30.pairs, bf16[1280,768]{1,0:T(8,128)(2,1)S(1)} %get-tuple-element.70.act, bf16[1024,768]{1,0:T(8,128)(2,1)S(1)} %bitcast.22, bf16[1280,768]{1,0:T(8,128)(2,1)S(1)} %get-tuple-element.60.tm, bf16[1408,768]{1,0:T(8,128)(2,1)S(1)} %get-tuple-element.47.mid.tc, ...), custom_call_target="tpu_custom_call" | custom-call | flops 3623878656 | bytes 3014656 | tf_op jit(solution)/shard_map/sums_top/pallas_call | solution.py:408
  50.2 0.0 copy-done.8
  50.2 0.0 copy-done.4
  50.2 0.0 copy-done.6
  50.2 0.0 copy-done.23
  50.2 0.0 copy-done.25
  50.2 0.0 copy-done.27
  50.3 0.0 copy-start.21
  50.3 11.8 %back.1 = (bf16[1152,768]{1,0:T(8,128)(2,1)S(1)}, bf16[1152,768]{1,0:T(8,128)(2,1)S(1)}, bf16[2304,128]{1,0:T(8,128)(2,1)S(1)}) custom-call(s32[2]{0:T(128)S(1)} %copy-done.19, s32[1]{0:T(128)} %bitcast.1.block, s32[1,768]{1,0:T(1,128)S(1)} %reshape.30.pairs, bf16[1280,768]{1,0:T(8,128)(2,1)S(1)} %get-tuple-element.49.mid.d_pre, ...), custom_call_target="tpu_custom_call" | custom-call | flops 6039797760 | bytes 8257536 | tf_op jit(solution)/shard_map/back/pallas_call | solution.py:414
  62.0 0.0 copy-start.10
  62.0 0.0 copy-done.21
  62.1 0.0 copy-start.30
  62.1 4.3 %sums.1 = (bf16[5888,128]{1,0:T(8,128)(2,1)S(1)}, bf16[5888,128]{1,0:T(8,128)(2,1)S(1)}) custom-call(s32[1]{0:T(128)} %bitcast.core.layer, s32[1,768]{1,0:T(1,128)S(1)} %reshape.30.pairs, bf16[1408,768]{1,0:T(8,128)(2,1)S(1)} %get-tuple-element.46.act, bf16[1152,768]{1,0:T(8,128)(2,1)S(1)} %get-tuple-element.55.cot, ...), custom_call_target="tpu_custom_call" | custom-call | flops 3623878656 | bytes 6029312 | tf_op jit(solution)/shard_map/sums/pallas_call | solution.py:422
  66.4 1.8 %collective-permute-start.4 = (bf16[5888,128]{1,0:T(8,128)(2,1)S(1)}, bf16[5888,128]{1,0:T(8,128)(2,1)S(1)}, u32[]{:S(2)}, u32[]{:S(2)}) collective-permute-start(bf16[5888,128]{1,0:T(8,128)(2,1)S(1)} %get-tuple-element.63), channel_id=1, source_target_pairs={{0,32},{32,0},{1,33},{33,1},{2,34},{34,2},{3,35},{35,3},{4,36},{36... | collective-permute-start | bytes 4521992 | tf_op jit(solution)/shard_map/ppermute | solution.py:370
  68.1 7.0 %last.1 = (bf16[2304,128]{1,0:T(8,128)(2,1)S(1)}, bf16[2304,128]{1,0:T(8,128)(2,1)S(1)}, bf16[1024,768]{1,0:T(8,128)(2,1)S(1)}) custom-call(s32[1]{0:T(128)} %bitcast.core.layer, s32[2]{0:T(128)S(1)} %copy-done.19, s32[1,768]{1,0:T(1,128)S(1)} %reshape.30.pairs, bf16[1152,768]{1,0:T(8,128)(2,1)S(1)} %get-tuple-element.58.d_pre.mid, ...), custom_call_target="tpu_custom_call" | custom-call | flops 3623878656 | bytes 5505024 | tf_op jit(solution)/shard_map/last/pallas_call | solution.py:427
  75.2 0.0 copy-start.12
  75.2 0.1 collective-permute-start.5
  75.3 2.0 %collective-permute-done.5.got_b = bf16[2304,128]{1,0:T(8,128)(2,1)S(1)} collective-permute-done((bf16[2304,128]{1,0:T(8,128)(2,1)S(1)}, bf16[2304,128]{1,0:T(8,128)(2,1)S(1)}, u32[]{:S(2)}, u32[]{:S(2)}) %collective-permute-start.5) | collective-permute-done | bytes 589856 | tf_op jit(solution)/shard_map/ppermute | solution.py:370
  77.3 0.0 collective-permute-done.4.got_a
  77.3 1.9 %join.1 = bf16[8192,128]{1,0:T(8,128)(2,1)} custom-call(bf16[5888,128]{1,0:T(8,128)(2,1)S(1)} %get-tuple-element.62.keep_a, bf16[5888,128]{1,0:T(8,128)(2,1)S(1)} %collective-permute-done.4.got_a, bf16[2304,128]{1,0:T(8,128)(2,1)S(1)} %get-tuple-element.66.keep_b, bf16[2304,128]{1,0:T(8,128)(2,1)S(1)} %collective-permute-done.5.got_b), custom_call_target="tpu_custom_call" | custom-call | bytes 4194304 | tf_op jit(solution)/shard_map/join/pallas_call | solution.py:434
  79.1 15.6 %all-to-all-start = ((bf16[64,128,128]{2,1,0:T(8,128)(2,1)}), bf16[64,128,128]{2,1,0:T(8,128)(2,1)S(1)}, u32[]{:S(2)}, u32[]{:S(2)}) async-start(bf16[64,128,128]{2,1,0:T(8,128)(2,1)} %bitcast.8), calls=%async_computation | async-start | bytes 4194304 | tf_op jit(solution)/shard_map/all_to_all | solution.py:366
  94.7 0.0 copy-start.1
  94.7 1.4 copy-done.1
  96.1 1.7 copy-done.5
  97.8 1.5 copy-done.11
  99.3 1.4 copy-done.13
  100.7 3.4 %input.1 = bf16[1024,768]{1,0:T(8,128)(2,1)} custom-call(bf16[1024,768]{1,0:T(8,128)(2,1)S(1)} %copy-done.13, bf16[1024,768]{1,0:T(8,128)(2,1)S(1)} %bitcast.20, bf16[1152,768]{1,0:T(8,128)(2,1)S(1)} %copy-done.11, bf16[2,768,768]{2,1,0:T(8,128)(2,1)S(1)} %copy-done.5), custom_call_target="tpu_custom_call" | custom-call | flops 1207959552 | bytes 3145728 | tf_op jit(solution)/shard_map/input/pallas_call | solution.py:441
  104.1 3.0 %out.1 = bf16[1024,768]{1,0:T(8,128)(2,1)} custom-call(bf16[1280,768]{1,0:T(8,128)(2,1)S(1)} %copy-done.9, bf16[1408,768]{1,0:T(8,128)(2,1)S(1)} %copy-done.7, bf16[2,768,768]{2,1,0:T(8,128)(2,1)S(1)} %copy-done.3), custom_call_target="tpu_custom_call" | custom-call | flops 1207959552 | bytes 3145728 | tf_op jit(solution)/shard_map/out/pallas_call | solution.py:438
  107.0 16.3 %all-to-all-done.parts = bf16[64,128,128]{2,1,0:T(8,128)(2,1)S(1)} async-done(((bf16[64,128,128]{2,1,0:T(8,128)(2,1)}), bf16[64,128,128]{2,1,0:T(8,128)(2,1)S(1)}, u32[]{:S(2)}, u32[]{:S(2)}) %all-to-all-start) | async-done | bytes 2097184 | tf_op jit(solution)/shard_map/all_to_all | solution.py:366
  123.4 0.5 share.1
  123.8 35.5 %all_to_all.10 = bf16[64,128,128]{2,1,0:T(8,128)(2,1)S(1)} all-to-all(bf16[64,128,128]{2,1,0:T(8,128)(2,1)S(1)} %share.1), channel_id=1, replica_groups=mesh['xh'=2,'core'=2,'z'=4,'xl'=2,'y'=4] {'xh','z','xl','y'}, dimensions={0} | all-to-all | bytes 4194304 | tf_op jit(solution)/shard_map/all_to_all | solution.py:366
  159.3 2.2 %collective-permute-start.6 = (bf16[8192,128]{1,0:T(8,128)(2,1)S(1)}, bf16[8192,128]{1,0:T(8,128)(2,1)S(1)}, u32[]{:S(2)}, u32[]{:S(2)}) collective-permute-start(bf16[8192,128]{1,0:T(8,128)(2,1)S(1)} %bitcast.16), channel_id=1, source_target_pairs={{0,32},{32,0},{1,33},{33,1},{2,34},{34,2},{3,35},{35,3},{4,36},{36... | collective-permute-start | bytes 6291464 | tf_op jit(solution)/shard_map/ppermute | solution.py:370
  161.6 2.3 %finish.2 = (f32[2,768,384]{2,1,0:T(8,128)}, f32[2,3,384,384]{3,2,1,0:T(8,128)}, f32[2,384,768]{2,1,0:T(8,128)}) custom-call(s32[1]{0:T(128)} %bitcast.core.layer, bf16[8192,128]{1,0:T(8,128)(2,1)S(1)} %bitcast.17), custom_call_target="tpu_custom_call" | custom-call | tf_op jit(solution)/shard_map/finish/pallas_call | solution.py:240
  163.8 1.5 collective-permute-done.6.ref
  165.4 2.3 %finish.3 = (f32[2,768,384]{2,1,0:T(8,128)}, f32[2,3,384,384]{3,2,1,0:T(8,128)}, f32[2,384,768]{2,1,0:T(8,128)}) custom-call(s32[1]{0:T(128)S(6)} %sub.3.layer, bf16[8192,128]{1,0:T(8,128)(2,1)S(1)} %collective-permute-done.6.ref, f32[2,768,384]{2,1,0:T(8,128)} %get-tuple-element.75.rest_0_, ...), custom_call_target="tpu_custom_call", output_to_operand_aliasing={{0}: (2, {}), {1}: (3, {}), {2}: (4, {})} | custom-call | tf_op jit(solution)/shard_map/finish/pallas_call | solution.py:240
  (33 shorter events, 0.1 us)
Async XLA Ops:
  0.6 13.8 %copy-start = (bf16[1,1024,768]{2,1,0:T(8,128)(2,1)S(1)}, bf16[1,1024,768]{2,1,0:T(8,128)(2,1)}, u32[]{:S(2)}) copy-start(bf16[1,1024,768]{2,1,0:T(8,128)(2,1)} %param.7) | copy-start | bytes 4718596
  0.6 13.8 %copy-start.31 = (s32[768]{0:T(1024)S(1)}, s32[768]{0:T(1024)}, u32[]{:S(2)}) copy-start(s32[768]{0:T(1024)} %param.9) | copy-start | bytes 9220
  1.9 21.6 %collective-permute-start = (bf16[256,768]{1,0:T(8,128)(2,1)S(1)}, bf16[256,768]{1,0:T(8,128)(2,1)S(1)}, u32[]{:S(2)}, u32[]{:S(2)}) collective-permute-start(bf16[256,768]{1,0:T(8,128)(2,1)S(1)} %get-tuple-element.84), channel_id=1, source_target_pairs={{0,1},{1,2},{2,3},{3,4},{4,5},{5,6},{6,7},{7,8},{8,9},{9,10},{10,1... | collective-permute-start | bytes 1179656 | tf_op jit(solution)/shard_map/ppermute | solution.py:356
  6.0 17.5 %collective-permute-start.1 = (bf16[256,768]{1,0:T(8,128)(2,1)S(1)}, bf16[256,768]{1,0:T(8,128)(2,1)S(1)}, u32[]{:S(2)}, u32[]{:S(2)}) collective-permute-start(bf16[256,768]{1,0:T(8,128)(2,1)S(1)} %get-tuple-element.83), channel_id=1, source_target_pairs={{1,0},{2,1},{3,2},{4,3},{5,4},{6,5},{7,6},{8,7},{9,8},{10,9},{11,1... | collective-permute-start | bytes 1179656 | tf_op jit(solution)/shard_map/ppermute | solution.py:357
  9.1 29.1 %collective-permute-start.2 = (bf16[128,768]{1,0:T(8,128)(2,1)}, bf16[128,768]{1,0:T(8,128)(2,1)S(1)}, u32[]{:S(2)}, u32[]{:S(2)}) collective-permute-start(bf16[128,768]{1,0:T(8,128)(2,1)} %get-tuple-element.82), channel_id=1, source_target_pairs={{0,1},{1,2},{2,3},{3,4},{4,5},{5,6},{6,7},{7,8},{8,9},{9,10},{10,1... | collective-permute-start | bytes 589832 | tf_op jit(solution)/shard_map/ppermute | solution.py:356
  13.1 25.1 %collective-permute-start.3 = (bf16[128,768]{1,0:T(8,128)(2,1)}, bf16[128,768]{1,0:T(8,128)(2,1)S(1)}, u32[]{:S(2)}, u32[]{:S(2)}) collective-permute-start(bf16[128,768]{1,0:T(8,128)(2,1)} %get-tuple-element.81), channel_id=1, source_target_pairs={{1,0},{2,1},{3,2},{4,3},{5,4},{6,5},{7,6},{8,7},{9,8},{10,9},{11,1... | collective-permute-start | bytes 589832 | tf_op jit(solution)/shard_map/ppermute | solution.py:357
  14.5 1.5 copy-start.15
  15.9 1.3 copy-start.17
  17.2 1.3 copy-start.18
  18.5 5.0 %copy-start.16 = (bf16[2,3,384,384]{3,2,1,0:T(8,128)(2,1)S(1)}, bf16[2,3,384,384]{3,2,1,0:T(8,128)(2,1)}, u32[]{:S(2)}) copy-start(bf16[2,3,384,384]{3,2,1,0:T(8,128)(2,1)} %weight.3) | copy-start | bytes 5308420
  18.5 5.0 %copy-start.19 = (s32[2]{0:T(128)S(1)}, s32[2]{0:T(128)}, u32[]{:S(2)}) copy-start(s32[2]{0:T(128)} %dil.7) | copy-start | bytes 28
  23.4 13.3 %copy-start.2 = (bf16[2,768,768]{2,1,0:T(8,128)(2,1)}, bf16[2,768,768]{2,1,0:T(8,128)(2,1)S(1)}, u32[]{:S(2)}) copy-start(bf16[2,768,768]{2,1,0:T(8,128)(2,1)S(1)} %get-tuple-element.45.upcat) | copy-start | bytes 7077892
  23.4 13.3 %copy-start.20 = (bf16[1024,768]{1,0:T(8,128)(2,1)}, bf16[1024,768]{1,0:T(8,128)(2,1)S(1)}, u32[]{:S(2)}) copy-start(bf16[1024,768]{1,0:T(8,128)(2,1)S(1)} %get-tuple-element.43.mid.tc) | copy-start | bytes 4718596
  23.4 13.3 %copy-start.26 = (bf16[2,3,384,384]{3,2,1,0:T(8,128)(2,1)}, bf16[2,3,384,384]{3,2,1,0:T(8,128)(2,1)S(1)}, u32[]{:S(2)}) copy-start(bf16[2,3,384,384]{3,2,1,0:T(8,128)(2,1)S(1)} %get-tuple-element.50.weight) | copy-start | bytes 5308420
  23.5 13.3 %copy-start.29 = (bf16[1024,768]{1,0:T(8,128)(2,1)}, bf16[1024,768]{1,0:T(8,128)(2,1)S(1)}, u32[]{:S(2)}) copy-start(bf16[1024,768]{1,0:T(8,128)(2,1)S(1)} %get-tuple-element.64.normed) | copy-start | bytes 4718596
  23.5 14.7 %copy-start.22 = (bf16[2,768,768]{2,1,0:T(8,128)(2,1)}, bf16[2,768,768]{2,1,0:T(8,128)(2,1)S(1)}, u32[]{:S(2)}) copy-start(bf16[2,768,768]{2,1,0:T(8,128)(2,1)S(1)} %get-tuple-element.48.upcat_t) | copy-start | bytes 7077892
  23.5 26.7 %copy-start.4 = (bf16[2,768,768]{2,1,0:T(8,128)(2,1)}, bf16[2,768,768]{2,1,0:T(8,128)(2,1)S(1)}, u32[]{:S(2)}) copy-start(bf16[2,768,768]{2,1,0:T(8,128)(2,1)S(1)} %get-tuple-element.53.dcat_t) | copy-start | bytes 7077892
  23.5 14.7 %copy-start.14 = (bf16[1,1024,768]{2,1,0:T(8,128)(2,1)S(1)}, bf16[1,1024,768]{2,1,0:T(8,128)(2,1)}, u32[]{:S(2)}) copy-start(bf16[1,1024,768]{2,1,0:T(8,128)(2,1)} %param.8) | copy-start | bytes 4718596
  36.8 1.4 copy-start.24
  38.2 12.0 %copy-start.6 = (bf16[1408,768]{1,0:T(8,128)(2,1)}, bf16[1408,768]{1,0:T(8,128)(2,1)S(1)}, u32[]{:S(2)}) copy-start(bf16[1408,768]{1,0:T(8,128)(2,1)S(1)} %get-tuple-element.52.stream) | copy-start | bytes 6488068
  46.1 4.1 %copy-start.8 = (bf16[1280,768]{1,0:T(8,128)(2,1)}, bf16[1280,768]{1,0:T(8,128)(2,1)S(1)}, u32[]{:S(2)}) copy-start(bf16[1280,768]{1,0:T(8,128)(2,1)S(1)} %get-tuple-element.70.act) | copy-start | bytes 5898244
  46.1 4.1 %copy-start.23 = (bf16[2,768,768]{2,1,0:T(8,128)(2,1)S(1)}, bf16[2,768,768]{2,1,0:T(8,128)(2,1)}, u32[]{:S(2)}) copy-start(bf16[2,768,768]{2,1,0:T(8,128)(2,1)} %copy-done.22) | copy-start | bytes 7077892
  46.1 4.1 %copy-start.25 = (bf16[1408,768]{1,0:T(8,128)(2,1)S(1)}, bf16[1408,768]{1,0:T(8,128)(2,1)}, u32[]{:S(2)}) copy-start(bf16[1408,768]{1,0:T(8,128)(2,1)} %copy-done.24) | copy-start | bytes 6488068
  46.1 4.1 %copy-start.27 = (bf16[2,3,384,384]{3,2,1,0:T(8,128)(2,1)S(1)}, bf16[2,3,384,384]{3,2,1,0:T(8,128)(2,1)}, u32[]{:S(2)}) copy-start(bf16[2,3,384,384]{3,2,1,0:T(8,128)(2,1)} %copy-done.26) | copy-start | bytes 5308420
  50.3 11.8 %copy-start.21 = (bf16[1024,768]{1,0:T(8,128)(2,1)S(1)}, bf16[1024,768]{1,0:T(8,128)(2,1)}, u32[]{:S(2)}) copy-start(bf16[1024,768]{1,0:T(8,128)(2,1)} %copy-done.20) | copy-start | bytes 4718596
  62.0 4.3 %copy-start.10 = (bf16[1152,768]{1,0:T(8,128)(2,1)}, bf16[1152,768]{1,0:T(8,128)(2,1)S(1)}, u32[]{:S(2)}) copy-start(bf16[1152,768]{1,0:T(8,128)(2,1)S(1)} %get-tuple-element.55.cot) | copy-start | bytes 5308420
  62.1 6.1 %copy-start.28 = (bf16[2,3,384,384]{3,2,1,0:T(8,128)(2,1)S(1)}, bf16[2,3,384,384]{3,2,1,0:T(8,128)(2,1)}, u32[]{:S(2)}) copy-start(bf16[2,3,384,384]{3,2,1,0:T(8,128)(2,1)} %copy-done.26) | copy-start | bytes 5308420
  62.1 6.1 %copy-start.30 = (bf16[1024,768]{1,0:T(8,128)(2,1)S(1)}, bf16[1024,768]{1,0:T(8,128)(2,1)}, u32[]{:S(2)}) copy-start(bf16[1024,768]{1,0:T(8,128)(2,1)} %copy-done.29) | copy-start | bytes 4718596
  66.4 10.9 %collective-permute-start.4 = (bf16[5888,128]{1,0:T(8,128)(2,1)S(1)}, bf16[5888,128]{1,0:T(8,128)(2,1)S(1)}, u32[]{:S(2)}, u32[]{:S(2)}) collective-permute-start(bf16[5888,128]{1,0:T(8,128)(2,1)S(1)} %get-tuple-element.63), channel_id=1, source_target_pairs={{0,32},{32,0},{1,33},{33,1},{2,34},{34,2},{3,35},{35,3},{4,36},{36... | collective-permute-start | bytes 4521992 | tf_op jit(solution)/shard_map/ppermute | solution.py:370
  75.2 4.0 %copy-start.12 = (bf16[1024,768]{1,0:T(8,128)(2,1)}, bf16[1024,768]{1,0:T(8,128)(2,1)S(1)}, u32[]{:S(2)}) copy-start(bf16[1024,768]{1,0:T(8,128)(2,1)S(1)} %get-tuple-element.71.d_inner) | copy-start | bytes 4718596
  75.2 2.1 %collective-permute-start.5 = (bf16[2304,128]{1,0:T(8,128)(2,1)S(1)}, bf16[2304,128]{1,0:T(8,128)(2,1)S(1)}, u32[]{:S(2)}, u32[]{:S(2)}) collective-permute-start(bf16[2304,128]{1,0:T(8,128)(2,1)S(1)} %get-tuple-element.67), channel_id=1, source_target_pairs={{0,32},{32,0},{1,33},{33,1},{2,34},{34,2},{3,35},{35,3},{4,36},{36... | collective-permute-start | bytes 1769480 | tf_op jit(solution)/shard_map/ppermute | solution.py:370
  79.1 44.2 %all-to-all-start = ((bf16[64,128,128]{2,1,0:T(8,128)(2,1)}), bf16[64,128,128]{2,1,0:T(8,128)(2,1)S(1)}, u32[]{:S(2)}, u32[]{:S(2)}) async-start(bf16[64,128,128]{2,1,0:T(8,128)(2,1)} %bitcast.8), calls=%async_computation | async-start | bytes 4194304 | tf_op jit(solution)/shard_map/all_to_all | solution.py:366
  94.7 1.4 copy-start.1
  96.1 1.7 copy-start.5
  97.8 1.5 copy-start.11
  99.3 1.4 copy-start.13
  100.7 3.4 %copy-start.3 = (bf16[2,768,768]{2,1,0:T(8,128)(2,1)S(1)}, bf16[2,768,768]{2,1,0:T(8,128)(2,1)}, u32[]{:S(2)}) copy-start(bf16[2,768,768]{2,1,0:T(8,128)(2,1)} %copy-done.2) | copy-start | bytes 7077892
  100.7 3.4 %copy-start.7 = (bf16[1408,768]{1,0:T(8,128)(2,1)S(1)}, bf16[1408,768]{1,0:T(8,128)(2,1)}, u32[]{:S(2)}) copy-start(bf16[1408,768]{1,0:T(8,128)(2,1)} %copy-done.6) | copy-start | bytes 6488068
  100.7 3.4 %copy-start.9 = (bf16[1280,768]{1,0:T(8,128)(2,1)S(1)}, bf16[1280,768]{1,0:T(8,128)(2,1)}, u32[]{:S(2)}) copy-start(bf16[1280,768]{1,0:T(8,128)(2,1)} %copy-done.8) | copy-start | bytes 5898244
  159.3 6.0 %collective-permute-start.6 = (bf16[8192,128]{1,0:T(8,128)(2,1)S(1)}, bf16[8192,128]{1,0:T(8,128)(2,1)S(1)}, u32[]{:S(2)}, u32[]{:S(2)}) collective-permute-start(bf16[8192,128]{1,0:T(8,128)(2,1)S(1)} %bitcast.16), channel_id=1, source_target_pairs={{0,32},{32,0},{1,33},{33,1},{2,34},{34,2},{3,35},{35,3},{4,36},{36... | collective-permute-start | bytes 6291464 | tf_op jit(solution)/shard_map/ppermute | solution.py:370

commit v4 on v3

--- a/solution.py
+++ b/solution.py
@@ -30,6 +30,10 @@
     return lax.dot_general(left, right, (((1,), (0,)), ((), ())), preferred_element_type=F32)
 
 
+def mm_nt(left, right):
+    return lax.dot_general(left, right, (((1,), (1,)), ((), ())), preferred_element_type=F32)
+
+
 def mm_tn(left, right):
     return lax.dot_general(left, right, (((0,), (0,)), ((), ())), preferred_element_type=F32)
 
@@ -73,12 +77,17 @@
     return cells[pl.ds(pl.multiple_of(start + PAD, 16), rows), :]
 
 
-def conv(first, last, mid, weight):
+def conv(first, last, mid, weight, product=mm):
     rows = mid.shape[0]
     rows_a = jnp.concatenate([first[:, :B], mid[:, :B], last[:, :B]], axis=1)
     rows_b = jnp.concatenate([last[:, B:], mid[:, B:], first[:, B:]], axis=1)
-    both = mm(jnp.concatenate([rows_a, rows_b], axis=0), weight)
+    both = product(jnp.concatenate([rows_a, rows_b], axis=0), weight)
     return jnp.concatenate([both[:rows], both[rows:]], axis=1)
+
+
+def conv_back(first, last, mid, weight):
+    beside = jnp.concatenate([weight[k] for k in range(3)], axis=1)
+    return conv(first, last, mid, beside, mm_nt)
 
 
 def inside(block, start, values):
@@ -94,23 +103,15 @@
     return act, half + (act * (1.0 - t)) * (ROOT + (3.0 * CUBE * ROOT) * sq)
 
 
-def k_enter(pairs, down, up, kern, x, dcat, dcat_t, upcat, upcat_t, kern_t, normed, inner):
+def k_enter(pairs, down, up, x, dcat, upcat, normed, inner):
     @pl.when(pl.program_id(0) == 0)
     def _():
         s = swap(pairs)
         for layer in range(2):
-            other = mm(s, down[layer])
             dcat[layer, :, :B] = down[layer]
-            dcat[layer, :, B:] = other.astype(BF)
-            dcat_t[layer, :B, :] = down[layer].astype(F32).T.astype(BF)
-            dcat_t[layer, B:, :] = other.T.astype(BF)
-            other = mm(up[layer], s)
+            dcat[layer, :, B:] = mm(s, down[layer]).astype(BF)
             upcat[layer, :B, :] = up[layer]
-            upcat[layer, B:, :] = other.astype(BF)
-            upcat_t[layer, :, :B] = up[layer].astype(F32).T.astype(BF)
-            upcat_t[layer, :, B:] = other.T.astype(BF)
-            for k in range(3):
-                kern_t[layer, k] = kern[layer, k].astype(F32).T.astype(BF)
+            upcat[layer, B:, :] = mm(up[layer], s).astype(BF)
 
     wide = x[...].astype(F32)
     n = (wide * scale_of(wide)).astype(BF)
@@ -146,7 +147,7 @@
     inner[...] = inside(block[0], start - 3 * PAD, mm(n, dcat[...])).astype(BF)
 
 
-def k_top(dil, mid, cot, top, bot, weight, upcat_t, act, d_pre, tm, tp, grad):
+def k_top(dil, mid, cot, top, bot, weight, upcat, act, d_pre, tm, tp, grad):
     start = pl.program_id(0) * TOP_TILE
 
     @pl.when(pl.program_id(0) == 0)
@@ -156,7 +157,7 @@
     shift(mid, dil[1], start, tm, tp)
     m = centre(mid, start, TOP_TILE)
     rows = pl.ds(pl.multiple_of(start, 16), TOP_TILE)
-    d_act = mm(grad[rows, :], upcat_t[...])
+    d_act = mm_nt(grad[rows, :], upcat[...])
     g, s = gelu_both(conv(tm[...], tp[...], m, weight[...].reshape(3 * B, B)))
     act[...] = g.astype(BF)
     d_pre[...] = (d_act * s).astype(BF)
@@ -259,7 +260,7 @@
     return scale * d_norm - wide * (scale * scale * scale * mixed)
 
 
-def k_back(factor, dil, block, pairs, mid, weight, normed, stream, cot, top, bot, dcat_t, upcat_t, slope,
+def k_back(factor, dil, block, pairs, mid, weight, normed, stream, cot, top, bot, dcat, upcat, slope,
            grad, d_pre, down, before, after, d_inner, given):
     start = pl.program_id(0) * BACK_TILE
 
@@ -268,14 +269,14 @@
         lay(given, top[PAD:, :], cot[...], bot[:PAD, :])
 
     shift(mid, dil[1], start, before, after)
-    di = conv(after[...], before[...], centre(mid, start, BACK_TILE), weight[...].reshape(3 * B, B)).astype(BF)
+    di = conv_back(after[...], before[...], centre(mid, start, BACK_TILE), weight).astype(BF)
     rows = pl.ds(pl.multiple_of(start, 16), BACK_TILE)
     saved = pl.ds(pl.multiple_of(start + 2 * PAD, 16), BACK_TILE)
     d_inner[rows, :] = di
-    g = given[rows, :].astype(F32) + norm_back(stream[saved, :], mm(di, dcat_t[...]))
+    g = given[rows, :].astype(F32) + norm_back(stream[saved, :], mm_nt(di, dcat[...]))
     g = inside(block[0], start - PAD, g).astype(BF)
     grad[...] = g
-    d_pre[...] = (mm(g, upcat_t[...]) * slope[saved, :].astype(F32)).astype(BF)
+    d_pre[...] = (mm_nt(g, upcat[...]) * slope[saved, :].astype(F32)).astype(BF)
 
     @pl.when(pl.program_id(0) == pl.num_programs(0) - 1)
     def _():
@@ -286,7 +287,7 @@
     start = pl.program_id(0) * TILE
 
     shift(mid, dil[0], start, before, after)
-    di = conv(after[...], before[...], centre(mid, start, TILE), weight[...].reshape(3 * B, B)).astype(BF)
+    di = conv_back(after[...], before[...], centre(mid, start, TILE), weight).astype(BF)
     d_inner[pl.ds(pl.multiple_of(start, 16), TILE), :] = di
 
     @pl.when(pl.program_id(0) == pl.num_programs(0) - 1)
@@ -302,9 +303,9 @@
     out[...] = (stream[base, :].astype(F32) + mm(act[rows, :], upcat[...])).astype(BF)
 
 
-def k_input(d_inner, x, cot, dcat_t, out):
+def k_input(d_inner, x, cot, dcat, out):
     rows = pl.ds(pl.multiple_of(pl.program_id(0) * TILE + PAD, 16), TILE)
-    out[...] = (cot[rows, :].astype(F32) + norm_back(x[...], mm(d_inner[...], dcat_t[...]))).astype(BF)
+    out[...] = (cot[rows, :].astype(F32) + norm_back(x[...], mm_nt(d_inner[...], dcat[...]))).astype(BF)
 
 
 def tile(rows=TILE):
@@ -323,7 +324,7 @@
     return jax.ShapeDtypeStruct(dims, kind)
 
 
-def call(body, steps, ins, outs, scratch, flops, name):
+def call(body, steps, ins, outs, scratch, flops, name, limit=20):
     size = lambda s: 2 * math.prod(s.shape)
     return pl.pallas_call(
         body,
@@ -332,7 +333,7 @@
         out_specs=[spec for spec, _ in outs],
         out_shape=[form for _, form in outs],
         scratch_shapes=scratch,
-        compiler_params=pltpu.CompilerParams(vmem_limit_bytes=20 * 1024 * 1024),
+        compiler_params=pltpu.CompilerParams(vmem_limit_bytes=limit * 1024 * 1024),
         cost_estimate=pl.CostEstimate(
             flops=int(flops), bytes_accessed=2 * sum(size(f) for _, f in outs), transcendentals=0
         ),
@@ -384,10 +385,10 @@
     top, bot = edges(x, 4 * PAD)
     ctop, cbot = edges(cot, 2 * PAD)
     squares = (whole(2, C, C), shape(2, C, C))
-    dcat, dcat_t, upcat, upcat_t, kern_t, normed0, inner0 = call(
-        k_enter, STEPS, [whole(1, C), whole(2, C, B), whole(2, B, C), whole(2, 3, B, B), tile()],
-        [squares] * 4 + [(whole(2, 3, B, B), shape(2, 3, B, B)), FULL, FULL], [], 3 * UNIT, "enter",
-    )(pairs, down_weight, up_weight, conv_weight, x)
+    dcat, upcat, normed0, inner0 = call(
+        k_enter, STEPS, [whole(1, C), whole(2, C, B), whole(2, B, C), tile()],
+        [squares] * 2 + [FULL, FULL], [], 3 * UNIT, "enter",
+    )(pairs, down_weight, up_weight, x)
     mid = (tile(MID_TILE), shape(MID_ROWS, C))
     act0, slope0, tm0, tp0, stream1, normed1, inner1 = call(
         k_middle, 4,
@@ -398,7 +399,7 @@
     act1, d_pre1, tm1, tp1 = call(
         k_top, 4, [scalar(), whole(MID_ROWS, C), resident, c_halo, c_halo, taps_w[1], square_of[1]],
         [upper] * 4, [store(TOP_ROWS)], 3 * UNIT, "top",
-    )(dilations, inner1, cot, ctop, cbot, conv_weight, upcat_t)
+    )(dilations, inner1, cot, ctop, cbot, conv_weight, upcat)
     core = lax.axis_index("core").reshape(1)
     sums = (whole(REST, LANES), shape(REST, LANES))
     downs = (whole(DOWN, LANES), shape(DOWN, LANES))
@@ -418,7 +419,7 @@
         [back, back, downs],
         [store(BACK_TILE), store(BACK_TILE), store(BACK_ROWS), store(BACK_ROWS)],
         5 * UNIT, "back",
-    )(dilations, block, pairs, d_pre1, kern_t, normed1, stream1, cot, ctop, cbot, dcat_t, upcat_t, slope0)
+    )(dilations, block, pairs, d_pre1, conv_weight, normed1, stream1, cot, ctop, cbot, dcat, upcat, slope0)
     send_a, keep_a = call(
         functools.partial(k_sums, factor), 1,
         [scalar(), whole(1, C), wide_mid, wide_back, wide_mid, resident, wide_mid, wide_back, sums[0]],
@@ -430,7 +431,7 @@
         [downs, downs, (resident, shape(ROWS, C))],
         [store(TILE), store(TILE), pltpu.VMEM((DOWN, LANES), BF)],
         3 * UNIT, "last",
-    )(core, dilations, pairs, d_pre0, kern_t, normed0, down1)
+    )(core, dilations, pairs, d_pre0, conv_weight, normed0, down1)
     (parts,) = call(
         k_join, 1, [sums[0], sums[0], downs[0], downs[0]], [joined], [], 0, "join",
     )(keep_a, other_core(send_a), keep_b, other_core(send_b))
@@ -440,7 +441,7 @@
     )(act1, stream1, upcat)
     (input_grad,) = call(
         k_input, STEPS, [tile(), tile(), wide_back, square_of[0]], [FULL], [], UNIT, "input",
-    )(d_inner0, x, grad, dcat_t)
+    )(d_inner0, x, grad, dcat)
     parts = exchange(parts.reshape(SHARES))
     parts, out, input_grad = lax.optimization_barrier((parts, out, input_grad))
     (shared,) = call(k_share, 1, [shares[0]], [shares], [], 0, "share")(parts)

time: 168 us -> 165 us (0.982)
  local copies, waits for them, and re-layouts: 14.6 us -> 11.6 us
    unnamed x64 -> x40, local copies, waits for them, and re-layouts: 11.5 us -> 8.56 us
  transfers between devices with their start and end apart: 8 -> 8, of which waited for: 3 -> 3; matrix products, arithmetic and copies ran while one was open for 1% -> 1% of each run, Pallas kernels for 20% -> 21%
where the time goes in v4:
time: 165 us
  Pallas kernels  66.6 us (40%)
  blocking collectives  35.5 us (22%)
  starting transfers between devices  30.4 us (18%)
  waiting for transfers between devices  19.7 us (12%)
  local copies, waits for them, and re-layouts  11.6 us (7%)
    all_to_all x1, blocking collectives, exchange(): return lax.all_to_all(parts, CHIPS, 0, 0, tiled=True)  35.5 us
    all_to_all x1, waiting for transfers between devices, exchange(): return lax.all_to_all(parts, CHIPS, 0, 0, tiled=True)  16.1 us
    all_to_all x1, starting transfers between devices, exchange(): return lax.all_to_all(parts, CHIPS, 0, 0, tiled=True)  15.6 us
    pallas_call x1, Pallas kernels, local(): call(k_middle, 4, [scalar(), scalar(), resident, resident, halo, halo, sq...  13.3 us
    pallas_call x1, Pallas kernels, local(): call(functools.partial(k_back, factor), 3, [scalar(), scalar(), whole(1,...  12 us
    unnamed x40, local copies, waits for them, and re-layouts  8.56 us
    ppermute x2, starting transfers between devices, edges(): lax.ppermute(cells[ROWS - rows:], SEQ, [(i, i + 1) for i in range(BLOCKS...  8.04 us
    pallas_call x1, Pallas kernels, local(): call(k_top, 4, [scalar(), whole(MID_ROWS, C), resident, c_halo, c_halo, t...  7.78 us
  transfers between devices with their start and end apart: 8, of which 3 were waited for; matrix products, arithmetic and copies ran while one was open for 1% of the time, Pallas kernels for 21%

profile of v4, /device:TPU:1, one launch (start us, length us, event | category | flops | bytes accessed | tf_op | source)
XLA Modules:
  0.0 164.7 jit_solution(16299323694071213762)
XLA Ops:
  0.6 0.0 copy-start
  0.6 0.0 copy-start.19
  0.7 1.3 slice_bitcast_fusion
  1.9 4.1 %collective-permute-start = (bf16[256,768]{1,0:T(8,128)(2,1)S(1)}, bf16[256,768]{1,0:T(8,128)(2,1)S(1)}, u32[]{:S(2)}, u32[]{:S(2)}) collective-permute-start(bf16[256,768]{1,0:T(8,128)(2,1)S(1)} %get-tuple-element.78), channel_id=1, source_target_pairs={{0,1},{1,2},{2,3},{3,4},{4,5},{5,6},{6,7},{7,8},{8,9},{9,10},{10,1... | collective-permute-start | bytes 1179656 | tf_op jit(solution)/shard_map/ppermute | solution.py:357
  6.0 1.3 collective-permute-start.1
  7.3 1.8 %slice_bitcast_fusion.2 = (bf16[128,768]{1,0:T(8,128)(2,1)}, bf16[128,768]{1,0:T(8,128)(2,1)}) fusion(bf16[1,1024,768]{2,1,0:T(8,128)(2,1)} %param.8), kind=kLoop, calls=%fused_computation.2 | loop fusion | bytes 786432 | tf_op jit(solution)/shard_map/slice | solution.py:358
  9.1 4.0 %collective-permute-start.2 = (bf16[128,768]{1,0:T(8,128)(2,1)}, bf16[128,768]{1,0:T(8,128)(2,1)S(1)}, u32[]{:S(2)}, u32[]{:S(2)}) collective-permute-start(bf16[128,768]{1,0:T(8,128)(2,1)} %get-tuple-element.76), channel_id=1, source_target_pairs={{0,1},{1,2},{2,3},{3,4},{4,5},{5,6},{6,7},{7,8},{8,9},{9,10},{10,1... | collective-permute-start | bytes 589832 | tf_op jit(solution)/shard_map/ppermute | solution.py:357
  13.1 1.3 collective-permute-start.3
  14.4 0.0 copy-done.19
  14.4 0.0 copy-done
  14.4 0.0 copy-start.16
  14.4 1.3 copy-done.16
  15.7 0.0 copy-start.17
  15.7 1.3 copy-done.17
  17.0 4.7 %enter.1 = (bf16[2,768,768]{2,1,0:T(8,128)(2,1)S(1)}, bf16[2,768,768]{2,1,0:T(8,128)(2,1)S(1)}, bf16[1024,768]{1,0:T(8,128)(2,1)S(1)}, bf16[1024,768]{1,0:T(8,128)(2,1)S(1)}) custom-call(s32[1,768]{1,0:T(1,128)S(1)} %reshape.30.pairs, bf16[2,768,384]{2,1,0:T(8,128)(2,1)S(1)} %copy-done.16, bf16[2,384,768]{2,1,0:T(8,128)(2,1)S(1)} %copy-done.17, ...), custom_call_target="tpu_custom_call" | custom-call | flops 3623878656 | bytes 15728640 | tf_op jit(solution)/shard_map/enter/pallas_call | solution.py:388
  21.7 0.0 copy-start.2
  21.7 0.0 copy-start.4
  21.7 0.0 collective-permute-done.top
  21.7 0.0 collective-permute-done.1.bot
  21.7 0.0 copy-done.15
  21.7 0.0 copy-done.18
  21.8 0.0 copy-start.14
  21.8 13.3 %middle.1 = (bf16[1408,768]{1,0:T(8,128)(2,1)S(1)}, bf16[1408,768]{1,0:T(8,128)(2,1)S(1)}, bf16[1408,768]{1,0:T(8,128)(2,1)S(1)}, bf16[1408,768]{1,0:T(8,128)(2,...) custom-call(s32[2]{0:T(128)S(1)} %copy-done.18, ...), custom_call_target="tpu_custom_call" | custom-call | flops 7247757312 | bytes 30277632 | tf_op jit(solution)/shard_map/middle/pallas_call | solution.py:393
  35.0 0.0 copy-start.6
  35.1 0.0 collective-permute-done.2.top
  35.1 0.0 collective-permute-done.3.bot
  35.1 0.0 copy-done.14
  35.1 7.8 %top.1 = (bf16[1280,768]{1,0:T(8,128)(2,1)S(1)}, bf16[1280,768]{1,0:T(8,128)(2,1)S(1)}, bf16[1280,768]{1,0:T(8,128)(2,1)S(1)}, bf16[1280,768]{1,0:T(8,128)(2,1)S(1)}) custom-call(s32[2]{0:T(128)S(1)} %copy-done.18, bf16[1408,768]{1,0:T(8,128)(2,1)S(1)} %get-tuple-element.44.mid.tc, bf16[1024,768]{1,0:T(8,128)(2,1)S(1)} %bitcast.21, ...), custom_call_target="tpu_custom_call" | custom-call | flops 3623878656 | bytes 15728640 | tf_op jit(solution)/shard_map/top/pallas_call | solution.py:399
  42.9 0.0 copy-start.8
  42.9 4.0 %sums_top.1.upper = bf16[5888,128]{1,0:T(8,128)(2,1)S(1)} custom-call(s32[1,768]{1,0:T(1,128)S(1)} %reshape.30.pairs, bf16[1280,768]{1,0:T(8,128)(2,1)S(1)} %get-tuple-element.64.act, bf16[1024,768]{1,0:T(8,128)(2,1)S(1)} %bitcast.22, bf16[1280,768]{1,0:T(8,128)(2,1)S(1)} %get-tuple-element.54.tm, bf16[1408,768]{1,0:T(8,128)(2,1)S(1)} %get-tuple-element.44.mid.tc, ...), custom_call_target="tpu_custom_call" | custom-call | flops 3623878656 | bytes 3014656 | tf_op jit(solution)/shard_map/sums_top/pallas_call | solution.py:409
  46.9 0.0 copy-done.8
  46.9 0.0 copy-done.2
  46.9 0.0 copy-done.4
  47.0 0.0 copy-done.6
  47.0 12.0 %back.1 = (bf16[1152,768]{1,0:T(8,128)(2,1)S(1)}, bf16[1152,768]{1,0:T(8,128)(2,1)S(1)}, bf16[2304,128]{1,0:T(8,128)(2,1)S(1)}) custom-call(s32[2]{0:T(128)S(1)} %copy-done.18, s32[1]{0:T(128)} %bitcast.1.block, s32[1,768]{1,0:T(1,128)S(1)} %reshape.30.pairs, bf16[1280,768]{1,0:T(8,128)(2,1)S(1)} %get-tuple-element.45.mid.d_pre, ...), custom_call_target="tpu_custom_call" | custom-call | flops 6039797760 | bytes 8257536 | tf_op jit(solution)/shard_map/back/pallas_call | solution.py:415
  59.0 0.0 copy-start.10
  59.0 4.3 %sums.1 = (bf16[5888,128]{1,0:T(8,128)(2,1)S(1)}, bf16[5888,128]{1,0:T(8,128)(2,1)S(1)}) custom-call(s32[1]{0:T(128)} %bitcast.core.layer, s32[1,768]{1,0:T(1,128)S(1)} %reshape.30.pairs, bf16[1408,768]{1,0:T(8,128)(2,1)S(1)} %get-tuple-element.43.act, bf16[1152,768]{1,0:T(8,128)(2,1)S(1)} %get-tuple-element.49.cot, ...), custom_call_target="tpu_custom_call" | custom-call | flops 3623878656 | bytes 6029312 | tf_op jit(solution)/shard_map/sums/pallas_call | solution.py:423
  63.3 0.0 copy-done.10
  63.3 1.6 collective-permute-start.4
  64.9 7.1 %last.1 = (bf16[2304,128]{1,0:T(8,128)(2,1)S(1)}, bf16[2304,128]{1,0:T(8,128)(2,1)S(1)}, bf16[1024,768]{1,0:T(8,128)(2,1)S(1)}) custom-call(s32[1]{0:T(128)} %bitcast.core.layer, s32[2]{0:T(128)S(1)} %copy-done.18, s32[1,768]{1,0:T(1,128)S(1)} %reshape.30.pairs, bf16[1152,768]{1,0:T(8,128)(2,1)S(1)} %get-tuple-element.52.d_pre.mid, ...), custom_call_target="tpu_custom_call" | custom-call | flops 3623878656 | bytes 5505024 | tf_op jit(solution)/shard_map/last/pallas_call | solution.py:428
  72.0 0.0 copy-start.12
  72.0 0.3 collective-permute-start.5
  72.3 2.0 %collective-permute-done.5.got_b = bf16[2304,128]{1,0:T(8,128)(2,1)S(1)} collective-permute-done((bf16[2304,128]{1,0:T(8,128)(2,1)S(1)}, bf16[2304,128]{1,0:T(8,128)(2,1)S(1)}, u32[]{:S(2)}, u32[]{:S(2)}) %collective-permute-start.5) | collective-permute-done | bytes 589856 | tf_op jit(solution)/shard_map/ppermute | solution.py:371
  74.3 0.0 collective-permute-done.4.got_a
  74.3 1.9 %join.1 = bf16[8192,128]{1,0:T(8,128)(2,1)} custom-call(bf16[5888,128]{1,0:T(8,128)(2,1)S(1)} %get-tuple-element.56.keep_a, bf16[5888,128]{1,0:T(8,128)(2,1)S(1)} %collective-permute-done.4.got_a, bf16[2304,128]{1,0:T(8,128)(2,1)S(1)} %get-tuple-element.60.keep_b, bf16[2304,128]{1,0:T(8,128)(2,1)S(1)} %collective-permute-done.5.got_b), custom_call_target="tpu_custom_call" | custom-call | bytes 4194304 | tf_op jit(solution)/shard_map/join/pallas_call | solution.py:435
  76.2 0.0 copy-done.12
  76.2 15.6 %all-to-all-start = ((bf16[64,128,128]{2,1,0:T(8,128)(2,1)}), bf16[64,128,128]{2,1,0:T(8,128)(2,1)S(1)}, u32[]{:S(2)}, u32[]{:S(2)}) async-start(bf16[64,128,128]{2,1,0:T(8,128)(2,1)} %bitcast.8), calls=%async_computation | async-start | bytes 4194304 | tf_op jit(solution)/shard_map/all_to_all | solution.py:367
  91.8 0.0 copy-start.1
  91.8 1.4 copy-done.1
  93.2 1.7 %copy-done.5 = bf16[2,768,768]{2,1,0:T(8,128)(2,1)S(1)} copy-done((bf16[2,768,768]{2,1,0:T(8,128)(2,1)S(1)}, bf16[2,768,768]{2,1,0:T(8,128)(2,1)}, u32[]{:S(2)}) %copy-start.5) | copy-done | bytes 2359320
  94.9 1.5 copy-done.11
  96.4 1.4 copy-done.13
  97.8 3.6 %input.1 = bf16[1024,768]{1,0:T(8,128)(2,1)} custom-call(bf16[1024,768]{1,0:T(8,128)(2,1)S(1)} %copy-done.13, bf16[1024,768]{1,0:T(8,128)(2,1)S(1)} %bitcast.20, bf16[1152,768]{1,0:T(8,128)(2,1)S(1)} %copy-done.11, bf16[2,768,768]{2,1,0:T(8,128)(2,1)S(1)} %copy-done.5), custom_call_target="tpu_custom_call" | custom-call | flops 1207959552 | bytes 3145728 | tf_op jit(solution)/shard_map/input/pallas_call | solution.py:442
  101.3 0.0 copy-done.3
  101.3 0.0 copy-done.7
  101.3 0.0 copy-done.9
  101.3 3.0 %out.1 = bf16[1024,768]{1,0:T(8,128)(2,1)} custom-call(bf16[1280,768]{1,0:T(8,128)(2,1)S(1)} %copy-done.9, bf16[1408,768]{1,0:T(8,128)(2,1)S(1)} %copy-done.7, bf16[2,768,768]{2,1,0:T(8,128)(2,1)S(1)} %copy-done.3), custom_call_target="tpu_custom_call" | custom-call | flops 1207959552 | bytes 3145728 | tf_op jit(solution)/shard_map/out/pallas_call | solution.py:439
  104.3 16.1 %all-to-all-done.parts = bf16[64,128,128]{2,1,0:T(8,128)(2,1)S(1)} async-done(((bf16[64,128,128]{2,1,0:T(8,128)(2,1)}), bf16[64,128,128]{2,1,0:T(8,128)(2,1)S(1)}, u32[]{:S(2)}, u32[]{:S(2)}) %all-to-all-start) | async-done | bytes 2097184 | tf_op jit(solution)/shard_map/all_to_all | solution.py:367
  120.5 0.5 share.1
  120.9 35.5 %all_to_all.10 = bf16[64,128,128]{2,1,0:T(8,128)(2,1)S(1)} all-to-all(bf16[64,128,128]{2,1,0:T(8,128)(2,1)S(1)} %share.1), channel_id=1, replica_groups=mesh['xh'=2,'core'=2,'z'=4,'xl'=2,'y'=4] {'xh','z','xl','y'}, dimensions={0} | all-to-all | bytes 4194304 | tf_op jit(solution)/shard_map/all_to_all | solution.py:367
  156.4 2.2 %collective-permute-start.6 = (bf16[8192,128]{1,0:T(8,128)(2,1)S(1)}, bf16[8192,128]{1,0:T(8,128)(2,1)S(1)}, u32[]{:S(2)}, u32[]{:S(2)}) collective-permute-start(bf16[8192,128]{1,0:T(8,128)(2,1)S(1)} %bitcast.16), channel_id=1, source_target_pairs={{0,32},{32,0},{1,33},{33,1},{2,34},{34,2},{3,35},{35,3},{4,36},{36... | collective-permute-start | bytes 6291464 | tf_op jit(solution)/shard_map/ppermute | solution.py:371
  158.7 2.3 %finish.2 = (f32[2,768,384]{2,1,0:T(8,128)}, f32[2,3,384,384]{3,2,1,0:T(8,128)}, f32[2,384,768]{2,1,0:T(8,128)}) custom-call(s32[1]{0:T(128)} %bitcast.core.layer, bf16[8192,128]{1,0:T(8,128)(2,1)S(1)} %bitcast.17), custom_call_target="tpu_custom_call" | custom-call | tf_op jit(solution)/shard_map/finish/pallas_call | solution.py:241
  160.9 1.5 collective-permute-done.6.ref
  162.4 2.3 %finish.3 = (f32[2,768,384]{2,1,0:T(8,128)}, f32[2,3,384,384]{3,2,1,0:T(8,128)}, f32[2,384,768]{2,1,0:T(8,128)}) custom-call(s32[1]{0:T(128)S(6)} %sub.3.layer, bf16[8192,128]{1,0:T(8,128)(2,1)S(1)} %collective-permute-done.6.ref, f32[2,768,384]{2,1,0:T(8,128)} %get-tuple-element.69.rest_0_, ...), custom_call_target="tpu_custom_call", output_to_operand_aliasing={{0}: (2, {}), {1}: (3, {}), {2}: (4, {})} | custom-call | tf_op jit(solution)/shard_map/finish/pallas_call | solution.py:241
  (9 shorter events, 0.0 us)
Async XLA Ops:
  0.6 13.8 %copy-start = (bf16[1,1024,768]{2,1,0:T(8,128)(2,1)S(1)}, bf16[1,1024,768]{2,1,0:T(8,128)(2,1)}, u32[]{:S(2)}) copy-start(bf16[1,1024,768]{2,1,0:T(8,128)(2,1)} %param.7) | copy-start | bytes 4718596
  0.6 13.8 %copy-start.19 = (s32[768]{0:T(1024)S(1)}, s32[768]{0:T(1024)}, u32[]{:S(2)}) copy-start(s32[768]{0:T(1024)} %param.9) | copy-start | bytes 9220
  1.9 19.8 %collective-permute-start = (bf16[256,768]{1,0:T(8,128)(2,1)S(1)}, bf16[256,768]{1,0:T(8,128)(2,1)S(1)}, u32[]{:S(2)}, u32[]{:S(2)}) collective-permute-start(bf16[256,768]{1,0:T(8,128)(2,1)S(1)} %get-tuple-element.78), channel_id=1, source_target_pairs={{0,1},{1,2},{2,3},{3,4},{4,5},{5,6},{6,7},{7,8},{8,9},{9,10},{10,1... | collective-permute-start | bytes 1179656 | tf_op jit(solution)/shard_map/ppermute | solution.py:357
  6.0 15.7 %collective-permute-start.1 = (bf16[256,768]{1,0:T(8,128)(2,1)S(1)}, bf16[256,768]{1,0:T(8,128)(2,1)S(1)}, u32[]{:S(2)}, u32[]{:S(2)}) collective-permute-start(bf16[256,768]{1,0:T(8,128)(2,1)S(1)} %get-tuple-element.77), channel_id=1, source_target_pairs={{1,0},{2,1},{3,2},{4,3},{5,4},{6,5},{7,6},{8,7},{9,8},{10,9},{11,1... | collective-permute-start | bytes 1179656 | tf_op jit(solution)/shard_map/ppermute | solution.py:358
  9.1 26.0 %collective-permute-start.2 = (bf16[128,768]{1,0:T(8,128)(2,1)}, bf16[128,768]{1,0:T(8,128)(2,1)S(1)}, u32[]{:S(2)}, u32[]{:S(2)}) collective-permute-start(bf16[128,768]{1,0:T(8,128)(2,1)} %get-tuple-element.76), channel_id=1, source_target_pairs={{0,1},{1,2},{2,3},{3,4},{4,5},{5,6},{6,7},{7,8},{8,9},{9,10},{10,1... | collective-permute-start | bytes 589832 | tf_op jit(solution)/shard_map/ppermute | solution.py:357
  13.1 22.0 %collective-permute-start.3 = (bf16[128,768]{1,0:T(8,128)(2,1)}, bf16[128,768]{1,0:T(8,128)(2,1)S(1)}, u32[]{:S(2)}, u32[]{:S(2)}) collective-permute-start(bf16[128,768]{1,0:T(8,128)(2,1)} %get-tuple-element.75), channel_id=1, source_target_pairs={{1,0},{2,1},{3,2},{4,3},{5,4},{6,5},{7,6},{8,7},{9,8},{10,9},{11,1... | collective-permute-start | bytes 589832 | tf_op jit(solution)/shard_map/ppermute | solution.py:358
  14.4 1.3 copy-start.16
  15.7 1.3 copy-start.17
  17.0 4.8 %copy-start.15 = (bf16[2,3,384,384]{3,2,1,0:T(8,128)(2,1)S(1)}, bf16[2,3,384,384]{3,2,1,0:T(8,128)(2,1)}, u32[]{:S(2)}) copy-start(bf16[2,3,384,384]{3,2,1,0:T(8,128)(2,1)} %weight.7) | copy-start | bytes 5308420
  17.0 4.8 %copy-start.18 = (s32[2]{0:T(128)S(1)}, s32[2]{0:T(128)}, u32[]{:S(2)}) copy-start(s32[2]{0:T(128)} %dil.7) | copy-start | bytes 28
  21.7 25.3 %copy-start.2 = (bf16[2,768,768]{2,1,0:T(8,128)(2,1)}, bf16[2,768,768]{2,1,0:T(8,128)(2,1)S(1)}, u32[]{:S(2)}) copy-start(bf16[2,768,768]{2,1,0:T(8,128)(2,1)S(1)} %get-tuple-element.42.upcat) | copy-start | bytes 7077892
  21.7 25.3 %copy-start.4 = (bf16[2,768,768]{2,1,0:T(8,128)(2,1)}, bf16[2,768,768]{2,1,0:T(8,128)(2,1)S(1)}, u32[]{:S(2)}) copy-start(bf16[2,768,768]{2,1,0:T(8,128)(2,1)S(1)} %get-tuple-element.41.dcat0.dcat) | copy-start | bytes 7077892
  21.8 13.3 %copy-start.14 = (bf16[1,1024,768]{2,1,0:T(8,128)(2,1)S(1)}, bf16[1,1024,768]{2,1,0:T(8,128)(2,1)}, u32[]{:S(2)}) copy-start(bf16[1,1024,768]{2,1,0:T(8,128)(2,1)} %param.8) | copy-start | bytes 4718596
  35.0 11.9 %copy-start.6 = (bf16[1408,768]{1,0:T(8,128)(2,1)}, bf16[1408,768]{1,0:T(8,128)(2,1)S(1)}, u32[]{:S(2)}) copy-start(bf16[1408,768]{1,0:T(8,128)(2,1)S(1)} %get-tuple-element.47.stream) | copy-start | bytes 6488068
  42.9 4.1 %copy-start.8 = (bf16[1280,768]{1,0:T(8,128)(2,1)}, bf16[1280,768]{1,0:T(8,128)(2,1)S(1)}, u32[]{:S(2)}) copy-start(bf16[1280,768]{1,0:T(8,128)(2,1)S(1)} %get-tuple-element.64.act) | copy-start | bytes 5898244
  59.0 4.3 %copy-start.10 = (bf16[1152,768]{1,0:T(8,128)(2,1)}, bf16[1152,768]{1,0:T(8,128)(2,1)S(1)}, u32[]{:S(2)}) copy-start(bf16[1152,768]{1,0:T(8,128)(2,1)S(1)} %get-tuple-element.49.cot) | copy-start | bytes 5308420
  63.3 11.0 %collective-permute-start.4 = (bf16[5888,128]{1,0:T(8,128)(2,1)S(1)}, bf16[5888,128]{1,0:T(8,128)(2,1)S(1)}, u32[]{:S(2)}, u32[]{:S(2)}) collective-permute-start(bf16[5888,128]{1,0:T(8,128)(2,1)S(1)} %get-tuple-element.57), channel_id=1, source_target_pairs={{0,32},{32,0},{1,33},{33,1},{2,34},{34,2},{3,35},{35,3},{4,36},{36... | collective-permute-start | bytes 4521992 | tf_op jit(solution)/shard_map/ppermute | solution.py:371
  72.0 4.2 %copy-start.12 = (bf16[1024,768]{1,0:T(8,128)(2,1)}, bf16[1024,768]{1,0:T(8,128)(2,1)S(1)}, u32[]{:S(2)}) copy-start(bf16[1024,768]{1,0:T(8,128)(2,1)S(1)} %get-tuple-element.65.d_inner) | copy-start | bytes 4718596
  72.0 2.3 %collective-permute-start.5 = (bf16[2304,128]{1,0:T(8,128)(2,1)S(1)}, bf16[2304,128]{1,0:T(8,128)(2,1)S(1)}, u32[]{:S(2)}, u32[]{:S(2)}) collective-permute-start(bf16[2304,128]{1,0:T(8,128)(2,1)S(1)} %get-tuple-element.61), channel_id=1, source_target_pairs={{0,32},{32,0},{1,33},{33,1},{2,34},{34,2},{3,35},{35,3},{4,36},{36... | collective-permute-start | bytes 1769480 | tf_op jit(solution)/shard_map/ppermute | solution.py:371
  76.2 44.2 %all-to-all-start = ((bf16[64,128,128]{2,1,0:T(8,128)(2,1)}), bf16[64,128,128]{2,1,0:T(8,128)(2,1)S(1)}, u32[]{:S(2)}, u32[]{:S(2)}) async-start(bf16[64,128,128]{2,1,0:T(8,128)(2,1)} %bitcast.8), calls=%async_computation | async-start | bytes 4194304 | tf_op jit(solution)/shard_map/all_to_all | solution.py:367
  91.8 1.4 copy-start.1
  93.2 1.7 %copy-start.5 = (bf16[2,768,768]{2,1,0:T(8,128)(2,1)S(1)}, bf16[2,768,768]{2,1,0:T(8,128)(2,1)}, u32[]{:S(2)}) copy-start(bf16[2,768,768]{2,1,0:T(8,128)(2,1)} %copy-done.4) | copy-start | bytes 7077892
  94.9 1.5 copy-start.11
  96.4 1.4 copy-start.13
  97.8 3.6 %copy-start.3 = (bf16[2,768,768]{2,1,0:T(8,128)(2,1)S(1)}, bf16[2,768,768]{2,1,0:T(8,128)(2,1)}, u32[]{:S(2)}) copy-start(bf16[2,768,768]{2,1,0:T(8,128)(2,1)} %copy-done.2) | copy-start | bytes 7077892
  97.8 3.6 %copy-start.7 = (bf16[1408,768]{1,0:T(8,128)(2,1)S(1)}, bf16[1408,768]{1,0:T(8,128)(2,1)}, u32[]{:S(2)}) copy-start(bf16[1408,768]{1,0:T(8,128)(2,1)} %copy-done.6) | copy-start | bytes 6488068
  97.8 3.6 %copy-start.9 = (bf16[1280,768]{1,0:T(8,128)(2,1)S(1)}, bf16[1280,768]{1,0:T(8,128)(2,1)}, u32[]{:S(2)}) copy-start(bf16[1280,768]{1,0:T(8,128)(2,1)} %copy-done.8) | copy-start | bytes 5898244
  156.4 6.0 %collective-permute-start.6 = (bf16[8192,128]{1,0:T(8,128)(2,1)S(1)}, bf16[8192,128]{1,0:T(8,128)(2,1)S(1)}, u32[]{:S(2)}, u32[]{:S(2)}) collective-permute-start(bf16[8192,128]{1,0:T(8,128)(2,1)S(1)} %bitcast.16), channel_id=1, source_target_pairs={{0,32},{32,0},{1,33},{33,1},{2,34},{34,2},{3,35},{35,3},{4,36},{36... | collective-permute-start | bytes 6291464 | tf_op jit(solution)/shard_map/ppermute | solution.py:371

commit v5 on v4

--- a/solution.py
+++ b/solution.py
@@ -16,7 +16,7 @@
 STEPS = ROWS // TILE
 BLOCKS = 32
 MID_ROWS, TOP_ROWS, BACK_ROWS = ROWS + 6 * PAD, ROWS + 4 * PAD, ROWS + 2 * PAD
-MID_TILE, TOP_TILE, BACK_TILE = MID_ROWS // 4, TOP_ROWS // 4, BACK_ROWS // 3
+MID_TILE, TOP_TILE, BACK_TILE = 2 * PAD, TOP_ROWS // 4, BACK_ROWS // 3
 EPS = 1e-06
 ROOT = math.sqrt(2.0 / math.pi)
 CUBE = 0.044715
@@ -119,32 +119,56 @@
     inner[...] = mm(n, dcat[0]).astype(BF)
 
 
-def k_middle(dil, block, mid, x, top, bot, dcat0, weight, upcat, dcat,
-             act, slope, tm, tp, stream, normed, inner, pad, field):
-    start = pl.program_id(0) * MID_TILE
-
-    @pl.when(pl.program_id(0) == 0)
-    def _():
-        lay(field, top[PAD : 4 * PAD, :], x[...], bot[: 3 * PAD, :])
-        ends = []
-        for halo in (top, bot):
-            wide = halo[...].astype(F32)
-            ends.append(mm((wide * scale_of(wide)).astype(BF), dcat0[...]).astype(BF))
-        lay(pad, ends[0], mid[...], ends[1])
-
-    shift(pad, dil[0], start, tm, tp)
-    m = centre(pad, start, MID_TILE)
+def middle_rows(m, x, weight, upcat, dcat, act, slope, tm, tp, stream, normed):
     g, s = gelu_both(conv(tm[...], tp[...], m, weight[...].reshape(3 * B, B)))
     g = g.astype(BF)
     act[...] = g
     slope[...] = s.astype(BF)
-    rows = pl.ds(pl.multiple_of(start, 16), MID_TILE)
-    out = (field[rows, :].astype(F32) + mm(g, upcat[...])).astype(BF)
+    out = (x.astype(F32) + mm(g, upcat[...])).astype(BF)
     stream[...] = out
     wide = out.astype(F32)
     n = (wide * scale_of(wide)).astype(BF)
     normed[...] = n
-    inner[...] = inside(block[0], start - 3 * PAD, mm(n, dcat[...])).astype(BF)
+    return mm(n, dcat[...])
+
+
+def k_within(dil, mid, x, weight, upcat, dcat, act, slope, tm, tp, stream, normed, inner):
+    start = pl.program_id(0) * MID_TILE
+    shift(mid, dil[0], start, tm, tp)
+    rows = centre(x, start, MID_TILE)
+    m = centre(mid, start, MID_TILE)
+    inner[...] = middle_rows(m, rows, weight, upcat, dcat, act, slope, tm, tp, stream, normed).astype(BF)
+
+
+def k_around(dil, block, mid, x, top, bot, dcat0, weight, upcat, dcat, *rest):
+    act, slope, tm, tp, stream, normed, inner, pad, field = rest[7:]
+    step = pl.program_id(0)
+
+    @pl.when(step == 0)
+    def _():
+        field[: 3 * PAD, :] = top[PAD : 4 * PAD, :]
+        field[3 * PAD : 4 * PAD, :] = x[:PAD, :]
+        field[4 * PAD : 5 * PAD, :] = x[ROWS - PAD :, :]
+        field[5 * PAD :, :] = bot[: 3 * PAD, :]
+        ends = []
+        for halo in (top, bot):
+            wide = halo[: 4 * PAD, :].astype(F32)
+            ends.append(mm((wide * scale_of(wide)).astype(BF), dcat0[...]).astype(BF))
+        pad[: 4 * PAD, :] = ends[0]
+        pad[4 * PAD : 6 * PAD, :] = mid[: 2 * PAD, :]
+        pad[6 * PAD : 8 * PAD, :] = mid[ROWS - 2 * PAD :, :]
+        pad[8 * PAD :, :] = ends[1]
+
+    start = pl.multiple_of((step + step // 2) * MID_TILE, MID_TILE)
+    shift(pad, dil[0], start, tm, tp)
+    m = centre(pad, start, MID_TILE)
+    rows = field[pl.ds(pl.multiple_of(step * MID_TILE, MID_TILE), MID_TILE), :]
+    values = middle_rows(m, rows, weight, upcat, dcat, act, slope, tm, tp, stream, normed)
+    inner[...] = inside(block[0], around(step) * MID_TILE - 3 * PAD, values).astype(BF)
+
+
+def around(step):
+    return step + 7 * (step // 2)
 
 
 def k_top(dil, mid, cot, top, bot, weight, upcat, act, d_pre, tm, tp, grad):
@@ -152,7 +176,7 @@
 
     @pl.when(pl.program_id(0) == 0)
     def _():
-        lay(grad, top[...], cot[...], bot[...])
+        lay(grad, top[4 * PAD :, :], cot[...], bot[4 * PAD :, :])
 
     shift(mid, dil[1], start, tm, tp)
     m = centre(mid, start, TOP_TILE)
@@ -266,7 +290,7 @@
 
     @pl.when(pl.program_id(0) == 0)
     def _():
-        lay(given, top[PAD:, :], cot[...], bot[:PAD, :])
+        lay(given, top[5 * PAD :, :], cot[...], bot[4 * PAD : 5 * PAD, :])
 
     shift(mid, dil[1], start, before, after)
     di = conv_back(after[...], before[...], centre(mid, start, BACK_TILE), weight).astype(BF)
@@ -324,7 +348,7 @@
     return jax.ShapeDtypeStruct(dims, kind)
 
 
-def call(body, steps, ins, outs, scratch, flops, name, limit=20):
+def call(body, steps, ins, outs, scratch, flops, name, limit=20, aliases=None):
     size = lambda s: 2 * math.prod(s.shape)
     return pl.pallas_call(
         body,
@@ -333,6 +357,7 @@
         out_specs=[spec for spec, _ in outs],
         out_shape=[form for _, form in outs],
         scratch_shapes=scratch,
+        input_output_aliases=aliases or {},
         compiler_params=pltpu.CompilerParams(vmem_limit_bytes=limit * 1024 * 1024),
         cost_estimate=pl.CostEstimate(
             flops=int(flops), bytes_accessed=2 * sum(size(f) for _, f in outs), transcendentals=0
@@ -353,9 +378,11 @@
     return pltpu.VMEM((rows, C), kind)
 
 
-def edges(cells, rows):
-    top = lax.ppermute(cells[ROWS - rows :], SEQ, [(i, i + 1) for i in range(BLOCKS - 1)])
-    bot = lax.ppermute(cells[:rows], SEQ, [(i + 1, i) for i in range(BLOCKS - 1)])
+def edges(x, cot):
+    last = jnp.concatenate([x[ROWS - 4 * PAD :], cot[ROWS - 2 * PAD :]], axis=0)
+    first = jnp.concatenate([x[: 4 * PAD], cot[: 2 * PAD]], axis=0)
+    top = lax.ppermute(last, SEQ, [(i, i + 1) for i in range(BLOCKS - 1)])
+    bot = lax.ppermute(first, SEQ, [(i + 1, i) for i in range(BLOCKS - 1)])
     return top, bot
 
 
@@ -380,26 +407,31 @@
     resident = whole(ROWS, C)
     taps_w = [pl.BlockSpec((None, 3, B, B), lambda i, n=n: (n, 0, 0, 0), pipeline_mode=pl.Buffered(1)) for n in range(2)]
     square_of = [pl.BlockSpec((None, C, C), lambda i, n=n: (n, 0, 0), pipeline_mode=pl.Buffered(1)) for n in range(2)]
-    halo, c_halo = whole(4 * PAD, C), whole(2 * PAD, C)
-
-    top, bot = edges(x, 4 * PAD)
-    ctop, cbot = edges(cot, 2 * PAD)
+    halo = whole(6 * PAD, C)
+
+    top, bot = edges(x, cot)
     squares = (whole(2, C, C), shape(2, C, C))
     dcat, upcat, normed0, inner0 = call(
         k_enter, STEPS, [whole(1, C), whole(2, C, B), whole(2, B, C), tile()],
         [squares] * 2 + [FULL, FULL], [], 3 * UNIT, "enter",
     )(pairs, down_weight, up_weight, x)
-    mid = (tile(MID_TILE), shape(MID_ROWS, C))
+    form = shape(MID_ROWS, C)
+    held = call(
+        k_within, 7, [scalar(), resident, resident, taps_w[0], square_of[0], square_of[1]],
+        [(pl.BlockSpec((MID_TILE, C), lambda i: (i + 2, 0)), form)] * 7, [], 3 * UNIT, "within",
+    )(dilations, inner0, x, conv_weight, upcat, dcat)
     act0, slope0, tm0, tp0, stream1, normed1, inner1 = call(
-        k_middle, 4,
-        [scalar(), scalar(), resident, resident, halo, halo, square_of[0], taps_w[0], square_of[0], square_of[1]],
-        [mid] * 7, [store(ROWS + 8 * PAD), store(MID_ROWS)], 6 * UNIT, "middle",
-    )(dilations, block, inner0, x, top, bot, dcat, conv_weight, upcat, dcat)
+        k_around, 4,
+        [scalar(), scalar(), resident, resident, halo, halo, square_of[0], taps_w[0], square_of[0], square_of[1]]
+        + [pl.BlockSpec(memory_space=pl.ANY)] * 7,
+        [(pl.BlockSpec((MID_TILE, C), lambda i: (around(i), 0)), form)] * 7,
+        [store(12 * PAD), store(8 * PAD)], 3 * UNIT, "around", aliases={10 + i: i for i in range(7)},
+    )(dilations, block, inner0, x, top, bot, dcat, conv_weight, upcat, dcat, *held)
     upper = (tile(TOP_TILE), shape(TOP_ROWS, C))
     act1, d_pre1, tm1, tp1 = call(
-        k_top, 4, [scalar(), whole(MID_ROWS, C), resident, c_halo, c_halo, taps_w[1], square_of[1]],
+        k_top, 4, [scalar(), whole(MID_ROWS, C), resident, halo, halo, taps_w[1], square_of[1]],
         [upper] * 4, [store(TOP_ROWS)], 3 * UNIT, "top",
-    )(dilations, inner1, cot, ctop, cbot, conv_weight, upcat)
+    )(dilations, inner1, cot, top, bot, conv_weight, upcat)
     core = lax.axis_index("core").reshape(1)
     sums = (whole(REST, LANES), shape(REST, LANES))
     downs = (whole(DOWN, LANES), shape(DOWN, LANES))
@@ -414,12 +446,12 @@
     back = (tile(BACK_TILE), shape(BACK_ROWS, C))
     grad, d_pre0, down1 = call(
         functools.partial(k_back, factor), 3,
-        [scalar(), scalar(), whole(1, C), wide_top, taps_w[1], wide_mid, wide_mid, resident, c_halo, c_halo,
+        [scalar(), scalar(), whole(1, C), wide_top, taps_w[1], wide_mid, wide_mid, resident, halo, halo,
          square_of[1], square_of[0], wide_mid],
         [back, back, downs],
         [store(BACK_TILE), store(BACK_TILE), store(BACK_ROWS), store(BACK_ROWS)],
         5 * UNIT, "back",
-    )(dilations, block, pairs, d_pre1, conv_weight, normed1, stream1, cot, ctop, cbot, dcat, upcat, slope0)
+    )(dilations, block, pairs, d_pre1, conv_weight, normed1, stream1, cot, top, bot, dcat, upcat, slope0)
     send_a, keep_a = call(
         functools.partial(k_sums, factor), 1,
         [scalar(), whole(1, C), wide_mid, wide_back, wide_mid, resident, wide_mid, wide_back, sums[0]],

time: 165 us -> 166 us (level)
  starting transfers between devices: 30.4 us -> 21.4 us
  Pallas kernels: 66.6 us -> 71.1 us
  other arithmetic: 0 us -> 1.71 us
    ppermute x4 -> x2, starting transfers between devices: 10.6 us -> 5.33 us  [the longest x1 4.05 us: edges(): top = lax.ppermute(last, SEQ, [(i, i + 1) for i in range(BLOCKS - 1)])]
    pallas_call x2 -> x3, Pallas kernels: 21 us -> 25.7 us  [the longest x1 10.6 us: local(): call(k_within, 7, [scalar(), resident, resident, taps_w[0], square_of[0],...]
    all_to_all x1, starting transfers between devices: 15.6 us -> 12.8 us  [exchange(): return lax.all_to_all(parts, CHIPS, 0, 0, tiled=True)]
    unnamed x40, local copies, waits for them, and re-layouts: 8.56 us -> 10.7 us
    concatenate x0 -> x2, other arithmetic: none -> 1.71 us  [the longest x1 0.85 us: edges(): last = jnp.concatenate([x[ROWS - 4 * PAD:], cot[ROWS - 2 * PAD:]], axis=0)]
  transfers between devices with their start and end apart: 8 -> 6, of which waited for: 3 -> 3; matrix products, arithmetic and copies ran while one was open for 1% -> 1% of each run, Pallas kernels for 21% -> 19%
where the time goes in v5:
time: 166 us; the launch traced here: 165 us
  Pallas kernels  71.1 us (43%)
  blocking collectives  35.5 us (21%)
  starting transfers between devices  21.4 us (13%)
  waiting for transfers between devices  21.2 us (13%)
  local copies, waits for them, and re-layouts  13 us (8%)
  other arithmetic  1.71 us (1%)
    all_to_all x1, blocking collectives, exchange(): return lax.all_to_all(parts, CHIPS, 0, 0, tiled=True)  35.5 us
    all_to_all x1, waiting for transfers between devices, exchange(): return lax.all_to_all(parts, CHIPS, 0, 0, tiled=True)  17.7 us
    all_to_all x1, starting transfers between devices, exchange(): return lax.all_to_all(parts, CHIPS, 0, 0, tiled=True)  12.8 us
    pallas_call x1, Pallas kernels, local(): call(functools.partial(k_back, factor), 3, [scalar(), scalar(), whole(1,...  11.9 us
    unnamed x40, local copies, waits for them, and re-layouts  10.7 us
    pallas_call x1, Pallas kernels, local(): call(k_within, 7, [scalar(), resident, resident, taps_w[0], square_of[0],...  10.6 us
    pallas_call x1, Pallas kernels, local(): call(k_top, 4, [scalar(), whole(MID_ROWS, C), resident, halo, halo, taps_...  7.78 us
    pallas_call x1, Pallas kernels, local(): call(k_around, 4, [scalar(), scalar(), resident, resident, halo, halo, sq...  7.29 us
  transfers between devices with their start and end apart: 6, of which 3 were waited for; matrix products, arithmetic and copies ran while one was open for 1% of the time, Pallas kernels for 19%

profile of v5, /device:TPU:1, one launch (start us, length us, event | category | flops | bytes accessed | tf_op | source)
XLA Modules:
  0.0 164.8 jit_solution(4791159384175046004)
XLA Ops:
  0.6 1.2 slice_bitcast_fusion
  1.8 0.0 copy-start.19
  1.8 1.1 slice_bitcast_fusion.2
  2.9 0.9 pad_maximum_fusion
  3.7 4.1 %collective-permute-start = (bf16[384,768]{1,0:T(8,128)(2,1)}, bf16[384,768]{1,0:T(8,128)(2,1)S(1)}, u32[]{:S(2)}, u32[]{:S(2)}) collective-permute-start(bf16[384,768]{1,0:T(8,128)(2,1)} %pad_maximum_fusion), channel_id=1, source_target_pairs={{0,1},{1,2},{2,3},{3,4},{4,5},{5,6},{6,7},{7,8},{8,9},{9,10},{10,1... | collective-permute-start | bytes 1769480 | tf_op jit(solution)/shard_map/ppermute | solution.py:384
  7.8 0.9 pad_maximum_fusion.1
  8.6 1.3 collective-permute-start.1
  9.9 0.0 copy-done.19
  10.0 0.0 copy-start
  10.0 1.4 copy-done
  11.4 0.0 copy-start.17
  11.4 1.3 copy-done.17
  12.6 0.0 copy-start.18
  12.7 1.3 copy-done.18
  13.9 0.0 copy-start.1
  13.9 4.6 %enter.1 = (bf16[2,768,768]{2,1,0:T(8,128)(2,1)S(1)}, bf16[2,768,768]{2,1,0:T(8,128)(2,1)S(1)}, bf16[1024,768]{1,0:T(8,128)(2,1)S(1)}, bf16[1024,768]{1,0:T(8,128)(2,1)S(1)}) custom-call(s32[1,768]{1,0:T(1,128)S(1)} %reshape.30.pairs, bf16[2,768,384]{2,1,0:T(8,128)(2,1)S(1)} %copy-done.17, bf16[2,384,768]{2,1,0:T(8,128)(2,1)S(1)} %copy-done.18, ...), custom_call_target="tpu_custom_call" | custom-call | flops 3623878656 | bytes 15728640 | tf_op jit(solution)/shard_map/enter/pallas_call | solution.py:414
  18.5 0.0 copy-start.3
  18.5 0.0 copy-done.1
  18.5 0.0 copy-done.10
  18.5 0.0 copy-done.16
  18.5 10.6 %within.1 = (bf16[1408,768]{1,0:T(8,128)(2,1)S(1)}, bf16[1408,768]{1,0:T(8,128)(2,1)S(1)}, bf16[1408,768]{1,0:T(8,128)(2,1)S(1)}, bf16[1408,768]{1,0:T(8,128)(2,...) custom-call(s32[2]{0:T(128)S(1)} %copy-done.16, ...), custom_call_target="tpu_custom_call" | custom-call | flops 3623878656 | bytes 30277632 | tf_op jit(solution)/shard_map/within/pallas_call | solution.py:419
  29.2 0.0 collective-permute-done.top
  29.2 0.0 collective-permute-done.1.bot
  29.2 0.0 copy-start.15
  29.2 7.3 %around.1 = (bf16[1408,768]{1,0:T(8,128)(2,1)S(1)}, bf16[1408,768]{1,0:T(8,128)(2,1)S(1)}, bf16[1408,768]{1,0:T(8,128)(2,1)S(1)}, bf16[1408,768]{1,0:T(8,128)(2,...) custom-call(s32[2]{0:T(128)S(1)} %copy-done.16, ...), custom_call_target="tpu_custom_call", output_to_operand_aliasing={{0}: (10, {}), {1}: (11, {}), {2}: (12, {}), {3}: (13, {}),... | custom-call | flops 3623878656 | bytes 30277632 | tf_op jit(solution)/shard_map/around/pallas_call | solution.py:423
  36.5 0.0 copy-start.5
  36.5 0.0 copy-done.15
  36.5 7.8 %top.1 = (bf16[1280,768]{1,0:T(8,128)(2,1)S(1)}, bf16[1280,768]{1,0:T(8,128)(2,1)S(1)}, bf16[1280,768]{1,0:T(8,128)(2,1)S(1)}, bf16[1280,768]{1,0:T(8,128)(2,1)S(1)}) custom-call(s32[2]{0:T(128)S(1)} %copy-done.16, bf16[1408,768]{1,0:T(8,128)(2,1)S(1)} %get-tuple-element.58.mid.tc, bf16[1024,768]{1,0:T(8,128)(2,1)S(1)} %bitcast.23, ...), custom_call_target="tpu_custom_call" | custom-call | flops 3623878656 | bytes 15728640 | tf_op jit(solution)/shard_map/top/pallas_call | solution.py:431
  44.3 0.0 copy-start.8
  44.3 4.1 %sums_top.1.upper = bf16[5888,128]{1,0:T(8,128)(2,1)S(1)} custom-call(s32[1,768]{1,0:T(1,128)S(1)} %reshape.30.pairs, bf16[1280,768]{1,0:T(8,128)(2,1)S(1)} %get-tuple-element.78.act, bf16[1024,768]{1,0:T(8,128)(2,1)S(1)} %bitcast.24, bf16[1280,768]{1,0:T(8,128)(2,1)S(1)} %get-tuple-element.68.tm, bf16[1408,768]{1,0:T(8,128)(2,1)S(1)} %get-tuple-element.58.mid.tc, ...), custom_call_target="tpu_custom_call" | custom-call | flops 3623878656 | bytes 3014656 | tf_op jit(solution)/shard_map/sums_top/pallas_call | solution.py:441
  48.4 0.0 copy-done.8
  48.4 0.0 copy-done.3
  48.4 0.0 copy-done.5
  48.4 11.9 %back.1 = (bf16[1152,768]{1,0:T(8,128)(2,1)S(1)}, bf16[1152,768]{1,0:T(8,128)(2,1)S(1)}, bf16[2304,128]{1,0:T(8,128)(2,1)S(1)}) custom-call(s32[2]{0:T(128)S(1)} %copy-done.16, s32[1]{0:T(128)} %bitcast.1.block, s32[1,768]{1,0:T(1,128)S(1)} %reshape.30.pairs, bf16[1280,768]{1,0:T(8,128)(2,1)S(1)} %get-tuple-element.59.mid.d_pre, ...), custom_call_target="tpu_custom_call" | custom-call | flops 6039797760 | bytes 8257536 | tf_op jit(solution)/shard_map/back/pallas_call | solution.py:447
  60.3 0.0 copy-start.11
  60.3 4.3 %sums.1 = (bf16[5888,128]{1,0:T(8,128)(2,1)S(1)}, bf16[5888,128]{1,0:T(8,128)(2,1)S(1)}) custom-call(s32[1]{0:T(128)} %bitcast.core.layer, s32[1,768]{1,0:T(1,128)S(1)} %reshape.30.pairs, bf16[1408,768]{1,0:T(8,128)(2,1)S(1)} %get-tuple-element.57.act, bf16[1152,768]{1,0:T(8,128)(2,1)S(1)} %get-tuple-element.63.cot, ...), custom_call_target="tpu_custom_call" | custom-call | flops 3623878656 | bytes 6029312 | tf_op jit(solution)/shard_map/sums/pallas_call | solution.py:455
  64.6 0.0 copy-done.11
  64.6 1.0 collective-permute-start.2
  65.6 7.1 %last.1 = (bf16[2304,128]{1,0:T(8,128)(2,1)S(1)}, bf16[2304,128]{1,0:T(8,128)(2,1)S(1)}, bf16[1024,768]{1,0:T(8,128)(2,1)S(1)}) custom-call(s32[1]{0:T(128)} %bitcast.core.layer, s32[2]{0:T(128)S(1)} %copy-done.16, s32[1,768]{1,0:T(1,128)S(1)} %reshape.30.pairs, bf16[1152,768]{1,0:T(8,128)(2,1)S(1)} %get-tuple-element.66.d_pre.mid, ...), custom_call_target="tpu_custom_call" | custom-call | flops 3623878656 | bytes 5505024 | tf_op jit(solution)/shard_map/last/pallas_call | solution.py:460
  72.7 0.0 copy-start.13
  72.7 1.1 copy-done.13
  73.8 0.0 collective-permute-start.3
  73.8 2.0 %collective-permute-done.3.got_b = bf16[2304,128]{1,0:T(8,128)(2,1)S(1)} collective-permute-done((bf16[2304,128]{1,0:T(8,128)(2,1)S(1)}, bf16[2304,128]{1,0:T(8,128)(2,1)S(1)}, u32[]{:S(2)}, u32[]{:S(2)}) %collective-permute-start.3) | collective-permute-done | bytes 589856 | tf_op jit(solution)/shard_map/ppermute | solution.py:398
  75.8 0.0 collective-permute-done.2.got_a
  75.8 0.5 join.1
  76.3 0.0 copy-start.7
  76.3 1.3 copy-done.7
  77.6 12.8 %all-to-all-start = ((bf16[64,128,128]{2,1,0:T(8,128)(2,1)}), bf16[64,128,128]{2,1,0:T(8,128)(2,1)}, u32[]{:S(2)}, u32[]{:S(2)}) async-start(bf16[64,128,128]{2,1,0:T(8,128)(2,1)} %bitcast.20), calls=%async_computation | async-start | bytes 4194304 | tf_op jit(solution)/shard_map/all_to_all | solution.py:394
  90.5 0.0 copy-start.2
  90.5 1.4 copy-done.2
  91.9 1.5 copy-done.12
  93.4 1.4 copy-done.14
  94.8 3.6 %input.1 = bf16[1024,768]{1,0:T(8,128)(2,1)} custom-call(bf16[1024,768]{1,0:T(8,128)(2,1)S(1)} %copy-done.14, bf16[1024,768]{1,0:T(8,128)(2,1)S(1)} %bitcast.19, bf16[1152,768]{1,0:T(8,128)(2,1)S(1)} %copy-done.12, bf16[2,768,768]{2,1,0:T(8,128)(2,1)S(1)} %get-tuple-element.48.dcat.dcat0), custom_call_target="tpu_custom_call" | custom-call | flops 1207959552 | bytes 3145728 | tf_op jit(solution)/shard_map/input/pallas_call | solution.py:474
  98.3 0.0 copy-done.4
  98.3 0.0 copy-done.6
  98.3 0.0 copy-done.9
  98.3 3.0 %out.1 = bf16[1024,768]{1,0:T(8,128)(2,1)} custom-call(bf16[1280,768]{1,0:T(8,128)(2,1)S(1)} %copy-done.9, bf16[1408,768]{1,0:T(8,128)(2,1)S(1)} %copy-done.6, bf16[2,768,768]{2,1,0:T(8,128)(2,1)S(1)} %copy-done.4), custom_call_target="tpu_custom_call" | custom-call | flops 1207959552 | bytes 3145728 | tf_op jit(solution)/shard_map/out/pallas_call | solution.py:471
  101.3 17.7 %all-to-all-done.parts = bf16[64,128,128]{2,1,0:T(8,128)(2,1)} async-done(((bf16[64,128,128]{2,1,0:T(8,128)(2,1)}), bf16[64,128,128]{2,1,0:T(8,128)(2,1)}, u32[]{:S(2)}, u32[]{:S(2)}) %all-to-all-start) | async-done | bytes 2097184 | tf_op jit(solution)/shard_map/all_to_all | solution.py:394
  119.0 2.1 %share.1 = bf16[64,128,128]{2,1,0:T(8,128)(2,1)S(1)} custom-call(bf16[64,128,128]{2,1,0:T(8,128)(2,1)} %all-to-all-done.parts), custom_call_target="tpu_custom_call" | custom-call | bytes 4194304 | tf_op jit(solution)/shard_map/share/pallas_call | solution.py:479
  121.0 35.5 %all_to_all.10 = bf16[64,128,128]{2,1,0:T(8,128)(2,1)S(1)} all-to-all(bf16[64,128,128]{2,1,0:T(8,128)(2,1)S(1)} %share.1), channel_id=1, replica_groups=mesh['xh'=2,'core'=2,'z'=4,'xl'=2,'y'=4] {'xh','z','xl','y'}, dimensions={0} | all-to-all | bytes 4194304 | tf_op jit(solution)/shard_map/all_to_all | solution.py:394
  156.6 2.2 %collective-permute-start.4 = (bf16[8192,128]{1,0:T(8,128)(2,1)S(1)}, bf16[8192,128]{1,0:T(8,128)(2,1)S(1)}, u32[]{:S(2)}, u32[]{:S(2)}) collective-permute-start(bf16[8192,128]{1,0:T(8,128)(2,1)S(1)} %bitcast.21), channel_id=1, source_target_pairs={{0,32},{32,0},{1,33},{33,1},{2,34},{34,2},{3,35},{35,3},{4,36},{36... | collective-permute-start | bytes 6291464 | tf_op jit(solution)/shard_map/ppermute | solution.py:398
  158.8 2.3 %finish.2 = (f32[2,768,384]{2,1,0:T(8,128)}, f32[2,3,384,384]{3,2,1,0:T(8,128)}, f32[2,384,768]{2,1,0:T(8,128)}) custom-call(s32[1]{0:T(128)} %bitcast.core.layer, bf16[8192,128]{1,0:T(8,128)(2,1)S(1)} %bitcast.22), custom_call_target="tpu_custom_call" | custom-call | tf_op jit(solution)/shard_map/finish/pallas_call | solution.py:265
  161.0 1.5 collective-permute-done.4.ref
  162.6 2.3 %finish.3 = (f32[2,768,384]{2,1,0:T(8,128)}, f32[2,3,384,384]{3,2,1,0:T(8,128)}, f32[2,384,768]{2,1,0:T(8,128)}) custom-call(s32[1]{0:T(128)S(6)} %sub.3.layer, bf16[8192,128]{1,0:T(8,128)(2,1)S(1)} %collective-permute-done.4.ref, f32[2,768,384]{2,1,0:T(8,128)} %get-tuple-element.83.rest_0_, ...), custom_call_target="tpu_custom_call", output_to_operand_aliasing={{0}: (2, {}), {1}: (3, {}), {2}: (4, {})} | custom-call | tf_op jit(solution)/shard_map/finish/pallas_call | solution.py:265
  (8 shorter events, 0.0 us)
Async XLA Ops:
  1.8 8.1 %copy-start.19 = (s32[768]{0:T(1024)S(1)}, s32[768]{0:T(1024)}, u32[]{:S(2)}) copy-start(s32[768]{0:T(1024)} %param.9) | copy-start | bytes 9220
  3.7 25.4 %collective-permute-start = (bf16[384,768]{1,0:T(8,128)(2,1)}, bf16[384,768]{1,0:T(8,128)(2,1)S(1)}, u32[]{:S(2)}, u32[]{:S(2)}) collective-permute-start(bf16[384,768]{1,0:T(8,128)(2,1)} %pad_maximum_fusion), channel_id=1, source_target_pairs={{0,1},{1,2},{2,3},{3,4},{4,5},{5,6},{6,7},{7,8},{8,9},{9,10},{10,1... | collective-permute-start | bytes 1769480 | tf_op jit(solution)/shard_map/ppermute | solution.py:384
  8.6 20.5 %collective-permute-start.1 = (bf16[384,768]{1,0:T(8,128)(2,1)}, bf16[384,768]{1,0:T(8,128)(2,1)S(1)}, u32[]{:S(2)}, u32[]{:S(2)}) collective-permute-start(bf16[384,768]{1,0:T(8,128)(2,1)} %pad_maximum_fusion.1), channel_id=1, source_target_pairs={{1,0},{2,1},{3,2},{4,3},{5,4},{6,5},{7,6},{8,7},{9,8},{10,9},{11,1... | collective-permute-start | bytes 1769480 | tf_op jit(solution)/shard_map/ppermute | solution.py:385
  10.0 1.4 copy-start
  11.4 1.3 copy-start.17
  12.6 1.3 copy-start.18
  13.9 4.6 %copy-start.1 = (bf16[1,1024,768]{2,1,0:T(8,128)(2,1)S(1)}, bf16[1,1024,768]{2,1,0:T(8,128)(2,1)}, u32[]{:S(2)}) copy-start(bf16[1,1024,768]{2,1,0:T(8,128)(2,1)} %param.7) | copy-start | bytes 4718596
  13.9 4.6 %copy-start.10 = (bf16[2,3,384,384]{3,2,1,0:T(8,128)(2,1)S(1)}, bf16[2,3,384,384]{3,2,1,0:T(8,128)(2,1)}, u32[]{:S(2)}) copy-start(bf16[2,3,384,384]{3,2,1,0:T(8,128)(2,1)} %weight.9) | copy-start | bytes 5308420
  13.9 4.6 %copy-start.16 = (s32[2]{0:T(128)S(1)}, s32[2]{0:T(128)}, u32[]{:S(2)}) copy-start(s32[2]{0:T(128)} %dil.9) | copy-start | bytes 28
  18.5 29.9 %copy-start.3 = (bf16[2,768,768]{2,1,0:T(8,128)(2,1)}, bf16[2,768,768]{2,1,0:T(8,128)(2,1)S(1)}, u32[]{:S(2)}) copy-start(bf16[2,768,768]{2,1,0:T(8,128)(2,1)S(1)} %get-tuple-element.49.upcat) | copy-start | bytes 7077892
  29.2 7.3 %copy-start.15 = (bf16[1,1024,768]{2,1,0:T(8,128)(2,1)S(1)}, bf16[1,1024,768]{2,1,0:T(8,128)(2,1)}, u32[]{:S(2)}) copy-start(bf16[1,1024,768]{2,1,0:T(8,128)(2,1)} %param.8) | copy-start | bytes 4718596
  36.5 11.9 %copy-start.5 = (bf16[1408,768]{1,0:T(8,128)(2,1)}, bf16[1408,768]{1,0:T(8,128)(2,1)S(1)}, u32[]{:S(2)}) copy-start(bf16[1408,768]{1,0:T(8,128)(2,1)S(1)} %get-tuple-element.61.stream) | copy-start | bytes 6488068
  44.3 4.1 %copy-start.8 = (bf16[1280,768]{1,0:T(8,128)(2,1)}, bf16[1280,768]{1,0:T(8,128)(2,1)S(1)}, u32[]{:S(2)}) copy-start(bf16[1280,768]{1,0:T(8,128)(2,1)S(1)} %get-tuple-element.78.act) | copy-start | bytes 5898244
  60.3 4.3 %copy-start.11 = (bf16[1152,768]{1,0:T(8,128)(2,1)}, bf16[1152,768]{1,0:T(8,128)(2,1)S(1)}, u32[]{:S(2)}) copy-start(bf16[1152,768]{1,0:T(8,128)(2,1)S(1)} %get-tuple-element.63.cot) | copy-start | bytes 5308420
  64.6 11.3 %collective-permute-start.2 = (bf16[5888,128]{1,0:T(8,128)(2,1)S(1)}, bf16[5888,128]{1,0:T(8,128)(2,1)S(1)}, u32[]{:S(2)}, u32[]{:S(2)}) collective-permute-start(bf16[5888,128]{1,0:T(8,128)(2,1)S(1)} %get-tuple-element.71), channel_id=1, source_target_pairs={{0,32},{32,0},{1,33},{33,1},{2,34},{34,2},{3,35},{35,3},{4,36},{36... | collective-permute-start | bytes 4521992 | tf_op jit(solution)/shard_map/ppermute | solution.py:398
  72.7 1.1 copy-start.13
  73.8 2.0 %collective-permute-start.3 = (bf16[2304,128]{1,0:T(8,128)(2,1)S(1)}, bf16[2304,128]{1,0:T(8,128)(2,1)S(1)}, u32[]{:S(2)}, u32[]{:S(2)}) collective-permute-start(bf16[2304,128]{1,0:T(8,128)(2,1)S(1)} %get-tuple-element.75), channel_id=1, source_target_pairs={{0,32},{32,0},{1,33},{33,1},{2,34},{34,2},{3,35},{35,3},{4,36},{36... | collective-permute-start | bytes 1769480 | tf_op jit(solution)/shard_map/ppermute | solution.py:398
  76.3 1.3 copy-start.7
  77.6 41.3 %all-to-all-start = ((bf16[64,128,128]{2,1,0:T(8,128)(2,1)}), bf16[64,128,128]{2,1,0:T(8,128)(2,1)}, u32[]{:S(2)}, u32[]{:S(2)}) async-start(bf16[64,128,128]{2,1,0:T(8,128)(2,1)} %bitcast.20), calls=%async_computation | async-start | bytes 4194304 | tf_op jit(solution)/shard_map/all_to_all | solution.py:394
  90.5 1.4 copy-start.2
  91.9 1.5 copy-start.12
  93.3 1.4 copy-start.14
  94.8 3.6 %copy-start.4 = (bf16[2,768,768]{2,1,0:T(8,128)(2,1)S(1)}, bf16[2,768,768]{2,1,0:T(8,128)(2,1)}, u32[]{:S(2)}) copy-start(bf16[2,768,768]{2,1,0:T(8,128)(2,1)} %copy-done.3) | copy-start | bytes 7077892
  94.8 3.6 %copy-start.6 = (bf16[1408,768]{1,0:T(8,128)(2,1)S(1)}, bf16[1408,768]{1,0:T(8,128)(2,1)}, u32[]{:S(2)}) copy-start(bf16[1408,768]{1,0:T(8,128)(2,1)} %copy-done.5) | copy-start | bytes 6488068
  94.8 3.6 %copy-start.9 = (bf16[1280,768]{1,0:T(8,128)(2,1)S(1)}, bf16[1280,768]{1,0:T(8,128)(2,1)}, u32[]{:S(2)}) copy-start(bf16[1280,768]{1,0:T(8,128)(2,1)} %copy-done.8) | copy-start | bytes 5898244
  156.6 6.0 %collective-permute-start.4 = (bf16[8192,128]{1,0:T(8,128)(2,1)S(1)}, bf16[8192,128]{1,0:T(8,128)(2,1)S(1)}, u32[]{:S(2)}, u32[]{:S(2)}) collective-permute-start(bf16[8192,128]{1,0:T(8,128)(2,1)S(1)} %bitcast.21), channel_id=1, source_target_pairs={{0,32},{32,0},{1,33},{33,1},{2,34},{34,2},{3,35},{35,3},{4,36},{36... | collective-permute-start | bytes 6291464 | tf_op jit(solution)/shard_map/ppermute | solution.py:398

commit v6 on v5

--- a/solution.py
+++ b/solution.py
@@ -225,7 +225,8 @@
         keep[...] = upper[...]
 
 
-def k_sums_top(factor, pairs, act, cot, tm, tc, tp, d_pre, rest):
+def k_sums_top(factor, pairs, act, cot, tm, tc, tp, d_pre, stream, upcat, rest, out):
+    out[...] = (own(stream, 3 * PAD).astype(F32) + mm(own(act, 2 * PAD), upcat[...])).astype(BF)
     taps = [own(tm, 2 * PAD), own(tc, 3 * PAD), own(tp, 2 * PAD)]
     weight_sums(factor, pairs, own(act, 2 * PAD), cot[...], taps, own(d_pre, 2 * PAD), rest)
 
@@ -251,30 +252,16 @@
     out[...] = jnp.broadcast_to(share[None], out.shape)
 
 
-def k_finish(layer, ref, *rest):
-    down, kern, up = rest[-3:]
-    up[0] = take(ref, 0, B, C)
-    for k in range(3):
-        kern[0, k] = take(ref, UP + k * 3 * B, B, B)
-    down[0] = take(ref, REST, C, B)
-
-
-def write_layer(layer, total, outs):
-    dims = ((C, B), (3, B, B), (B, C))
-    blocks = [pl.BlockSpec((1,) + d, lambda i, n, d=d: (n[0],) + (0,) * len(d)) for d in dims]
-    return pl.pallas_call(
-        k_finish,
-        grid_spec=pltpu.PrefetchScalarGridSpec(
-            num_scalar_prefetch=1,
-            grid=(1,),
-            in_specs=[pl.BlockSpec(total.shape, lambda i, n: (0, 0))] + [pl.BlockSpec(memory_space=pl.ANY)] * len(outs),
-            out_specs=blocks,
-        ),
-        out_shape=[shape(2, *d, kind=F32) for d in dims],
-        input_output_aliases={2 + i: i for i in range(len(outs))},
-        compiler_params=pltpu.CompilerParams(vmem_limit_bytes=20 * 1024 * 1024),
-        name="finish",
-    )(layer, total, *outs)
+def k_finish(core, own, other, down, kern, up):
+    layer = pl.program_id(0)
+    for mine, ref in ((True, own), (False, other)):
+
+        @pl.when((core[0] == layer) == mine)
+        def _():
+            up[0] = take(ref, 0, B, C)
+            for k in range(3):
+                kern[0, k] = take(ref, UP + k * 3 * B, B, B)
+            down[0] = take(ref, REST, C, B)
 
 
 def norm_back(v, d_norm):
@@ -320,13 +307,6 @@
         sort_out(core, down, upper, send, keep)
 
 
-def k_out(act, stream, upcat, out):
-    step = pl.program_id(0) * TILE
-    rows = pl.ds(pl.multiple_of(step + 2 * PAD, 16), TILE)
-    base = pl.ds(pl.multiple_of(step + 3 * PAD, 16), TILE)
-    out[...] = (stream[base, :].astype(F32) + mm(act[rows, :], upcat[...])).astype(BF)
-
-
 def k_input(d_inner, x, cot, dcat, out):
     rows = pl.ds(pl.multiple_of(pl.program_id(0) * TILE + PAD, 16), TILE)
     out[...] = (cot[rows, :].astype(F32) + norm_back(x[...], mm_nt(d_inner[...], dcat[...]))).astype(BF)
@@ -348,7 +328,7 @@
     return jax.ShapeDtypeStruct(dims, kind)
 
 
-def call(body, steps, ins, outs, scratch, flops, name, limit=20, aliases=None):
+def call(body, steps, ins, outs, scratch, flops, name, limit=16, aliases=None):
     size = lambda s: 2 * math.prod(s.shape)
     return pl.pallas_call(
         body,
@@ -438,11 +418,11 @@
     joined = (whole(REST + DOWN, LANES), shape(REST + DOWN, LANES))
     shares = (whole(*SHARES), shape(*SHARES))
     wide_top, wide_mid, wide_back = whole(TOP_ROWS, C), whole(MID_ROWS, C), whole(BACK_ROWS, C)
-    (rest1,) = call(
+    rest1, out = call(
         functools.partial(k_sums_top, factor), 1,
-        [whole(1, C), wide_top, resident, wide_top, wide_mid, wide_top, wide_top],
-        [sums], [], 3 * UNIT, "sums_top",
-    )(pairs, act1, cot, tm1, inner1, tp1, d_pre1)
+        [whole(1, C), wide_top, resident, wide_top, wide_mid, wide_top, wide_top, wide_mid, square_of[1]],
+        [sums, (resident, shape(ROWS, C))], [], 3 * UNIT, "sums_top",
+    )(pairs, act1, cot, tm1, inner1, tp1, d_pre1, stream1, upcat)
     back = (tile(BACK_TILE), shape(BACK_ROWS, C))
     grad, d_pre0, down1 = call(
         functools.partial(k_back, factor), 3,
@@ -467,20 +447,19 @@
     (parts,) = call(
         k_join, 1, [sums[0], sums[0], downs[0], downs[0]], [joined], [], 0, "join",
     )(keep_a, other_core(send_a), keep_b, other_core(send_b))
-    parts, act1, d_inner0 = lax.optimization_barrier((parts, act1, d_inner0))
-    (out,) = call(
-        k_out, STEPS, [wide_top, wide_mid, square_of[1]], [FULL], [], UNIT, "out",
-    )(act1, stream1, upcat)
     (input_grad,) = call(
         k_input, STEPS, [tile(), tile(), wide_back, square_of[0]], [FULL], [], UNIT, "input",
     )(d_inner0, x, grad, dcat)
     parts = exchange(parts.reshape(SHARES))
-    parts, out, input_grad = lax.optimization_barrier((parts, out, input_grad))
     (shared,) = call(k_share, 1, [shares[0]], [shares], [], 0, "share")(parts)
     mine = exchange(shared).reshape(REST + DOWN, LANES)
-    other = other_core(mine)
-    grads = write_layer(core, mine, ())
-    grads = write_layer(1 - core, other, grads)
+    layered = lambda *dims: (
+        pl.BlockSpec((1,) + dims, lambda i: (i,) + (0,) * len(dims)), shape(2, *dims, kind=F32)
+    )
+    grads = call(
+        k_finish, 2, [scalar()] + [joined[0]] * 2,
+        [layered(C, B), layered(3, B, B), layered(B, C)], [], 0, "finish",
+    )(core, mine, other_core(mine))
     return (out[None], input_grad[None], *grads)
 
 

time: 166 us -> 166 us (level)
  blocking collectives: 35.5 us -> 75.8 us
  waiting for transfers between devices: 21.2 us -> 2.12 us
  starting transfers between devices: 21.4 us -> 9.49 us
  local copies, waits for them, and re-layouts: 13 us -> 4.9 us
    all_to_all x1 -> x2, blocking collectives: 35.5 us -> 75.8 us  [exchange(): return lax.all_to_all(parts, CHIPS, 0, 0, tiled=True)]
    all_to_all x1 -> x0, waiting for transfers between devices: 17.7 us -> none  [exchange(): return lax.all_to_all(parts, CHIPS, 0, 0, tiled=True)]
    all_to_all x1 -> x0, starting transfers between devices: 12.8 us -> none  [exchange(): return lax.all_to_all(parts, CHIPS, 0, 0, tiled=True)]
    unnamed x40 -> x14, local copies, waits for them, and re-layouts: 10.7 us -> 2.56 us
    pallas_call x3 -> x1, Pallas kernels: 7.46 us -> 3.58 us  [local(): call(k_finish, 2, [scalar()] + [joined[0]] * 2, [layered(C, B), layered(3...]
  transfers between devices with their start and end apart: 6 -> 5, of which waited for: 3 -> 2; matrix products, arithmetic and copies ran while one was open for 1% -> 1% of each run, Pallas kernels for 19% -> 16%
where the time goes in v6:
time: 166 us; the launch traced here: 165 us
  blocking collectives  75.8 us (46%)
  Pallas kernels  70.4 us (42%)
  starting transfers between devices  9.49 us (6%)
  local copies, waits for them, and re-layouts  4.9 us (3%)
  waiting for transfers between devices  2.12 us (1%)
  other arithmetic  1.71 us (1%)
    all_to_all x2, blocking collectives, exchange(): return lax.all_to_all(parts, CHIPS, 0, 0, tiled=True)  75.8 us
    pallas_call x1, Pallas kernels, local(): call(functools.partial(k_back, factor), 3, [scalar(), scalar(), whole(1,...  12.8 us
    pallas_call x1, Pallas kernels, local(): call(k_within, 7, [scalar(), resident, resident, taps_w[0], square_of[0],...  10.8 us
    pallas_call x1, Pallas kernels, local(): call(k_top, 4, [scalar(), whole(MID_ROWS, C), resident, halo, halo, taps_...  8.7 us
    pallas_call x1, Pallas kernels, local(): call(k_around, 4, [scalar(), scalar(), resident, resident, halo, halo, sq...  8.23 us
    pallas_call x1, Pallas kernels, local(): call(functools.partial(k_last, factor), STEPS, [scalar(), scalar(), whole...  7.09 us
    pallas_call x1, Pallas kernels, local(): call(functools.partial(k_sums_top, factor), 1, [whole(1, C), wide_top, re...  5.7 us
    ppermute x1, starting transfers between devices, edges(): top = lax.ppermute(last, SEQ, [(i, i + 1) for i in range(BLOCKS - 1)])  4.85 us
  transfers between devices with their start and end apart: 5, of which 2 were waited for; matrix products, arithmetic and copies ran while one was open for 1% of the time, Pallas kernels for 16%

profile of v6, /device:TPU:1, one launch (start us, length us, event | category | flops | bytes accessed | tf_op | source)
XLA Modules:
  0.0 165.3 jit_solution(5421138897333582078)
XLA Ops:
  0.6 1.1 slice_bitcast_fusion.2
  1.7 0.0 copy-start.6
  1.7 0.0 copy-start
  1.7 1.3 slice_bitcast_fusion
  3.0 0.9 pad_maximum_fusion
  3.9 4.8 %collective-permute-start = (bf16[384,768]{1,0:T(8,128)(2,1)}, bf16[384,768]{1,0:T(8,128)(2,1)}, u32[]{:S(2)}, u32[]{:S(2)}) collective-permute-start(bf16[384,768]{1,0:T(8,128)(2,1)} %pad_maximum_fusion), channel_id=1, source_target_pairs={{0,1},{1,2},{2,3},{3,4},{4,5},{5,6},{6,7},{7,8},{8,9},{9,10},{10,1... | collective-permute-start | bytes 1769480 | tf_op jit(solution)/shard_map/ppermute | solution.py:364
  8.7 0.9 pad_maximum_fusion.1
  9.6 1.3 collective-permute-start.1
  10.8 0.0 copy-done.6
  10.9 0.0 copy-done
  10.9 0.0 copy-start.4
  10.9 1.3 copy-done.4
  12.2 0.0 copy-start.5
  12.2 1.3 copy-done.5
  13.4 0.0 copy-start.2
  13.4 0.0 copy-start.3
  13.4 4.7 %enter.1 = (bf16[2,768,768]{2,1,0:T(8,128)(2,1)S(1)}, bf16[2,768,768]{2,1,0:T(8,128)(2,1)S(1)}, bf16[1024,768]{1,0:T(8,128)(2,1)S(1)}, bf16[1024,768]{1,0:T(8,128)(2,1)S(1)}) custom-call(s32[1,768]{1,0:T(1,128)S(1)} %reshape.29.pairs, bf16[2,768,384]{2,1,0:T(8,128)(2,1)S(1)} %copy-done.4, bf16[2,384,768]{2,1,0:T(8,128)(2,1)S(1)} %copy-done.5, ...), custom_call_target="tpu_custom_call" | custom-call | flops 3623878656 | bytes 15728640 | tf_op jit(solution)/shard_map/enter/pallas_call | solution.py:394
  18.1 0.0 copy-done.2
  18.1 0.0 copy-done.3
  18.2 10.8 %within.1 = (bf16[1408,768]{1,0:T(8,128)(2,1)S(1)}, bf16[1408,768]{1,0:T(8,128)(2,1)S(1)}, bf16[1408,768]{1,0:T(8,128)(2,1)S(1)}, bf16[1408,768]{1,0:T(8,128)(2,...) custom-call(s32[2]{0:T(128)S(1)} %copy-done.3, ...), custom_call_target="tpu_custom_call" | custom-call | flops 3623878656 | bytes 30277632 | tf_op jit(solution)/shard_map/within/pallas_call | solution.py:399
  28.9 0.0 collective-permute-done.top
  28.9 0.0 collective-permute-done.1.bot
  28.9 0.0 copy-start.1
  29.0 8.2 %around.1 = (bf16[1408,768]{1,0:T(8,128)(2,1)S(1)}, bf16[1408,768]{1,0:T(8,128)(2,1)S(1)}, bf16[1408,768]{1,0:T(8,128)(2,1)S(1)}, bf16[1408,768]{1,0:T(8,128)(2,...) custom-call(s32[2]{0:T(128)S(1)} %copy-done.3, ...), custom_call_target="tpu_custom_call", output_to_operand_aliasing={{0}: (10, {}), {1}: (11, {}), {2}: (12, {}), {3}: (13, {}),... | custom-call | flops 3623878656 | bytes 30277632 | tf_op jit(solution)/shard_map/around/pallas_call | solution.py:403
  37.2 0.0 copy-done.1
  37.2 8.7 %top.1 = (bf16[1280,768]{1,0:T(8,128)(2,1)S(1)}, bf16[1280,768]{1,0:T(8,128)(2,1)S(1)}, bf16[1280,768]{1,0:T(8,128)(2,1)S(1)}, bf16[1280,768]{1,0:T(8,128)(2,1)S(1)}) custom-call(s32[2]{0:T(128)S(1)} %copy-done.3, bf16[1408,768]{1,0:T(8,128)(2,1)S(1)} %get-tuple-element.50.mid.tc, bf16[1024,768]{1,0:T(8,128)(2,1)S(1)} %bitcast.23, ...), custom_call_target="tpu_custom_call" | custom-call | flops 3623878656 | bytes 15728640 | tf_op jit(solution)/shard_map/top/pallas_call | solution.py:411
  45.9 5.7 %sums_top.1 = (bf16[5888,128]{1,0:T(8,128)(2,1)S(1)}, bf16[1024,768]{1,0:T(8,128)(2,1)}) custom-call(s32[1,768]{1,0:T(1,128)S(1)} %reshape.29.pairs, bf16[1280,768]{1,0:T(8,128)(2,1)S(1)} %get-tuple-element.51.act, bf16[1024,768]{1,0:T(8,128)(2,1)S(1)} %bitcast.24, bf16[1280,768]{1,0:T(8,128)(2,1)S(1)} %get-tuple-element.52.tm, ...), custom_call_target="tpu_custom_call" | custom-call | flops 3623878656 | bytes 6160384 | tf_op jit(solution)/shard_map/sums_top/pallas_call | solution.py:421
  51.6 12.8 %back.1 = (bf16[1152,768]{1,0:T(8,128)(2,1)S(1)}, bf16[1152,768]{1,0:T(8,128)(2,1)S(1)}, bf16[2304,128]{1,0:T(8,128)(2,1)S(1)}) custom-call(s32[2]{0:T(128)S(1)} %copy-done.3, s32[1]{0:T(128)} %bitcast.block, s32[1,768]{1,0:T(1,128)S(1)} %reshape.29.pairs, bf16[1280,768]{1,0:T(8,128)(2,1)S(1)} %get-tuple-element.54.d_pre.mid, ...), custom_call_target="tpu_custom_call" | custom-call | flops 6039797760 | bytes 8257536 | tf_op jit(solution)/shard_map/back/pallas_call | solution.py:427
  64.4 4.3 %sums.1 = (bf16[5888,128]{1,0:T(8,128)(2,1)S(1)}, bf16[5888,128]{1,0:T(8,128)(2,1)S(1)}) custom-call(s32[1]{0:T(128)} %bitcast.8.core, s32[1,768]{1,0:T(1,128)S(1)} %reshape.29.pairs, bf16[1408,768]{1,0:T(8,128)(2,1)S(1)} %get-tuple-element.64.act, bf16[1152,768]{1,0:T(8,128)(2,1)S(1)} %get-tuple-element.63.cot, bf16[1408,768]{1,0:T(8,128)(2,1)S(1)} %get-tuple-element.65.tm, ...), custom_call_target="tpu_custom_call" | custom-call | flops 3623878656 | bytes 6029312 | tf_op jit(solution)/shard_map/sums/pallas_call | solution.py:435
  68.7 1.0 collective-permute-start.2
  69.7 7.1 %last.1 = (bf16[2304,128]{1,0:T(8,128)(2,1)S(1)}, bf16[2304,128]{1,0:T(8,128)(2,1)S(1)}, bf16[1024,768]{1,0:T(8,128)(2,1)S(1)}) custom-call(s32[1]{0:T(128)} %bitcast.8.core, s32[2]{0:T(128)S(1)} %copy-done.3, s32[1,768]{1,0:T(1,128)S(1)} %reshape.29.pairs, bf16[1152,768]{1,0:T(8,128)(2,1)S(1)} %get-tuple-element.59.mid.d_pre, ...), custom_call_target="tpu_custom_call" | custom-call | flops 3623878656 | bytes 5505024 | tf_op jit(solution)/shard_map/last/pallas_call | solution.py:440
  76.8 0.1 collective-permute-start.3
  76.9 2.0 %collective-permute-done.3.got_b = bf16[2304,128]{1,0:T(8,128)(2,1)S(1)} collective-permute-done((bf16[2304,128]{1,0:T(8,128)(2,1)S(1)}, bf16[2304,128]{1,0:T(8,128)(2,1)S(1)}, u32[]{:S(2)}, u32[]{:S(2)}) %collective-permute-start.3) | collective-permute-done | bytes 589856 | tf_op jit(solution)/shard_map/ppermute | solution.py:378
  78.9 0.0 collective-permute-done.2.got_a
  78.9 0.5 join.1
  79.4 40.2 %all_to_all.10.parts = bf16[64,128,128]{2,1,0:T(8,128)(2,1)S(1)} all-to-all(bf16[64,128,128]{2,1,0:T(8,128)(2,1)S(1)} %bitcast.20), channel_id=1, replica_groups=mesh['xh'=2,'core'=2,'z'=4,'xl'=2,'y'=4] {'xh','z','xl','y'}, dimensions={0} | all-to-all | bytes 4194304 | tf_op jit(solution)/shard_map/all_to_all | solution.py:374
  119.6 0.5 share.1
  120.1 35.5 %all_to_all.11 = bf16[64,128,128]{2,1,0:T(8,128)(2,1)S(1)} all-to-all(bf16[64,128,128]{2,1,0:T(8,128)(2,1)S(1)} %share.1), channel_id=1, replica_groups=mesh['xh'=2,'core'=2,'z'=4,'xl'=2,'y'=4] {'xh','z','xl','y'}, dimensions={0} | all-to-all | bytes 4194304 | tf_op jit(solution)/shard_map/all_to_all | solution.py:374
  155.7 2.2 %collective-permute-start.4 = (bf16[8192,128]{1,0:T(8,128)(2,1)S(1)}, bf16[8192,128]{1,0:T(8,128)(2,1)S(1)}, u32[]{:S(2)}, u32[]{:S(2)}) collective-permute-start(bf16[8192,128]{1,0:T(8,128)(2,1)S(1)} %bitcast.21), channel_id=1, source_target_pairs={{0,32},{32,0},{1,33},{33,1},{2,34},{34,2},{3,35},{35,3},{4,36},{36... | collective-permute-start | bytes 6291464 | tf_op jit(solution)/shard_map/ppermute | solution.py:378
  157.9 3.7 %input.1 = bf16[1024,768]{1,0:T(8,128)(2,1)} custom-call(bf16[1024,768]{1,0:T(8,128)(2,1)S(1)} %get-tuple-element.62.d_inner, bf16[1024,768]{1,0:T(8,128)(2,1)S(1)} %bitcast.19, bf16[1152,768]{1,0:T(8,128)(2,1)S(1)} %get-tuple-element.63.cot, bf16[2,768,768]{2,1,0:T(8,128)(2,1)S(1)} %get-tuple-element.41.dcat.dcat0), custom_call_target="tpu_custom_call" | custom-call | flops 1207959552 | bytes 3145728 | tf_op jit(solution)/shard_map/input/pallas_call | solution.py:450
  161.6 0.1 collective-permute-done.4.other
  161.7 3.6 %finish.1 = (f32[2,768,384]{2,1,0:T(8,128)}, f32[2,3,384,384]{3,2,1,0:T(8,128)}, f32[2,384,768]{2,1,0:T(8,128)}) custom-call(s32[1]{0:T(128)} %bitcast.8.core, bf16[8192,128]{1,0:T(8,128)(2,1)S(1)} %bitcast.22, bf16[8192,128]{1,0:T(8,128)(2,1)S(1)} %collective-permute-done.4.other), custom_call_target="tpu_custom_call" | custom-call | bytes 8257536 | tf_op jit(solution)/shard_map/finish/pallas_call | solution.py:459
  (1 shorter events, 0.0 us)
Async XLA Ops:
  1.7 9.2 %copy-start.6 = (s32[768]{0:T(1024)S(1)}, s32[768]{0:T(1024)}, u32[]{:S(2)}) copy-start(s32[768]{0:T(1024)} %param.9) | copy-start | bytes 9220
  1.7 9.2 %copy-start = (bf16[1,1024,768]{2,1,0:T(8,128)(2,1)S(1)}, bf16[1,1024,768]{2,1,0:T(8,128)(2,1)}, u32[]{:S(2)}) copy-start(bf16[1,1024,768]{2,1,0:T(8,128)(2,1)} %param.7) | copy-start | bytes 4718596
  3.9 25.1 %collective-permute-start = (bf16[384,768]{1,0:T(8,128)(2,1)}, bf16[384,768]{1,0:T(8,128)(2,1)}, u32[]{:S(2)}, u32[]{:S(2)}) collective-permute-start(bf16[384,768]{1,0:T(8,128)(2,1)} %pad_maximum_fusion), channel_id=1, source_target_pairs={{0,1},{1,2},{2,3},{3,4},{4,5},{5,6},{6,7},{7,8},{8,9},{9,10},{10,1... | collective-permute-start | bytes 1769480 | tf_op jit(solution)/shard_map/ppermute | solution.py:364
  9.6 19.4 %collective-permute-start.1 = (bf16[384,768]{1,0:T(8,128)(2,1)}, bf16[384,768]{1,0:T(8,128)(2,1)}, u32[]{:S(2)}, u32[]{:S(2)}) collective-permute-start(bf16[384,768]{1,0:T(8,128)(2,1)} %pad_maximum_fusion.1), channel_id=1, source_target_pairs={{1,0},{2,1},{3,2},{4,3},{5,4},{6,5},{7,6},{8,7},{9,8},{10,9},{11,1... | collective-permute-start | bytes 1769480 | tf_op jit(solution)/shard_map/ppermute | solution.py:365
  10.9 1.3 copy-start.4
  12.2 1.3 copy-start.5
  13.4 4.7 %copy-start.2 = (bf16[2,3,384,384]{3,2,1,0:T(8,128)(2,1)S(1)}, bf16[2,3,384,384]{3,2,1,0:T(8,128)(2,1)}, u32[]{:S(2)}) copy-start(bf16[2,3,384,384]{3,2,1,0:T(8,128)(2,1)} %weight.9) | copy-start | bytes 5308420
  13.4 4.7 %copy-start.3 = (s32[2]{0:T(128)S(1)}, s32[2]{0:T(128)}, u32[]{:S(2)}) copy-start(s32[2]{0:T(128)} %dil.9) | copy-start | bytes 28
  28.9 8.2 %copy-start.1 = (bf16[1,1024,768]{2,1,0:T(8,128)(2,1)S(1)}, bf16[1,1024,768]{2,1,0:T(8,128)(2,1)}, u32[]{:S(2)}) copy-start(bf16[1,1024,768]{2,1,0:T(8,128)(2,1)} %param.8) | copy-start | bytes 4718596
  68.7 10.2 %collective-permute-start.2 = (bf16[5888,128]{1,0:T(8,128)(2,1)S(1)}, bf16[5888,128]{1,0:T(8,128)(2,1)S(1)}, u32[]{:S(2)}, u32[]{:S(2)}) collective-permute-start(bf16[5888,128]{1,0:T(8,128)(2,1)S(1)} %get-tuple-element.69), channel_id=1, source_target_pairs={{0,32},{32,0},{1,33},{33,1},{2,34},{34,2},{3,35},{35,3},{4,36},{36... | collective-permute-start | bytes 4521992 | tf_op jit(solution)/shard_map/ppermute | solution.py:378
  76.8 2.1 %collective-permute-start.3 = (bf16[2304,128]{1,0:T(8,128)(2,1)S(1)}, bf16[2304,128]{1,0:T(8,128)(2,1)S(1)}, u32[]{:S(2)}, u32[]{:S(2)}) collective-permute-start(bf16[2304,128]{1,0:T(8,128)(2,1)S(1)} %get-tuple-element.71), channel_id=1, source_target_pairs={{0,32},{32,0},{1,33},{33,1},{2,34},{34,2},{3,35},{35,3},{4,36},{36... | collective-permute-start | bytes 1769480 | tf_op jit(solution)/shard_map/ppermute | solution.py:378
  155.7 6.0 %collective-permute-start.4 = (bf16[8192,128]{1,0:T(8,128)(2,1)S(1)}, bf16[8192,128]{1,0:T(8,128)(2,1)S(1)}, u32[]{:S(2)}, u32[]{:S(2)}) collective-permute-start(bf16[8192,128]{1,0:T(8,128)(2,1)S(1)} %bitcast.21), channel_id=1, source_target_pairs={{0,32},{32,0},{1,33},{33,1},{2,34},{34,2},{3,35},{35,3},{4,36},{36... | collective-permute-start | bytes 6291464 | tf_op jit(solution)/shard_map/ppermute | solution.py:378

commit v7 on v4

--- a/solution.py
+++ b/solution.py
@@ -12,11 +12,11 @@
 B = 384
 PAD = 64
 ROWS = 1024
-TILE = 256
+TILE = 512
 STEPS = ROWS // TILE
 BLOCKS = 32
 MID_ROWS, TOP_ROWS, BACK_ROWS = ROWS + 6 * PAD, ROWS + 4 * PAD, ROWS + 2 * PAD
-MID_TILE, TOP_TILE, BACK_TILE = MID_ROWS // 4, TOP_ROWS // 4, BACK_ROWS // 3
+MID_TILE, TOP_TILE, BACK_TILE = MID_ROWS // 4, TOP_ROWS // 2, BACK_ROWS // 2
 EPS = 1e-06
 ROOT = math.sqrt(2.0 / math.pi)
 CUBE = 0.044715
@@ -397,7 +397,7 @@
     )(dilations, block, inner0, x, top, bot, dcat, conv_weight, upcat, dcat)
     upper = (tile(TOP_TILE), shape(TOP_ROWS, C))
     act1, d_pre1, tm1, tp1 = call(
-        k_top, 4, [scalar(), whole(MID_ROWS, C), resident, c_halo, c_halo, taps_w[1], square_of[1]],
+        k_top, 2, [scalar(), whole(MID_ROWS, C), resident, c_halo, c_halo, taps_w[1], square_of[1]],
         [upper] * 4, [store(TOP_ROWS)], 3 * UNIT, "top",
     )(dilations, inner1, cot, ctop, cbot, conv_weight, upcat)
     core = lax.axis_index("core").reshape(1)
@@ -413,7 +413,7 @@
     )(pairs, act1, cot, tm1, inner1, tp1, d_pre1)
     back = (tile(BACK_TILE), shape(BACK_ROWS, C))
     grad, d_pre0, down1 = call(
-        functools.partial(k_back, factor), 3,
+        functools.partial(k_back, factor), 2,
         [scalar(), scalar(), whole(1, C), wide_top, taps_w[1], wide_mid, wide_mid, resident, c_halo, c_halo,
          square_of[1], square_of[0], wide_mid],
         [back, back, downs],

time: 165 us -> 164 us (level)
  Pallas kernels: 66.6 us -> 64.2 us
  transfers between devices with their start and end apart: 8 -> 8, of which waited for: 3 -> 3; matrix products, arithmetic and copies ran while one was open for 1% -> 1% of each run, Pallas kernels for 21% -> 20%
where the time goes in v7:
time: 164 us; the launch traced here: 163 us
  Pallas kernels  64.2 us (39%)
  blocking collectives  35.5 us (22%)
  starting transfers between devices  30.1 us (18%)
  waiting for transfers between devices  20.5 us (12%)
  local copies, waits for them, and re-layouts  11.8 us (7%)
    all_to_all x1, blocking collectives, exchange(): return lax.all_to_all(parts, CHIPS, 0, 0, tiled=True)  35.5 us
    all_to_all x1, waiting for transfers between devices, exchange(): return lax.all_to_all(parts, CHIPS, 0, 0, tiled=True)  17 us
    all_to_all x1, starting transfers between devices, exchange(): return lax.all_to_all(parts, CHIPS, 0, 0, tiled=True)  15.6 us
    pallas_call x1, Pallas kernels, local(): call(k_middle, 4, [scalar(), scalar(), resident, resident, halo, halo, sq...  13.3 us
    pallas_call x1, Pallas kernels, local(): call(functools.partial(k_back, factor), 2, [scalar(), scalar(), whole(1,...  11.7 us
    unnamed x40, local copies, waits for them, and re-layouts  8.74 us
    ppermute x2, starting transfers between devices, edges(): lax.ppermute(cells[ROWS - rows:], SEQ, [(i, i + 1) for i in range(BLOCKS...  8.04 us
    pallas_call x1, Pallas kernels, local(): call(k_top, 2, [scalar(), whole(MID_ROWS, C), resident, c_halo, c_halo, t...  7.62 us
  transfers between devices with their start and end apart: 8, of which 3 were waited for; matrix products, arithmetic and copies ran while one was open for 1% of the time, Pallas kernels for 20%

profile of v7, /device:TPU:1, one launch (start us, length us, event | category | flops | bytes accessed | tf_op | source)
XLA Modules:
  0.0 163.1 jit_solution(2960206254551755988)
XLA Ops:
  0.6 0.0 copy-start
  0.6 0.0 copy-start.19
  0.7 1.3 slice_bitcast_fusion
  1.9 4.1 %collective-permute-start = (bf16[256,768]{1,0:T(8,128)(2,1)S(1)}, bf16[256,768]{1,0:T(8,128)(2,1)S(1)}, u32[]{:S(2)}, u32[]{:S(2)}) collective-permute-start(bf16[256,768]{1,0:T(8,128)(2,1)S(1)} %get-tuple-element.78), channel_id=1, source_target_pairs={{0,1},{1,2},{2,3},{3,4},{4,5},{5,6},{6,7},{7,8},{8,9},{9,10},{10,1... | collective-permute-start | bytes 1179656 | tf_op jit(solution)/shard_map/ppermute | solution.py:357
  6.0 1.3 collective-permute-start.1
  7.3 1.8 %slice_bitcast_fusion.2 = (bf16[128,768]{1,0:T(8,128)(2,1)}, bf16[128,768]{1,0:T(8,128)(2,1)}) fusion(bf16[1,1024,768]{2,1,0:T(8,128)(2,1)} %param.8), kind=kLoop, calls=%fused_computation.2 | loop fusion | bytes 786432 | tf_op jit(solution)/shard_map/slice | solution.py:358
  9.1 4.0 %collective-permute-start.2 = (bf16[128,768]{1,0:T(8,128)(2,1)}, bf16[128,768]{1,0:T(8,128)(2,1)S(1)}, u32[]{:S(2)}, u32[]{:S(2)}) collective-permute-start(bf16[128,768]{1,0:T(8,128)(2,1)} %get-tuple-element.76), channel_id=1, source_target_pairs={{0,1},{1,2},{2,3},{3,4},{4,5},{5,6},{6,7},{7,8},{8,9},{9,10},{10,1... | collective-permute-start | bytes 589832 | tf_op jit(solution)/shard_map/ppermute | solution.py:357
  13.1 1.3 collective-permute-start.3
  14.4 0.0 copy-done.19
  14.4 0.0 copy-done
  14.4 0.0 copy-start.16
  14.4 1.3 copy-done.16
  15.7 0.0 copy-start.17
  15.7 1.3 copy-done.17
  17.0 4.2 %enter.1 = (bf16[2,768,768]{2,1,0:T(8,128)(2,1)S(1)}, bf16[2,768,768]{2,1,0:T(8,128)(2,1)S(1)}, bf16[1024,768]{1,0:T(8,128)(2,1)S(1)}, bf16[1024,768]{1,0:T(8,128)(2,1)S(1)}) custom-call(s32[1,768]{1,0:T(1,128)S(1)} %reshape.30.pairs, bf16[2,768,384]{2,1,0:T(8,128)(2,1)S(1)} %copy-done.16, bf16[2,384,768]{2,1,0:T(8,128)(2,1)S(1)} %copy-done.17, ...), custom_call_target="tpu_custom_call" | custom-call | flops 3623878656 | bytes 15728640 | tf_op jit(solution)/shard_map/enter/pallas_call | solution.py:388
  21.2 0.0 copy-start.2
  21.2 0.0 copy-start.4
  21.3 0.0 collective-permute-done.top
  21.3 0.0 collective-permute-done.1.bot
  21.3 0.0 copy-done.15
  21.3 0.0 copy-done.18
  21.3 0.0 copy-start.14
  21.3 13.3 %middle.1 = (bf16[1408,768]{1,0:T(8,128)(2,1)S(1)}, bf16[1408,768]{1,0:T(8,128)(2,1)S(1)}, bf16[1408,768]{1,0:T(8,128)(2,1)S(1)}, bf16[1408,768]{1,0:T(8,128)(2,...) custom-call(s32[2]{0:T(128)S(1)} %copy-done.18, ...), custom_call_target="tpu_custom_call" | custom-call | flops 7247757312 | bytes 30277632 | tf_op jit(solution)/shard_map/middle/pallas_call | solution.py:393
  34.6 0.0 copy-start.6
  34.6 0.0 collective-permute-done.2.top
  34.6 0.0 collective-permute-done.3.bot
  34.6 0.0 copy-done.14
  34.6 7.6 %top.1 = (bf16[1280,768]{1,0:T(8,128)(2,1)S(1)}, bf16[1280,768]{1,0:T(8,128)(2,1)S(1)}, bf16[1280,768]{1,0:T(8,128)(2,1)S(1)}, bf16[1280,768]{1,0:T(8,128)(2,1)S(1)}) custom-call(s32[2]{0:T(128)S(1)} %copy-done.18, bf16[1408,768]{1,0:T(8,128)(2,1)S(1)} %get-tuple-element.44.mid.tc, bf16[1024,768]{1,0:T(8,128)(2,1)S(1)} %bitcast.21, ...), custom_call_target="tpu_custom_call" | custom-call | flops 3623878656 | bytes 15728640 | tf_op jit(solution)/shard_map/top/pallas_call | solution.py:399
  42.3 0.0 copy-start.8
  42.3 4.0 %sums_top.1.upper = bf16[5888,128]{1,0:T(8,128)(2,1)S(1)} custom-call(s32[1,768]{1,0:T(1,128)S(1)} %reshape.30.pairs, bf16[1280,768]{1,0:T(8,128)(2,1)S(1)} %get-tuple-element.64.act, bf16[1024,768]{1,0:T(8,128)(2,1)S(1)} %bitcast.22, bf16[1280,768]{1,0:T(8,128)(2,1)S(1)} %get-tuple-element.54.tm, bf16[1408,768]{1,0:T(8,128)(2,1)S(1)} %get-tuple-element.44.mid.tc, ...), custom_call_target="tpu_custom_call" | custom-call | flops 3623878656 | bytes 3014656 | tf_op jit(solution)/shard_map/sums_top/pallas_call | solution.py:409
  46.3 0.0 copy-done.8
  46.3 0.0 copy-done.2
  46.4 0.0 copy-done.4
  46.4 0.0 copy-done.6
  46.4 11.7 %back.1 = (bf16[1152,768]{1,0:T(8,128)(2,1)S(1)}, bf16[1152,768]{1,0:T(8,128)(2,1)S(1)}, bf16[2304,128]{1,0:T(8,128)(2,1)S(1)}) custom-call(s32[2]{0:T(128)S(1)} %copy-done.18, s32[1]{0:T(128)} %bitcast.1.block, s32[1,768]{1,0:T(1,128)S(1)} %reshape.30.pairs, bf16[1280,768]{1,0:T(8,128)(2,1)S(1)} %get-tuple-element.45.mid.d_pre, ...), custom_call_target="tpu_custom_call" | custom-call | flops 6039797760 | bytes 8257536 | tf_op jit(solution)/shard_map/back/pallas_call | solution.py:415
  58.1 0.0 copy-start.10
  58.1 4.3 %sums.1 = (bf16[5888,128]{1,0:T(8,128)(2,1)S(1)}, bf16[5888,128]{1,0:T(8,128)(2,1)S(1)}) custom-call(s32[1]{0:T(128)} %bitcast.core.layer, s32[1,768]{1,0:T(1,128)S(1)} %reshape.30.pairs, bf16[1408,768]{1,0:T(8,128)(2,1)S(1)} %get-tuple-element.43.act, bf16[1152,768]{1,0:T(8,128)(2,1)S(1)} %get-tuple-element.49.cot, ...), custom_call_target="tpu_custom_call" | custom-call | flops 3623878656 | bytes 6029312 | tf_op jit(solution)/shard_map/sums/pallas_call | solution.py:423
  62.3 0.0 copy-done.10
  62.4 1.6 collective-permute-start.4
  63.9 6.7 %last.1 = (bf16[2304,128]{1,0:T(8,128)(2,1)S(1)}, bf16[2304,128]{1,0:T(8,128)(2,1)S(1)}, bf16[1024,768]{1,0:T(8,128)(2,1)S(1)}) custom-call(s32[1]{0:T(128)} %bitcast.core.layer, s32[2]{0:T(128)S(1)} %copy-done.18, s32[1,768]{1,0:T(1,128)S(1)} %reshape.30.pairs, bf16[1152,768]{1,0:T(8,128)(2,1)S(1)} %get-tuple-element.52.d_pre.mid, ...), custom_call_target="tpu_custom_call" | custom-call | flops 3623878656 | bytes 5505024 | tf_op jit(solution)/shard_map/last/pallas_call | solution.py:428
  70.6 0.0 copy-start.12
  70.6 0.1 collective-permute-start.5
  70.7 2.0 %collective-permute-done.5.got_b = bf16[2304,128]{1,0:T(8,128)(2,1)S(1)} collective-permute-done((bf16[2304,128]{1,0:T(8,128)(2,1)S(1)}, bf16[2304,128]{1,0:T(8,128)(2,1)S(1)}, u32[]{:S(2)}, u32[]{:S(2)}) %collective-permute-start.5) | collective-permute-done | bytes 589856 | tf_op jit(solution)/shard_map/ppermute | solution.py:371
  72.7 0.0 collective-permute-done.4.got_a
  72.7 1.9 %join.1 = bf16[8192,128]{1,0:T(8,128)(2,1)} custom-call(bf16[5888,128]{1,0:T(8,128)(2,1)S(1)} %get-tuple-element.56.keep_a, bf16[5888,128]{1,0:T(8,128)(2,1)S(1)} %collective-permute-done.4.got_a, bf16[2304,128]{1,0:T(8,128)(2,1)S(1)} %get-tuple-element.60.keep_b, bf16[2304,128]{1,0:T(8,128)(2,1)S(1)} %collective-permute-done.5.got_b), custom_call_target="tpu_custom_call" | custom-call | bytes 4194304 | tf_op jit(solution)/shard_map/join/pallas_call | solution.py:435
  74.6 0.0 copy-done.12
  74.6 15.6 %all-to-all-start = ((bf16[64,128,128]{2,1,0:T(8,128)(2,1)}), bf16[64,128,128]{2,1,0:T(8,128)(2,1)S(1)}, u32[]{:S(2)}, u32[]{:S(2)}) async-start(bf16[64,128,128]{2,1,0:T(8,128)(2,1)} %bitcast.8), calls=%async_computation | async-start | bytes 4194304 | tf_op jit(solution)/shard_map/all_to_all | solution.py:367
  90.2 0.0 copy-start.1
  90.2 1.4 copy-done.1
  91.6 1.7 %copy-done.5 = bf16[2,768,768]{2,1,0:T(8,128)(2,1)S(1)} copy-done((bf16[2,768,768]{2,1,0:T(8,128)(2,1)S(1)}, bf16[2,768,768]{2,1,0:T(8,128)(2,1)}, u32[]{:S(2)}) %copy-start.5) | copy-done | bytes 2359320
  93.3 1.5 copy-done.11
  94.7 1.4 copy-done.13
  96.2 3.0 %input.1 = bf16[1024,768]{1,0:T(8,128)(2,1)} custom-call(bf16[1024,768]{1,0:T(8,128)(2,1)S(1)} %copy-done.13, bf16[1024,768]{1,0:T(8,128)(2,1)S(1)} %bitcast.20, bf16[1152,768]{1,0:T(8,128)(2,1)S(1)} %copy-done.11, bf16[2,768,768]{2,1,0:T(8,128)(2,1)S(1)} %copy-done.5), custom_call_target="tpu_custom_call" | custom-call | flops 1207959552 | bytes 3145728 | tf_op jit(solution)/shard_map/input/pallas_call | solution.py:442
  99.2 0.0 copy-done.3
  99.2 0.0 copy-done.7
  99.2 0.2 copy-done.9
  99.4 2.5 %out.1 = bf16[1024,768]{1,0:T(8,128)(2,1)} custom-call(bf16[1280,768]{1,0:T(8,128)(2,1)S(1)} %copy-done.9, bf16[1408,768]{1,0:T(8,128)(2,1)S(1)} %copy-done.7, bf16[2,768,768]{2,1,0:T(8,128)(2,1)S(1)} %copy-done.3), custom_call_target="tpu_custom_call" | custom-call | flops 1207959552 | bytes 3145728 | tf_op jit(solution)/shard_map/out/pallas_call | solution.py:439
  101.8 17.0 %all-to-all-done.parts = bf16[64,128,128]{2,1,0:T(8,128)(2,1)S(1)} async-done(((bf16[64,128,128]{2,1,0:T(8,128)(2,1)}), bf16[64,128,128]{2,1,0:T(8,128)(2,1)S(1)}, u32[]{:S(2)}, u32[]{:S(2)}) %all-to-all-start) | async-done | bytes 2097184 | tf_op jit(solution)/shard_map/all_to_all | solution.py:367
  118.9 0.5 share.1
  119.3 35.5 %all_to_all.10 = bf16[64,128,128]{2,1,0:T(8,128)(2,1)S(1)} all-to-all(bf16[64,128,128]{2,1,0:T(8,128)(2,1)S(1)} %share.1), channel_id=1, replica_groups=mesh['xh'=2,'core'=2,'z'=4,'xl'=2,'y'=4] {'xh','z','xl','y'}, dimensions={0} | all-to-all | bytes 4194304 | tf_op jit(solution)/shard_map/all_to_all | solution.py:367
  154.8 2.2 %collective-permute-start.6 = (bf16[8192,128]{1,0:T(8,128)(2,1)S(1)}, bf16[8192,128]{1,0:T(8,128)(2,1)S(1)}, u32[]{:S(2)}, u32[]{:S(2)}) collective-permute-start(bf16[8192,128]{1,0:T(8,128)(2,1)S(1)} %bitcast.16), channel_id=1, source_target_pairs={{0,32},{32,0},{1,33},{33,1},{2,34},{34,2},{3,35},{35,3},{4,36},{36... | collective-permute-start | bytes 6291464 | tf_op jit(solution)/shard_map/ppermute | solution.py:371
  157.0 2.3 %finish.2 = (f32[2,768,384]{2,1,0:T(8,128)}, f32[2,3,384,384]{3,2,1,0:T(8,128)}, f32[2,384,768]{2,1,0:T(8,128)}) custom-call(s32[1]{0:T(128)} %bitcast.core.layer, bf16[8192,128]{1,0:T(8,128)(2,1)S(1)} %bitcast.17), custom_call_target="tpu_custom_call" | custom-call | tf_op jit(solution)/shard_map/finish/pallas_call | solution.py:241
  159.3 1.5 collective-permute-done.6.ref
  160.8 2.3 %finish.3 = (f32[2,768,384]{2,1,0:T(8,128)}, f32[2,3,384,384]{3,2,1,0:T(8,128)}, f32[2,384,768]{2,1,0:T(8,128)}) custom-call(s32[1]{0:T(128)S(6)} %sub.3.layer, bf16[8192,128]{1,0:T(8,128)(2,1)S(1)} %collective-permute-done.6.ref, f32[2,768,384]{2,1,0:T(8,128)} %get-tuple-element.69.rest_0_, ...), custom_call_target="tpu_custom_call", output_to_operand_aliasing={{0}: (2, {}), {1}: (3, {}), {2}: (4, {})} | custom-call | tf_op jit(solution)/shard_map/finish/pallas_call | solution.py:241
  (9 shorter events, 0.0 us)
Async XLA Ops:
  0.6 13.8 %copy-start = (bf16[1,1024,768]{2,1,0:T(8,128)(2,1)S(1)}, bf16[1,1024,768]{2,1,0:T(8,128)(2,1)}, u32[]{:S(2)}) copy-start(bf16[1,1024,768]{2,1,0:T(8,128)(2,1)} %param.7) | copy-start | bytes 4718596
  0.6 13.8 %copy-start.19 = (s32[768]{0:T(1024)S(1)}, s32[768]{0:T(1024)}, u32[]{:S(2)}) copy-start(s32[768]{0:T(1024)} %param.9) | copy-start | bytes 9220
  1.9 19.3 %collective-permute-start = (bf16[256,768]{1,0:T(8,128)(2,1)S(1)}, bf16[256,768]{1,0:T(8,128)(2,1)S(1)}, u32[]{:S(2)}, u32[]{:S(2)}) collective-permute-start(bf16[256,768]{1,0:T(8,128)(2,1)S(1)} %get-tuple-element.78), channel_id=1, source_target_pairs={{0,1},{1,2},{2,3},{3,4},{4,5},{5,6},{6,7},{7,8},{8,9},{9,10},{10,1... | collective-permute-start | bytes 1179656 | tf_op jit(solution)/shard_map/ppermute | solution.py:357
  6.0 15.3 %collective-permute-start.1 = (bf16[256,768]{1,0:T(8,128)(2,1)S(1)}, bf16[256,768]{1,0:T(8,128)(2,1)S(1)}, u32[]{:S(2)}, u32[]{:S(2)}) collective-permute-start(bf16[256,768]{1,0:T(8,128)(2,1)S(1)} %get-tuple-element.77), channel_id=1, source_target_pairs={{1,0},{2,1},{3,2},{4,3},{5,4},{6,5},{7,6},{8,7},{9,8},{10,9},{11,1... | collective-permute-start | bytes 1179656 | tf_op jit(solution)/shard_map/ppermute | solution.py:358
  9.1 25.5 %collective-permute-start.2 = (bf16[128,768]{1,0:T(8,128)(2,1)}, bf16[128,768]{1,0:T(8,128)(2,1)S(1)}, u32[]{:S(2)}, u32[]{:S(2)}) collective-permute-start(bf16[128,768]{1,0:T(8,128)(2,1)} %get-tuple-element.76), channel_id=1, source_target_pairs={{0,1},{1,2},{2,3},{3,4},{4,5},{5,6},{6,7},{7,8},{8,9},{9,10},{10,1... | collective-permute-start | bytes 589832 | tf_op jit(solution)/shard_map/ppermute | solution.py:357
  13.1 21.5 %collective-permute-start.3 = (bf16[128,768]{1,0:T(8,128)(2,1)}, bf16[128,768]{1,0:T(8,128)(2,1)S(1)}, u32[]{:S(2)}, u32[]{:S(2)}) collective-permute-start(bf16[128,768]{1,0:T(8,128)(2,1)} %get-tuple-element.75), channel_id=1, source_target_pairs={{1,0},{2,1},{3,2},{4,3},{5,4},{6,5},{7,6},{8,7},{9,8},{10,9},{11,1... | collective-permute-start | bytes 589832 | tf_op jit(solution)/shard_map/ppermute | solution.py:358
  14.4 1.3 copy-start.16
  15.7 1.3 copy-start.17
  17.0 4.3 %copy-start.15 = (bf16[2,3,384,384]{3,2,1,0:T(8,128)(2,1)S(1)}, bf16[2,3,384,384]{3,2,1,0:T(8,128)(2,1)}, u32[]{:S(2)}) copy-start(bf16[2,3,384,384]{3,2,1,0:T(8,128)(2,1)} %weight.7) | copy-start | bytes 5308420
  17.0 4.3 %copy-start.18 = (s32[2]{0:T(128)S(1)}, s32[2]{0:T(128)}, u32[]{:S(2)}) copy-start(s32[2]{0:T(128)} %dil.7) | copy-start | bytes 28
  21.2 25.1 %copy-start.2 = (bf16[2,768,768]{2,1,0:T(8,128)(2,1)}, bf16[2,768,768]{2,1,0:T(8,128)(2,1)S(1)}, u32[]{:S(2)}) copy-start(bf16[2,768,768]{2,1,0:T(8,128)(2,1)S(1)} %get-tuple-element.42.upcat) | copy-start | bytes 7077892
  21.2 25.1 %copy-start.4 = (bf16[2,768,768]{2,1,0:T(8,128)(2,1)}, bf16[2,768,768]{2,1,0:T(8,128)(2,1)S(1)}, u32[]{:S(2)}) copy-start(bf16[2,768,768]{2,1,0:T(8,128)(2,1)S(1)} %get-tuple-element.41.dcat0.dcat) | copy-start | bytes 7077892
  21.3 13.3 %copy-start.14 = (bf16[1,1024,768]{2,1,0:T(8,128)(2,1)S(1)}, bf16[1,1024,768]{2,1,0:T(8,128)(2,1)}, u32[]{:S(2)}) copy-start(bf16[1,1024,768]{2,1,0:T(8,128)(2,1)} %param.8) | copy-start | bytes 4718596
  34.6 11.8 %copy-start.6 = (bf16[1408,768]{1,0:T(8,128)(2,1)}, bf16[1408,768]{1,0:T(8,128)(2,1)S(1)}, u32[]{:S(2)}) copy-start(bf16[1408,768]{1,0:T(8,128)(2,1)S(1)} %get-tuple-element.47.stream) | copy-start | bytes 6488068
  42.3 4.1 %copy-start.8 = (bf16[1280,768]{1,0:T(8,128)(2,1)}, bf16[1280,768]{1,0:T(8,128)(2,1)S(1)}, u32[]{:S(2)}) copy-start(bf16[1280,768]{1,0:T(8,128)(2,1)S(1)} %get-tuple-element.64.act) | copy-start | bytes 5898244
  58.1 4.3 %copy-start.10 = (bf16[1152,768]{1,0:T(8,128)(2,1)}, bf16[1152,768]{1,0:T(8,128)(2,1)S(1)}, u32[]{:S(2)}) copy-start(bf16[1152,768]{1,0:T(8,128)(2,1)S(1)} %get-tuple-element.49.cot) | copy-start | bytes 5308420
  62.4 10.4 %collective-permute-start.4 = (bf16[5888,128]{1,0:T(8,128)(2,1)S(1)}, bf16[5888,128]{1,0:T(8,128)(2,1)S(1)}, u32[]{:S(2)}, u32[]{:S(2)}) collective-permute-start(bf16[5888,128]{1,0:T(8,128)(2,1)S(1)} %get-tuple-element.57), channel_id=1, source_target_pairs={{0,32},{32,0},{1,33},{33,1},{2,34},{34,2},{3,35},{35,3},{4,36},{36... | collective-permute-start | bytes 4521992 | tf_op jit(solution)/shard_map/ppermute | solution.py:371
  70.6 4.0 %copy-start.12 = (bf16[1024,768]{1,0:T(8,128)(2,1)}, bf16[1024,768]{1,0:T(8,128)(2,1)S(1)}, u32[]{:S(2)}) copy-start(bf16[1024,768]{1,0:T(8,128)(2,1)S(1)} %get-tuple-element.65.d_inner) | copy-start | bytes 4718596
  70.6 2.1 %collective-permute-start.5 = (bf16[2304,128]{1,0:T(8,128)(2,1)S(1)}, bf16[2304,128]{1,0:T(8,128)(2,1)S(1)}, u32[]{:S(2)}, u32[]{:S(2)}) collective-permute-start(bf16[2304,128]{1,0:T(8,128)(2,1)S(1)} %get-tuple-element.61), channel_id=1, source_target_pairs={{0,32},{32,0},{1,33},{33,1},{2,34},{34,2},{3,35},{35,3},{4,36},{36... | collective-permute-start | bytes 1769480 | tf_op jit(solution)/shard_map/ppermute | solution.py:371
  74.6 44.2 %all-to-all-start = ((bf16[64,128,128]{2,1,0:T(8,128)(2,1)}), bf16[64,128,128]{2,1,0:T(8,128)(2,1)S(1)}, u32[]{:S(2)}, u32[]{:S(2)}) async-start(bf16[64,128,128]{2,1,0:T(8,128)(2,1)} %bitcast.8), calls=%async_computation | async-start | bytes 4194304 | tf_op jit(solution)/shard_map/all_to_all | solution.py:367
  90.2 1.4 copy-start.1
  91.6 1.7 %copy-start.5 = (bf16[2,768,768]{2,1,0:T(8,128)(2,1)S(1)}, bf16[2,768,768]{2,1,0:T(8,128)(2,1)}, u32[]{:S(2)}) copy-start(bf16[2,768,768]{2,1,0:T(8,128)(2,1)} %copy-done.4) | copy-start | bytes 7077892
  93.3 1.5 copy-start.11
  94.7 1.4 copy-start.13
  96.2 3.1 %copy-start.3 = (bf16[2,768,768]{2,1,0:T(8,128)(2,1)S(1)}, bf16[2,768,768]{2,1,0:T(8,128)(2,1)}, u32[]{:S(2)}) copy-start(bf16[2,768,768]{2,1,0:T(8,128)(2,1)} %copy-done.2) | copy-start | bytes 7077892
  96.2 3.1 %copy-start.7 = (bf16[1408,768]{1,0:T(8,128)(2,1)S(1)}, bf16[1408,768]{1,0:T(8,128)(2,1)}, u32[]{:S(2)}) copy-start(bf16[1408,768]{1,0:T(8,128)(2,1)} %copy-done.6) | copy-start | bytes 6488068
  96.2 3.2 %copy-start.9 = (bf16[1280,768]{1,0:T(8,128)(2,1)S(1)}, bf16[1280,768]{1,0:T(8,128)(2,1)}, u32[]{:S(2)}) copy-start(bf16[1280,768]{1,0:T(8,128)(2,1)} %copy-done.8) | copy-start | bytes 5898244
  154.8 6.0 %collective-permute-start.6 = (bf16[8192,128]{1,0:T(8,128)(2,1)S(1)}, bf16[8192,128]{1,0:T(8,128)(2,1)S(1)}, u32[]{:S(2)}, u32[]{:S(2)}) collective-permute-start(bf16[8192,128]{1,0:T(8,128)(2,1)S(1)} %bitcast.16), channel_id=1, source_target_pairs={{0,32},{32,0},{1,33},{33,1},{2,34},{34,2},{3,35},{35,3},{4,36},{36... | collective-permute-start | bytes 6291464 | tf_op jit(solution)/shard_map/ppermute | solution.py:371
